TPU v7x, 256 devices: a whole 4x4x8 slice. The times are simulated.
256 devices in a mesh: chan: 8 (over z_hi, x), seq: 32 (over z_lo, y, core).
Axes of the slice: x: 4, y: 4, z: 8 (z_hi: 2, z_lo: 4; z = z_hi * 4 + z_lo), core: 2. Of those that a mesh axis runs over, the one named last changes fastest.
Arguments:
- query_input: bfloat16 [16384, 4096], P('seq', 'chan'), may hold values from -6 to 6
- key_input: bfloat16 [16384, 4096], P('seq', 'chan'), may hold values from -6 to 6
- value_input: bfloat16 [16384, 4096], P('seq', 'chan'), may hold values from -6 to 6
- filter_taps: bfloat16 [16384, 4096], P('seq', 'chan'), may hold values from -2 to 2
- short_taps: float32 [3, 3, 4096], P(None, None, 'chan'), may hold values from -3 to 3
- skip_gain: float32 [4096], P('chan'), may hold values from -3 to 3
Outputs:
- operator_out: bfloat16 [16384, 4096], P('seq', 'chan')
All inputs are finite; a program needn't handle non-finite values.
Results may differ from a plain program's by a relative error of at most 0.001.
Values may be sent and summed in bfloat16 or wider, within the bound.
No kernel may reach another device: no remote copies, remote signals or barrier semaphores. Data moves between devices by JAX's collectives and lax.ppermute only.
A program may use at most 128 MiB of HBM per device.

v0:
```python
import math

import jax
import jax.numpy as jnp
from jax import lax
from jax.sharding import PartitionSpec as P

HIGHEST_PRECISION = lax.Precision.HIGHEST


def from_behind(array, axis, by):
    devices = lax.axis_size(axis)
    pairs = [(i, i + by) for i in range(devices) if 0 <= i + by < devices]
    return lax.ppermute(array, axis, pairs)


def apply_taps(rows, before_rows, tap_weights):
    row_count = rows.shape[0]
    whole = jnp.concatenate([before_rows, rows], 0).astype(jnp.float32)
    return (
        tap_weights[0] * whole[2:]
        + tap_weights[1] * whole[1 : row_count + 1]
        + tap_weights[2] * whole[:row_count]
    )


def angles(index_product, period):
    phase_angle = 2.0 * math.pi / period * (index_product % period).astype(jnp.float32)
    return (jnp.cos(phase_angle), jnp.sin(phase_angle))


def rotate(real_part, imag_part, cosine, sine_part):
    return (real_part * cosine - imag_part * sine_part, real_part * sine_part + imag_part * cosine)


def contract(pattern, left_side, right_side):
    return jnp.einsum(
        pattern,
        left_side,
        right_side,
        precision=HIGHEST_PRECISION,
        preferred_element_type=jnp.float32,
    )


def row_transform(real_part, imag_part, cos_table, sin_table, pattern, orient):
    out_real = contract(pattern, real_part, cos_table) - orient * contract(
        pattern, imag_part, sin_table
    )
    out_imag = contract(pattern, imag_part, cos_table) + orient * contract(
        pattern, real_part, sin_table
    )
    return (out_real, out_imag)


def spectral_core(
    data_real,
    data_imag,
    filt_real,
    filt_imag,
    cos_table,
    sin_table,
    forward_pattern,
    inverse_pattern,
):
    data_real, data_imag = row_transform(
        data_real, data_imag, cos_table, sin_table, forward_pattern, -1.0
    )
    filt_real, filt_imag = row_transform(
        filt_real, filt_imag, cos_table, sin_table, forward_pattern, -1.0
    )
    prod_real = data_real * filt_real - data_imag * filt_imag
    prod_imag = data_real * filt_imag + data_imag * filt_real
    return row_transform(prod_real, prod_imag, cos_table, sin_table, inverse_pattern, 1.0)


def local(query_input, key_input, value_input, filter_taps, short_taps, skip_gain):
    last_rows = jnp.stack([query_input[-2:], key_input[-2:], value_input[-2:]])
    before = from_behind(last_rows, "seq", 1)
    query_mix = apply_taps(query_input, before[0], short_taps[0])
    key_mix = apply_taps(key_input, before[1], short_taps[1])
    value_mix = apply_taps(value_input, before[2], short_taps[2])
    product = key_mix * value_mix
    kernel = filter_taps.astype(jnp.float32)
    blocks = lax.axis_size("seq")
    tok_rows = product.shape[0]
    length = 2 * blocks * tok_rows
    freq_ids = jnp.arange(2 * blocks, dtype=jnp.int32)
    block_ids = jnp.arange(blocks, dtype=jnp.int32)
    row_ids = jnp.arange(tok_rows, dtype=jnp.int32)
    outer_cos, outer_sin = angles(freq_ids[:, None] * block_ids[None, :], 2 * blocks)
    inner_cos, inner_sin = angles(row_ids[:, None] * row_ids[None, :], tok_rows)
    slice_rows = tok_rows // blocks
    arrived = (
        lax.all_to_all(product[None], "seq", split_axis=1, concat_axis=0, tiled=True),
        lax.all_to_all(kernel[None], "seq", split_axis=1, concat_axis=0, tiled=True),
    )
    local_rows = lax.axis_index("seq") * slice_rows + jnp.arange(slice_rows, dtype=jnp.int32)
    twist_cos, twist_sin = angles(freq_ids[:, None] * local_rows[None, :], length)
    twist_cos = twist_cos[:, :, None]
    twist_sin = twist_sin[:, :, None]

    def first_section(block_data):
        real_part = contract("ar,rjc->ajc", outer_cos, block_data)
        imag_part = -contract("ar,rjc->ajc", outer_sin, block_data)
        real_part, imag_part = rotate(real_part, imag_part, twist_cos, -twist_sin)
        return jnp.stack([real_part, imag_part])

    data_section = first_section(arrived[0])
    filt_section = first_section(arrived[1])
    own_freq = 2 * lax.axis_index("seq") + jnp.arange(2, dtype=jnp.int32)
    back_cos, back_sin = angles(own_freq[:, None] * row_ids[None, :], length)
    back_cos = back_cos[:, :, None]
    back_sin = back_sin[:, :, None]
    data_part = lax.all_to_all(data_section, "seq", split_axis=1, concat_axis=2, tiled=True)
    filt_part = lax.all_to_all(filt_section, "seq", split_axis=1, concat_axis=2, tiled=True)
    out_real, out_imag = spectral_core(
        data_part[0],
        data_part[1],
        filt_part[0],
        filt_part[1],
        inner_cos,
        inner_sin,
        "ajc,jb->abc",
        "abc,bj->ajc",
    )
    out_real, out_imag = rotate(out_real, out_imag, back_cos, back_sin)
    spectral_out = jnp.stack([out_real, out_imag])
    returned = lax.all_to_all(spectral_out, "seq", split_axis=2, concat_axis=1, tiled=True)
    conv_part = (
        contract("ar,ajc->rjc", outer_cos, returned[0])
        - contract("ar,ajc->rjc", outer_sin, returned[1])
    ) / length
    convolved = lax.all_to_all(conv_part, "seq", split_axis=0, concat_axis=1, tiled=True)[0]
    return (query_mix * (convolved + skip_gain * product)).astype(jnp.bfloat16)


def solution(mesh):
    placed = (
        P("seq", "chan"),
        P("seq", "chan"),
        P("seq", "chan"),
        P("seq", "chan"),
        P(None, None, "chan"),
        P("chan"),
    )
    return jax.shard_map(
        local, mesh=mesh, in_specs=placed, out_specs=P("seq", "chan"), check_vma=False
    )
```

profile of v0, /device:TPU:1, one launch (start us, length us, event | category | flops | bytes accessed | tf_op | source)
XLA Modules:
  0.0 503.7 jit_solution(13040818460079726596)
XLA Ops:
  0.0 2.7 reshape.155
  2.7 10.2 %all-to-all-start.2 = ((f32[1,512,512]{2,0,1:T(1,128)}), f32[1,512,512]{2,0,1:T(1,128)S(1)}, u32[]{:S(2)}, u32[]{:S(2)}) async-start(f32[1,512,512]{2,0,1:T(1,128)} %reshape.155), calls=%async_computation.2 | async-start | bytes 2097152 | tf_op jit(solution)/shard_map/all_to_all | solution.py:96
  12.9 0.7 slice_bitcast_fusion.5
  13.6 0.0 copy-done.4
  13.6 0.0 copy-done.3
  13.6 3.5 collective-permute-start
  17.2 0.0 copy-done.5
  17.2 0.7 collective-permute-done
  17.9 0.2 maximum_convert_fusion.1
  18.1 0.2 maximum_convert_fusion.2
  18.3 0.7 fusion.23
  18.9 2.1 copy.24
  21.0 18.5 %all-to-all-done.2 = f32[1,512,512]{2,0,1:T(1,128)S(1)} async-done(((f32[1,512,512]{2,0,1:T(1,128)}), f32[1,512,512]{2,0,1:T(1,128)S(1)}, u32[]{:S(2)}, u32[]{:S(2)}) %all-to-all-start.2) | async-done | bytes 1048608 | tf_op jit(solution)/shard_map/all_to_all | solution.py:96
  39.5 7.4 %all-to-all-start = ((f32[1,512,512]{2,0,1:T(1,128)}), f32[1,512,512]{2,0,1:T(1,128)S(1)}, u32[]{:S(2)}, u32[]{:S(2)}) async-start(f32[1,512,512]{2,0,1:T(1,128)} %copy.24), calls=%async_computation | async-start | bytes 2097152 | tf_op jit(solution)/shard_map/all_to_all | solution.py:95
  46.9 0.1 fusion.102
  47.1 0.1 copy.37
  47.2 3.8 fusion.50
  50.9 3.7 fusion.52
  54.6 18.8 %all-to-all-done = f32[1,512,512]{2,0,1:T(1,128)S(1)} async-done(((f32[1,512,512]{2,0,1:T(1,128)}), f32[1,512,512]{2,0,1:T(1,128)S(1)}, u32[]{:S(2)}, u32[]{:S(2)}) %all-to-all-start) | async-done | bytes 1048608 | tf_op jit(solution)/shard_map/all_to_all | solution.py:95
  73.4 0.1 copy.36
  73.5 0.0 copy-start
  73.5 2.4 fusion.54
  75.9 0.0 copy-done.1
  75.9 0.0 copy-done
  75.9 4.3 subtract_bitcast_fusion
  80.2 0.6 pad_maximum_fusion.1
  80.8 4.4 copy.31
  85.2 5.3 %all-to-all-start.3 = ((f32[2,64,16,512]{3,2,0,1:T(8,128)}), f32[2,64,16,512]{3,2,0,1:T(8,128)}, u32[]{:S(2)}, u32[]{:S(2)}) async-start(f32[2,64,16,512]{3,2,0,1:T(8,128)} %copy.31), calls=%async_computation.3 | async-start | bytes 8388608 | tf_op jit(solution)/shard_map/all_to_all | solution.py:116
  90.5 2.2 pad_maximum_fusion
  92.7 4.5 copy.27
  97.2 86.6 %all-to-all-done.3 = f32[2,64,16,512]{3,2,0,1:T(8,128)} async-done(((f32[2,64,16,512]{3,2,0,1:T(8,128)}), f32[2,64,16,512]{3,2,0,1:T(8,128)}, u32[]{:S(2)}, u32[]{:S(2)}) %all-to-all-start.3) | async-done | bytes 4194336 | tf_op jit(solution)/shard_map/all_to_all | solution.py:116
  183.8 6.5 %all-to-all-start.1 = ((f32[2,64,16,512]{3,2,0,1:T(8,128)}), f32[2,64,16,512]{3,2,0,1:T(8,128)}, u32[]{:S(2)}, u32[]{:S(2)}) async-start(f32[2,64,16,512]{3,2,0,1:T(8,128)} %copy.27), calls=%async_computation.1 | async-start | bytes 8388608 | tf_op jit(solution)/shard_map/all_to_all | solution.py:115
  190.4 0.2 fusion.104
  190.5 2.6 copy.52
  193.2 0.8 fusion.178
  194.0 7.3 %fusion.43 = f32[512,2,512]{2,0,1:T(8,128)S(1)} fusion(f32[2,512,512]{2,1,0:T(8,128)S(1)} %bitcast.161), kind=kOutput, calls=%fused_computation.73 | convolution fusion | flops 3224895488 | bytes 4194304 | tf_op jit(solution)/shard_map/ajc,jb->abc/dot_general | solution.py:37
  201.3 7.5 %fusion.39 = f32[512,2,512]{2,0,1:T(8,128)S(1)} fusion(f32[2,512,512]{2,1,0:T(8,128)S(1)} %bitcast.163), kind=kOutput, calls=%fused_computation.69 | convolution fusion | flops 3224895488 | bytes 4194304 | tf_op jit(solution)/shard_map/ajc,jb->abc/dot_general | solution.py:37
  208.8 7.5 %multiply_subtract_fusion.1 = f32[512,2,512]{2,0,1:T(8,128)S(1)} fusion(f32[512,2,512]{2,0,1:T(8,128)S(1)} %fusion.43, f32[2,512,512]{2,1,0:T(8,128)S(1)} %bitcast.164), kind=kOutput, calls=%fused_computation.26 | convolution fusion | flops 3225944064 | bytes 6291456 | tf_op jit(solution)/shard_map/ajc,jb->abc/dot_general | solution.py:37
  216.3 9.4 %multiply_add_fusion.1 = f32[512,2,512]{2,0,1:T(8,128)} fusion(f32[512,2,512]{2,0,1:T(8,128)S(1)} %fusion.39, f32[2,512,512]{2,1,0:T(8,128)S(1)} %bitcast.162), kind=kOutput, calls=%fused_computation.24 | convolution fusion | flops 3225944064 | bytes 6291456 | tf_op jit(solution)/shard_map/ajc,jb->abc/dot_general | solution.py:37
  225.7 58.0 %all-to-all-done.1 = f32[2,64,16,512]{3,2,0,1:T(8,128)} async-done(((f32[2,64,16,512]{3,2,0,1:T(8,128)}), f32[2,64,16,512]{3,2,0,1:T(8,128)}, u32[]{:S(2)}, u32[]{:S(2)}) %all-to-all-start.1) | async-done | bytes 4194336 | tf_op jit(solution)/shard_map/all_to_all | solution.py:115
  283.7 2.6 copy.53
  286.3 0.8 fusion.179
  287.2 7.3 %fusion.41 = f32[512,2,512]{2,0,1:T(8,128)S(1)} fusion(f32[2,512,512]{2,1,0:T(8,128)S(1)} %bitcast.165), kind=kOutput, calls=%fused_computation.71 | convolution fusion | flops 3224895488 | bytes 4194304 | tf_op jit(solution)/shard_map/ajc,jb->abc/dot_general | solution.py:37
  294.5 7.5 %fusion.45 = f32[512,2,512]{2,0,1:T(8,128)S(1)} fusion(f32[2,512,512]{2,1,0:T(8,128)S(1)} %bitcast.159), kind=kOutput, calls=%fused_computation.75 | convolution fusion | flops 3224895488 | bytes 4194304 | tf_op jit(solution)/shard_map/ajc,jb->abc/dot_general | solution.py:37
  302.0 7.5 %multiply_subtract_fusion.2 = f32[512,2,512]{2,0,1:T(8,128)S(1)} fusion(f32[512,2,512]{2,0,1:T(8,128)S(1)} %fusion.45, f32[2,512,512]{2,1,0:T(8,128)S(1)} %bitcast.166), kind=kOutput, calls=%fused_computation.29 | convolution fusion | flops 3225944064 | bytes 6291456 | tf_op jit(solution)/shard_map/ajc,jb->abc/dot_general | solution.py:37
  309.6 8.3 %multiply_subtract_fusion = (f32[512,2,512]{2,0,1:T(8,128)S(1)}, f32[512,2,512]{2,0,1:T(8,128)S(1)}) fusion(f32[512,2,512]{2,0,1:T(8,128)S(1)} %copy-done.2, f32[512,2,512]{2,0,1:T(8,128)S(1)} %multiply_subtract_fusion.2, f32[512,2,512]{2,0,1:T(8,128)S(1)} %multiply_subtract_fusion.1, f32[512,2,512]{2,0,1:T(8,128)S(1)} %fusion.41, ...), kind=kOutput, calls=%fused_computation.23 | convolution fusion | flops 3229089792 | bytes 14680064 | tf_op jit(solution)/shard_map/ajc,jb->abc/dot_general | solution.py:37
  317.8 7.7 %fusion.4 = f32[512,2,512]{2,0,1:T(8,128)S(1)} fusion(f32[512,2,512]{2,0,1:T(8,128)S(1)} %get-tuple-element.6), kind=kOutput, calls=%fused_computation.14 | convolution fusion | flops 3224895488 | bytes 4194304 | tf_op jit(solution)/shard_map/abc,bj->ajc/dot_general | solution.py:37
  325.6 7.4 %fusion.6 = f32[512,2,512]{2,0,1:T(8,128)S(1)} fusion(f32[512,2,512]{2,0,1:T(8,128)S(1)} %get-tuple-element.6), kind=kOutput, calls=%fused_computation.16 | convolution fusion | flops 3224895488 | bytes 4194304 | tf_op jit(solution)/shard_map/abc,bj->ajc/dot_general | solution.py:37
  332.9 7.6 %fusion.12 = f32[512,2,512]{2,0,1:T(8,128)S(1)} fusion(f32[512,2,512]{2,0,1:T(8,128)S(1)} %fusion.6, f32[512,2,512]{2,0,1:T(8,128)S(1)} %get-tuple-element.5), kind=kOutput, calls=%fused_computation.32 | convolution fusion | flops 3225419776 | bytes 6291456 | tf_op jit(solution)/shard_map/abc,bj->ajc/dot_general | solution.py:37
  340.5 7.8 %fusion.1 = (f32[1,2,512,512]{3,2,1,0:T(8,128)S(1)}, f32[1,2,512,512]{3,2,1,0:T(8,128)S(1)}) fusion(f32[512,2,512]{2,0,1:T(8,128)S(1)} %fusion.12, f32[2,512]{1,0:T(2,128)S(1)} %get-tuple-element.34, f32[2,512]{1,0:T(2,128)S(1)} %get-tuple-element.33, f32[512,2,512]{2,0,1:T(8,128)S(1)} %fusion.4, f32[512,2,512]{2,0,1:T(8,128)S(1)} %get-tuple-element.5), kind=kOutput, calls=%fused_computation.9 | convolution fusion | flops 3228565504 | bytes 10493952 | tf_op jit(solution)/shard_map/abc,bj->ajc/dot_general | solution.py:37
  348.3 0.4 pad_maximum_fusion.2
  348.7 3.4 copy.33
  352.2 100.3 %all_to_all.78 = f32[2,2,512,512]{3,1,0,2:T(2,128)S(1)} all-to-all(f32[2,2,512,512]{3,1,0,2:T(2,128)S(1)} %copy.33), channel_id=1, replica_groups=mesh['chan'=8,'seq'=32] {'seq'}, dimensions={2} | all-to-all | bytes 8388608 | tf_op jit(solution)/shard_map/all_to_all | solution.py:129
  452.5 2.3 copy.51
  454.8 3.4 fusion.177
  458.2 2.7 squeeze.41
  460.9 3.6 squeeze.40
  464.6 2.8 fusion.78
  467.4 1.2 fusion.18
  468.6 1.6 copy.35
  470.2 5.4 %all-to-all-start.5 = ((f32[32,16,512]{2,1,0:T(8,128)}), f32[32,16,512]{2,1,0:T(8,128)S(1)}, u32[]{:S(2)}, u32[]{:S(2)}) async-start(f32[32,16,512]{2,1,0:T(8,128)} %copy.35), calls=%async_computation.5 | async-start | bytes 2097152 | tf_op jit(solution)/shard_map/all_to_all | solution.py:134
  475.6 1.2 maximum_convert_fusion
  476.8 25.4 %all-to-all-done.5 = f32[32,16,512]{2,1,0:T(8,128)S(1)} async-done(((f32[32,16,512]{2,1,0:T(8,128)}), f32[32,16,512]{2,1,0:T(8,128)S(1)}, u32[]{:S(2)}, u32[]{:S(2)}) %all-to-all-start.5) | async-done | bytes 1048608 | tf_op jit(solution)/shard_map/all_to_all | solution.py:134
  502.2 1.2 fusion.29
  (14 shorter events, 0.1 us)
Async XLA Ops:
  0.0 13.6 %copy-start.4 = (bf16[512,512]{1,0:T(8,128)(2,1)S(1)}, bf16[512,512]{1,0:T(8,128)(2,1)}, u32[]{:S(2)}) copy-start(bf16[512,512]{1,0:T(8,128)(2,1)} %param.8) | copy-start | bytes 1572868
  0.0 13.6 %copy-start.3 = (bf16[512,512]{1,0:T(8,128)(2,1)S(1)}, bf16[512,512]{1,0:T(8,128)(2,1)}, u32[]{:S(2)}) copy-start(bf16[512,512]{1,0:T(8,128)(2,1)} %param.7) | copy-start | bytes 1572868
  0.0 17.2 %copy-start.5 = (f32[3,3,512]{2,1,0:T(4,128)S(1)}, f32[3,3,512]{2,1,0:T(4,128)}, u32[]{:S(2)}) copy-start(f32[3,3,512]{2,1,0:T(4,128)} %param.10) | copy-start | bytes 55300
  2.7 36.8 %all-to-all-start.2 = ((f32[1,512,512]{2,0,1:T(1,128)}), f32[1,512,512]{2,0,1:T(1,128)S(1)}, u32[]{:S(2)}, u32[]{:S(2)}) async-start(f32[1,512,512]{2,0,1:T(1,128)} %reshape.155), calls=%async_computation.2 | async-start | bytes 2097152 | tf_op jit(solution)/shard_map/all_to_all | solution.py:96
  13.6 4.3 collective-permute-start
  39.5 33.9 %all-to-all-start = ((f32[1,512,512]{2,0,1:T(1,128)}), f32[1,512,512]{2,0,1:T(1,128)S(1)}, u32[]{:S(2)}, u32[]{:S(2)}) async-start(f32[1,512,512]{2,0,1:T(1,128)} %copy.24), calls=%async_computation | async-start | bytes 2097152 | tf_op jit(solution)/shard_map/all_to_all | solution.py:95
  73.4 2.5 copy-start.1
  73.5 2.4 copy-start
  85.2 98.6 %all-to-all-start.3 = ((f32[2,64,16,512]{3,2,0,1:T(8,128)}), f32[2,64,16,512]{3,2,0,1:T(8,128)}, u32[]{:S(2)}, u32[]{:S(2)}) async-start(f32[2,64,16,512]{3,2,0,1:T(8,128)} %copy.31), calls=%async_computation.3 | async-start | bytes 8388608 | tf_op jit(solution)/shard_map/all_to_all | solution.py:116
  183.8 99.9 %all-to-all-start.1 = ((f32[2,64,16,512]{3,2,0,1:T(8,128)}), f32[2,64,16,512]{3,2,0,1:T(8,128)}, u32[]{:S(2)}, u32[]{:S(2)}) async-start(f32[2,64,16,512]{3,2,0,1:T(8,128)} %copy.27), calls=%async_computation.1 | async-start | bytes 8388608 | tf_op jit(solution)/shard_map/all_to_all | solution.py:115
  302.0 7.5 %copy-start.2 = (f32[512,2,512]{2,0,1:T(8,128)S(1)}, f32[512,2,512]{2,0,1:T(8,128)}, u32[]{:S(2)}) copy-start(f32[512,2,512]{2,0,1:T(8,128)} %multiply_add_fusion.1) | copy-start | bytes 6291460
  470.2 32.0 %copy-start.6 = (f32[512]{0:T(512)S(1)}, f32[512]{0:T(512)}, u32[]{:S(2)}) copy-start(f32[512]{0:T(512)} %param.11) | copy-start | bytes 6148
  470.2 32.0 %all-to-all-start.5 = ((f32[32,16,512]{2,1,0:T(8,128)}), f32[32,16,512]{2,1,0:T(8,128)S(1)}, u32[]{:S(2)}, u32[]{:S(2)}) async-start(f32[32,16,512]{2,1,0:T(8,128)} %copy.35), calls=%async_computation.5 | async-start | bytes 2097152 | tf_op jit(solution)/shard_map/all_to_all | solution.py:134
where the time goes:
time: 508 us; the launch traced here: 504 us
  waiting for transfers between devices  208 us (41%)
  matrix products  111 us (22%)
  blocking collectives  100 us (20%)
  local copies, waits for them, and re-layouts  38.7 us (8%)
  starting transfers between devices  38.4 us (8%)
  other arithmetic  6.92 us (1%)
    dot_general x18, matrix products, contract(): jnp.einsum(pattern, left_side, right_side, precision=HIGHEST_PRECISION, p...  111 us
    all_to_all x1, blocking collectives, local(): lax.all_to_all(spectral_out, 'seq', split_axis=2, concat_axis=1, tiled=True)  100 us
    all_to_all x1, waiting for transfers between devices, local(): lax.all_to_all(filt_section, 'seq', split_axis=1, concat_axis=2, tiled=True)  86.6 us
    all_to_all x1, waiting for transfers between devices, local(): lax.all_to_all(data_section, 'seq', split_axis=1, concat_axis=2, tiled=True)  58 us
    all_to_all x1, waiting for transfers between devices, local(): lax.all_to_all(conv_part, 'seq', split_axis=0, concat_axis=1, tiled=True)[0]  25.4 us
    all_to_all x1, waiting for transfers between devices, local(): lax.all_to_all(product[None], 'seq', split_axis=1, concat_axis=0, tiled=T...  18.8 us
    all_to_all x1, waiting for transfers between devices, local(): lax.all_to_all(kernel[None], 'seq', split_axis=1, concat_axis=0, tiled=True)  18.5 us
    all_to_all x1, starting transfers between devices, local(): lax.all_to_all(kernel[None], 'seq', split_axis=1, concat_axis=0, tiled=True)  10.2 us
  transfers between devices with their start and end apart: 6, of which 6 were waited for; matrix products, arithmetic and copies ran while one was open for 11% of the time, Pallas kernels for 0%

commit v1 on v0

v1 whole, which is shorter than its diff:
```python
import functools
import math

import jax
import jax.numpy as jnp
import ml_dtypes
import numpy as np
from jax import lax
from jax.experimental import pallas as pl
from jax.experimental.pallas import tpu as pltpu
from jax.sharding import PartitionSpec as P

F32 = jnp.float32
BF16 = jnp.bfloat16

SIDE = 128
LENGTH = SIDE * SIDE
PACK = 16
BLOCKS = 32
TOKENS = 512
CHANS = 512
QUARTERS = TOKENS // SIDE
GROUP = 128
SENDS = GROUP // PACK
IN_TILES = 2 * QUARTERS + 1
OUT_TILES = QUARTERS + 1

SPAN = 252.0
DROP = 125.5
TINY = 1e-35


def split_const(table):
    hi = table.astype(ml_dtypes.bfloat16)
    lo = (table - hi.astype(np.float64)).astype(ml_dtypes.bfloat16)
    return hi, lo


def tables():
    n = np.arange(SIDE, dtype=np.float64)
    ang = 2.0 * np.pi / SIDE * np.outer(n - 0.25, n)
    first = np.concatenate([np.cos(ang), -np.sin(ang)], 0)
    last = np.concatenate([np.cos(ang).T, -np.sin(ang).T], 1) / LENGTH
    tw = 2.0 * np.pi / LENGTH * np.outer(n - 0.25, n)
    mid = 2.0 * np.pi / SIDE * (np.outer(n, n) % SIDE)
    cos, sin = np.cos(mid), np.sin(mid)
    fwd = np.block([[cos, -sin], [sin, cos]])
    inv = np.block([[cos, sin], [-sin, cos]])
    first_hi, first_lo = split_const(first)
    last_hi, last_lo = split_const(last)
    fwd_hi, fwd_lo = split_const(fwd)
    inv_hi, inv_lo = split_const(inv)
    return (
        np.concatenate([first_hi, first_hi, first_lo], 1),
        np.concatenate([first_hi, first_lo], 1),
        np.concatenate([fwd_hi, fwd_hi, fwd_lo], 0),
        np.concatenate([inv_hi, inv_hi, inv_lo], 0),
        np.concatenate([last_hi, last_hi, last_lo], 1),
        np.cos(tw).astype(np.float32),
        np.sin(tw).astype(np.float32),
    )


def split(x):
    hi = x.astype(BF16)
    lo = (x - hi.astype(F32)).astype(BF16)
    return hi, lo


def scale_up(largest):
    return jnp.maximum(largest * 1.004, TINY).astype(BF16).astype(F32)


def encode(x, inverse_scale):
    y = jnp.exp2(SPAN * jnp.sqrt(jnp.abs(x) * inverse_scale) - DROP)
    return jnp.where(x < 0.0, -y, y)


def decode(y, scale):
    g = (jnp.log2(jnp.abs(y)) + DROP) * (1.0 / SPAN)
    x = g * g * scale
    return jnp.where(y < 0.0, -x, x)


def mixed(rows, before, taps, pad_ref):
    count = rows.shape[0]
    pad_ref[pl.ds(8, count), :] = rows
    pad_ref[6:8, :] = before
    return (
        taps[0:1] * rows
        + taps[1:2] * pad_ref[pl.ds(7, count), :]
        + taps[2:3] * pad_ref[pl.ds(6, count), :]
    )


def front_kernel(key_ref, value_ref, filter_ref, taps_ref, out_ref, pad_ref, edge_ref):
    zero = jnp.zeros((2, GROUP), F32)
    key = key_ref[...].astype(F32)
    value = value_ref[...].astype(F32)
    product = mixed(key, zero, taps_ref[1], pad_ref) * mixed(value, zero, taps_ref[2], pad_ref)
    scale = scale_up(jnp.max(jnp.abs(product), axis=0, keepdims=True))
    code = encode(product, 1.0 / scale)

    edge_ref[...] = jnp.zeros_like(edge_ref)
    edge_ref[0:1, :] = scale
    for place, (rows, taps) in enumerate(((key, taps_ref[1]), (value, taps_ref[2]))):
        first, second = rows[0:1], rows[1:2]
        before, last = rows[TOKENS - 2 : TOKENS - 1], rows[TOKENS - 1 :]
        parts = (
            taps[0:1] * first,
            taps[0:1] * second + taps[1:2] * first,
            taps[1:2] * last + taps[2:3] * before,
            taps[2:3] * last,
        )
        for i, part in enumerate(parts):
            hi, lo = split(part)
            row = 8 + place * 8 + 2 * i
            edge_ref[row : row + 1, :] = hi.astype(F32)
            edge_ref[row + 1 : row + 2, :] = lo.astype(F32)

    def put(tile, block):
        out_ref[:, tile * PACK : (tile + 1) * PACK, :] = block.T.astype(BF16).reshape(SENDS, PACK, SIDE)

    for q in range(QUARTERS):
        rows = slice(q * SIDE, (q + 1) * SIDE)
        put(q, code[rows])
        put(QUARTERS + q, filter_ref[rows, :].astype(F32))
    put(2 * QUARTERS, edge_ref[...])


def middle_kernel(in_ref, first_ref, first_exact_ref, fwd_ref, inv_ref, last_ref, cos_ref, sin_ref, out_ref, prod_ref, filt_ref, conv_ref):
    rows = BLOCKS * QUARTERS * PACK
    edge = in_ref[:, 2 * QUARTERS * PACK :, :].astype(F32)
    scale = edge[:, :, 0:1]
    for q in range(QUARTERS):
        prod_ref[:, q] = decode(in_ref[:, q * PACK : (q + 1) * PACK, :].astype(F32), scale)
        filt_ref[:, q] = in_ref[:, (QUARTERS + q) * PACK : (QUARTERS + q + 1) * PACK, :].astype(F32)

    def part(place, i):
        lane = 8 + place * 8 + 2 * i
        return edge[:, :, lane : lane + 1] + edge[:, :, lane + 1 : lane + 2]

    def behind(x):
        return jnp.concatenate([jnp.zeros_like(x[:1]), x[:-1]], 0)

    first = (part(0, 0) + behind(part(0, 2))) * (part(1, 0) + behind(part(1, 2)))
    second = (part(0, 1) + behind(part(0, 3))) * (part(1, 1) + behind(part(1, 3)))
    lane = lax.broadcasted_iota(jnp.int32, (BLOCKS, PACK, SIDE), 2)
    prod_ref[:, 0] = jnp.where(lane == 0, first, jnp.where(lane == 1, second, prod_ref[:, 0]))

    prod_rows = prod_ref.reshape(rows, SIDE)
    filt_rows = filt_ref.reshape(rows, SIDE)
    conv_rows = conv_ref.reshape(rows, SIDE)

    def halves(x):
        return x[:SIDE], x[SIDE:]

    def one_pair(pair, carry):
        chans = [2 * pair, 2 * pair + 1]
        cos, sin = cos_ref[...], sin_ref[...]

        def channels(ref):
            return jnp.concatenate([ref[pl.ds(c, SIDE, stride=PACK), :] for c in chans], 1)

        hi, lo = split(channels(prod_rows))
        data = jnp.dot(first_ref[...], jnp.concatenate([hi, lo, hi], 0), preferred_element_type=F32)
        taps = channels(filt_rows).astype(BF16)
        filt = jnp.dot(first_exact_ref[...], jnp.concatenate([taps, taps], 0), preferred_element_type=F32)

        lhs = []
        for block in (data, filt):
            for i in range(2):
                re, im = halves(block[:, i * SIDE : (i + 1) * SIDE])
                both = jnp.concatenate([re * cos + im * sin, im * cos - re * sin], 1)
                hi, lo = split(both)
                lhs.append(jnp.concatenate([hi, lo, hi], 1))
        spectra = jnp.dot(jnp.concatenate(lhs, 0), fwd_ref[...], preferred_element_type=F32)
        x, h = spectra[: 2 * SIDE], spectra[2 * SIDE :]
        x_re, x_im, h_re, h_im = x[:, :SIDE], x[:, SIDE:], h[:, :SIDE], h[:, SIDE:]
        z = jnp.concatenate([x_re * h_re - x_im * h_im, x_re * h_im + x_im * h_re], 1)
        hi, lo = split(z)
        back = jnp.dot(jnp.concatenate([hi, lo, hi], 1), inv_ref[...], preferred_element_type=F32)
        cols = []
        for i in range(2):
            re, im = back[i * SIDE : (i + 1) * SIDE, :SIDE], back[i * SIDE : (i + 1) * SIDE, SIDE:]
            cols.append(jnp.concatenate([re * cos - im * sin, im * cos + re * sin], 0))
        hi, lo = split(jnp.concatenate(cols, 1))
        y = jnp.dot(last_ref[...], jnp.concatenate([hi, lo, hi], 0), preferred_element_type=F32)
        for i, c in enumerate(chans):
            conv_rows[pl.ds(c, SIDE, stride=PACK), :] = y[:, i * SIDE : (i + 1) * SIDE]
        return carry

    lax.fori_loop(0, PACK // 2, one_pair, 0)

    conv = [conv_ref[:, q] for q in range(QUARTERS)]
    largest = functools.reduce(jnp.maximum, [jnp.abs(c) for c in conv])
    scale = scale_up(jnp.max(largest, axis=2, keepdims=True))
    inverse = 1.0 / scale
    for q in range(QUARTERS):
        out_ref[:, q * PACK : (q + 1) * PACK, :] = encode(conv[q], inverse).astype(BF16)
    out_ref[:, QUARTERS * PACK :, :] = jnp.broadcast_to(scale, (BLOCKS, PACK, SIDE)).astype(BF16)


def end_kernel(query_ref, key_ref, value_ref, halo_ref, taps_ref, gain_ref, conv_ref, out_ref, pad_ref):
    def stream(place, ref):
        return mixed(ref[...].astype(F32), halo_ref[place].astype(F32), taps_ref[place], pad_ref)

    product = stream(1, key_ref) * stream(2, value_ref)
    query = stream(0, query_ref)
    direct = gain_ref[...] * product
    scale = conv_ref[:, QUARTERS * PACK :, 0:1].astype(F32)
    for q in range(QUARTERS):
        conv = decode(conv_ref[:, q * PACK : (q + 1) * PACK, :].astype(F32), scale)
        rows = slice(q * SIDE, (q + 1) * SIDE)
        out_ref[rows, :] = (query[rows] * (conv.reshape(GROUP, SIDE).T + direct[rows])).astype(BF16)


def local(consts, query_input, key_input, value_input, filter_taps, short_taps, skip_gain):
    steps = CHANS // GROUP
    rows_spec = pl.BlockSpec((TOKENS, GROUP), lambda i: (0, i))
    taps_spec = pl.BlockSpec((3, 3, GROUP), lambda i: (0, 0, i))
    params = pltpu.CompilerParams(vmem_limit_bytes=48 * 1024 * 1024)

    last_rows = jnp.stack([query_input[-2:], key_input[-2:], value_input[-2:]])
    pairs = [(i, i + 1) for i in range(BLOCKS - 1)]
    halo = lax.ppermute(last_rows, "seq", pairs)

    sent = pl.pallas_call(
        front_kernel,
        grid=(steps,),
        in_specs=[rows_spec, rows_spec, rows_spec, taps_spec],
        out_specs=pl.BlockSpec((SENDS, IN_TILES * PACK, SIDE), lambda i: (i, 0, 0)),
        out_shape=jax.ShapeDtypeStruct((BLOCKS, IN_TILES * PACK, SIDE), BF16),
        scratch_shapes=[pltpu.VMEM((TOKENS + 8, GROUP), F32), pltpu.VMEM((SIDE, GROUP), F32)],
        compiler_params=params,
        name="front",
    )(key_input, value_input, filter_taps, short_taps)
    arrived = lax.all_to_all(sent, "seq", split_axis=0, concat_axis=0, tiled=True)

    work = pltpu.VMEM((BLOCKS, QUARTERS, PACK, SIDE), F32)
    conv = pl.pallas_call(
        middle_kernel,
        out_shape=jax.ShapeDtypeStruct((BLOCKS, OUT_TILES * PACK, SIDE), BF16),
        scratch_shapes=[work, work, work],
        compiler_params=params,
        name="middle",
    )(arrived, *[jnp.asarray(c) for c in consts])
    returned = lax.all_to_all(conv, "seq", split_axis=0, concat_axis=0, tiled=True)

    return pl.pallas_call(
        end_kernel,
        grid=(steps,),
        in_specs=[
            rows_spec,
            rows_spec,
            rows_spec,
            pl.BlockSpec((3, 2, GROUP), lambda i: (0, 0, i)),
            taps_spec,
            pl.BlockSpec((1, GROUP), lambda i: (0, i)),
            pl.BlockSpec((SENDS, OUT_TILES * PACK, SIDE), lambda i: (i, 0, 0)),
        ],
        out_specs=rows_spec,
        out_shape=jax.ShapeDtypeStruct((TOKENS, CHANS), BF16),
        scratch_shapes=[pltpu.VMEM((TOKENS + 8, GROUP), F32)],
        compiler_params=params,
        name="end",
    )(query_input, key_input, value_input, halo, short_taps, skip_gain[None, :], returned)


def solution(mesh):
    placed = (
        P("seq", "chan"),
        P("seq", "chan"),
        P("seq", "chan"),
        P("seq", "chan"),
        P(None, None, "chan"),
        P("chan"),
    )
    return jax.shard_map(
        functools.partial(local, tables()),
        mesh=mesh,
        in_specs=placed,
        out_specs=P("seq", "chan"),
        check_vma=False,
    )
```

time: 508 us -> 87.2 us (0.17)
  waiting for transfers between devices: 208 us -> 15.4 us
  matrix products: 111 us -> 0 us
  blocking collectives: 100 us -> 41 us
  local copies, waits for them, and re-layouts: 38.7 us -> 3.94 us
  starting transfers between devices: 38.4 us -> 7.65 us
  Pallas kernels: 0 us -> 18.5 us
  other arithmetic: 6.92 us -> 0.01 us
    all_to_all x5 -> x1, waiting for transfers between devices: 207 us -> 14.7 us  [local(): lax.all_to_all(conv, 'seq', split_axis=0, concat_axis=0, tiled=True)]
    dot_general x18 -> x0, matrix products: 111 us -> none  [contract(): jnp.einsum(pattern, left_side, right_side, precision=HIGHEST_PRECISION, p...]
    all_to_all x1, blocking collectives: 100 us -> 41 us  [local(): lax.all_to_all(sent, 'seq', split_axis=0, concat_axis=0, tiled=True)]
    all_to_all x5 -> x1, starting transfers between devices: 34.9 us -> 4.11 us  [local(): lax.all_to_all(conv, 'seq', split_axis=0, concat_axis=0, tiled=True)]
    pallas_call x0 -> x3, Pallas kernels: none -> 18.5 us  [the longest x1 13.3 us: local(): pl.pallas_call(middle_kernel, out_shape=jax.ShapeDtypeStruct((BLOCKS, OUT...]
    another operation x3 -> x0, local copies, waits for them, and re-layouts: 12.3 us -> none  [the longest x2 8.88 us: first_section(): return jnp.stack([real_part, imag_part])]
    all_to_all x3 -> x0, local copies, waits for them, and re-layouts: 7.63 us -> none  [the longest x1 2.64 us: local(): lax.all_to_all(filt_section, 'seq', split_axis=1, concat_axis=2, tiled=True)]
    squeeze x3 -> x0, local copies, waits for them, and re-layouts: 6.34 us -> none  [the longest x1 3.64 us: local(): returned[0]]
  transfers between devices with their start and end apart: 6 -> 2, of which waited for: 6 -> 2; matrix products, arithmetic and copies ran while one was open for 11% -> 0% of each run, Pallas kernels for 0% -> 0%
where the time goes in v1:
time: 87.2 us; the launch traced here: 86.8 us
  blocking collectives  41 us (47%)
  Pallas kernels  18.5 us (21%)
  waiting for transfers between devices  15.4 us (18%)
  starting transfers between devices  7.65 us (9%)
  local copies, waits for them, and re-layouts  3.94 us (5%)
    all_to_all x1, blocking collectives, local(): lax.all_to_all(sent, 'seq', split_axis=0, concat_axis=0, tiled=True)  41 us
    all_to_all x1, waiting for transfers between devices, local(): lax.all_to_all(conv, 'seq', split_axis=0, concat_axis=0, tiled=True)  14.7 us
    pallas_call x1, Pallas kernels, local(): pl.pallas_call(middle_kernel, out_shape=jax.ShapeDtypeStruct((BLOCKS, OUT...  13.3 us
    all_to_all x1, starting transfers between devices, local(): lax.all_to_all(conv, 'seq', split_axis=0, concat_axis=0, tiled=True)  4.11 us
    unnamed x32, local copies, waits for them, and re-layouts  3.93 us
    ppermute x1, starting transfers between devices, local(): halo = lax.ppermute(last_rows, 'seq', pairs)  3.54 us
    pallas_call x1, Pallas kernels, local(): pl.pallas_call(end_kernel, grid=(steps,), in_specs=[rows_spec, rows_spec,...  2.79 us
    pallas_call x1, Pallas kernels, local(): pl.pallas_call(front_kernel, grid=(steps,), in_specs=[rows_spec, rows_spe...  2.36 us
  transfers between devices with their start and end apart: 2, of which 2 were waited for; matrix products, arithmetic and copies ran while one was open for 0% of the time, Pallas kernels for 0%

profile of v1, /device:TPU:1, one launch (start us, length us, event | category | flops | bytes accessed | tf_op | source)
XLA Modules:
  0.0 86.8 jit_solution(15793618716163783679)
XLA Ops:
  0.0 0.0 copy-start
  0.0 1.0 %copy-done = bf16[512,512]{1,0:T(8,128)(2,1)S(1)} copy-done((bf16[512,512]{1,0:T(8,128)(2,1)S(1)}, bf16[512,512]{1,0:T(8,128)(2,1)}, u32[]{:S(2)}) %copy-start) | copy-done | bytes 524312
  1.0 0.0 copy-start.2
  1.0 1.0 %copy-done.2 = bf16[512,512]{1,0:T(8,128)(2,1)S(1)} copy-done((bf16[512,512]{1,0:T(8,128)(2,1)S(1)}, bf16[512,512]{1,0:T(8,128)(2,1)}, u32[]{:S(2)}) %copy-start.2) | copy-done | bytes 524312
  2.1 0.0 copy-start.5
  2.1 1.0 %copy-done.5 = bf16[512,512]{1,0:T(8,128)(2,1)S(1)} copy-done((bf16[512,512]{1,0:T(8,128)(2,1)S(1)}, bf16[512,512]{1,0:T(8,128)(2,1)}, u32[]{:S(2)}) %copy-start.5) | copy-done | bytes 524312
  3.1 0.0 copy-start.11
  3.1 0.7 copy-done.11
  3.9 2.4 %front.1 = bf16[32,144,128]{2,1,0:T(8,128)(2,1)S(1)} custom-call(bf16[512,512]{1,0:T(8,128)(2,1)S(1)} %copy-done, bf16[512,512]{1,0:T(8,128)(2,1)S(1)} %copy-done.2, bf16[512,512]{1,0:T(8,128)(2,1)S(1)} %copy-done.5, f32[3,3,512]{2,1,0:T(4,128)S(1)} %copy-done.11), custom_call_target="tpu_custom_call" | custom-call | tf_op jit(solution)/shard_map/front/pallas_call | solution.py:228
  6.2 0.0 copy-start.6
  6.2 0.0 copy-start.7
  6.3 0.0 copy-start.8
  6.3 0.0 copy-start.9
  6.3 0.0 copy-start.10
  6.3 0.0 copy-start.13
  6.3 0.0 copy-start.14
  6.3 41.0 %all_to_all.10.in_ref = bf16[32,144,128]{2,1,0:T(8,128)(2,1)S(1)} all-to-all(bf16[32,144,128]{2,1,0:T(8,128)(2,1)S(1)} %front.1), channel_id=1, replica_groups=mesh['chan'=8,'seq'=32] {'seq'}, dimensions={0} | all-to-all | bytes 2359296 | tf_op jit(solution)/shard_map/all_to_all | solution.py:238
  47.4 0.0 copy-done.6
  47.4 0.0 copy-done.7
  47.4 0.0 copy-done.8
  47.4 0.0 copy-done.9
  47.4 0.0 copy-done.10
  47.4 0.0 copy-done.13
  47.4 0.0 copy-done.14
  47.4 0.0 copy-start.4
  47.4 13.3 %middle.1 = bf16[32,80,128]{2,1,0:T(8,128)(2,1)} custom-call(bf16[32,144,128]{2,1,0:T(8,128)(2,1)S(1)} %all_to_all.10.in_ref, bf16[256,384]{1,0:T(8,128)(2,1)S(1)} %copy-done.9, bf16[256,256]{1,0:T(8,128)(2,1)S(1)} %copy-done.10, bf16[768,256]{1,0:T(8,128)(2,1)S(1)} %copy-done.7, bf16[768,256]{1,0:T(8,128)(2,1)S(1)} %copy-done.6, ...), custom_call_target="tpu_custom_call" | custom-call | tf_op jit(solution)/shard_map/middle/pallas_call | solution.py:241
  60.8 0.0 copy-start.1
  60.8 0.0 copy-start.3
  60.8 0.0 copy-start.12
  60.8 0.0 copy-start.15
  60.8 4.1 %all-to-all-start.1 = ((bf16[32,80,128]{2,1,0:T(8,128)(2,1)}), bf16[32,80,128]{2,1,0:T(8,128)(2,1)S(1)}, u32[]{:S(2)}, u32[]{:S(2)}) async-start(bf16[32,80,128]{2,1,0:T(8,128)(2,1)} %middle.1), calls=%async_computation.1 | async-start | bytes 1310720 | tf_op jit(solution)/shard_map/all_to_all | solution.py:248
  64.9 0.0 copy-done.4
  64.9 0.0 copy-done.1
  65.0 0.0 copy-done.3
  65.0 3.5 %collective-permute-start = (bf16[3,2,512]{2,1,0:T(2,128)(2,1)S(1)}, bf16[3,2,512]{2,1,0:T(2,128)(2,1)S(1)}, u32[]{:S(2)}, u32[]{:S(2)}) collective-permute-start(bf16[3,2,512]{2,1,0:T(2,128)(2,1)S(1)} %pad_maximum_fusion), channel_id=1, source_target_pairs={{0,1},{1,2},{2,3},{3,4},{4,5},{5,6},{6,7},{7,8},{8,9},{9,10},{10,1... | collective-permute-start | bytes 18440 | tf_op jit(solution)/shard_map/ppermute | solution.py:226
  68.5 0.8 collective-permute-done.halo_ref
  69.3 14.7 %all-to-all-done.1.conv_ref = bf16[32,80,128]{2,1,0:T(8,128)(2,1)S(1)} async-done(((bf16[32,80,128]{2,1,0:T(8,128)(2,1)}), bf16[32,80,128]{2,1,0:T(8,128)(2,1)S(1)}, u32[]{:S(2)}, u32[]{:S(2)}) %all-to-all-start.1) | async-done | bytes 655392 | tf_op jit(solution)/shard_map/all_to_all | solution.py:248
  84.0 0.0 copy-done.12
  84.0 0.0 copy-done.15
  84.0 2.8 %end.1 = bf16[512,512]{1,0:T(8,128)(2,1)} custom-call(bf16[512,512]{1,0:T(8,128)(2,1)S(1)} %copy-done.4, bf16[512,512]{1,0:T(8,128)(2,1)S(1)} %copy-done.1, bf16[512,512]{1,0:T(8,128)(2,1)S(1)} %copy-done.3, bf16[3,2,512]{2,1,0:T(2,128)(2,1)S(1)} %collective-permute-done.halo_ref, f32[3,3,512]{2,1,0:T(4,128)S(1)} %copy-done.12, f32[1,512]{1,0:T(1,128)S(1)} %bitcast.7, ...), custom_call_target="tpu_custom_call" | custom-call | tf_op jit(solution)/shard_map/end/pallas_call | solution.py:250
  (3 shorter events, 0.0 us)
Async XLA Ops:
  0.0 1.0 %copy-start = (bf16[512,512]{1,0:T(8,128)(2,1)S(1)}, bf16[512,512]{1,0:T(8,128)(2,1)}, u32[]{:S(2)}) copy-start(bf16[512,512]{1,0:T(8,128)(2,1)} %key_ref.3) | copy-start | bytes 1572868
  1.0 1.0 %copy-start.2 = (bf16[512,512]{1,0:T(8,128)(2,1)S(1)}, bf16[512,512]{1,0:T(8,128)(2,1)}, u32[]{:S(2)}) copy-start(bf16[512,512]{1,0:T(8,128)(2,1)} %value_ref.3) | copy-start | bytes 1572868
  2.1 1.0 %copy-start.5 = (bf16[512,512]{1,0:T(8,128)(2,1)S(1)}, bf16[512,512]{1,0:T(8,128)(2,1)}, u32[]{:S(2)}) copy-start(bf16[512,512]{1,0:T(8,128)(2,1)} %filter_ref.1) | copy-start | bytes 1572868
  3.1 0.7 copy-start.11
  6.2 41.1 %copy-start.6 = (bf16[768,256]{1,0:T(8,128)(2,1)S(1)}, bf16[768,256]{1,0:T(8,128)(2,1)}, u32[]{:S(2)}) copy-start(bf16[768,256]{1,0:T(8,128)(2,1)} %constant.17.clone.inv_ref) | copy-start | bytes 1179652
  6.2 41.1 %copy-start.7 = (bf16[768,256]{1,0:T(8,128)(2,1)S(1)}, bf16[768,256]{1,0:T(8,128)(2,1)}, u32[]{:S(2)}) copy-start(bf16[768,256]{1,0:T(8,128)(2,1)} %constant.16.clone.fwd_ref) | copy-start | bytes 1179652
  6.3 41.1 %copy-start.8 = (bf16[128,768]{1,0:T(8,128)(2,1)S(1)}, bf16[128,768]{1,0:T(8,128)(2,1)}, u32[]{:S(2)}) copy-start(bf16[128,768]{1,0:T(8,128)(2,1)} %constant.18.clone.last_ref) | copy-start | bytes 589828
  6.3 41.1 %copy-start.9 = (bf16[256,384]{1,0:T(8,128)(2,1)S(1)}, bf16[256,384]{1,0:T(8,128)(2,1)}, u32[]{:S(2)}) copy-start(bf16[256,384]{1,0:T(8,128)(2,1)} %constant.14.clone.first_ref) | copy-start | bytes 589828
  6.3 41.1 %copy-start.10 = (bf16[256,256]{1,0:T(8,128)(2,1)S(1)}, bf16[256,256]{1,0:T(8,128)(2,1)}, u32[]{:S(2)}) copy-start(bf16[256,256]{1,0:T(8,128)(2,1)} %constant.15.clone.first_exact_ref) | copy-start | bytes 393220
  6.3 41.1 %copy-start.13 = (f32[128,128]{1,0:T(8,128)S(1)}, f32[128,128]{1,0:T(8,128)}, u32[]{:S(2)}) copy-start(f32[128,128]{1,0:T(8,128)} %constant.20.clone.sin_ref) | copy-start | bytes 196612
  6.3 41.1 %copy-start.14 = (f32[128,128]{1,0:T(8,128)S(1)}, f32[128,128]{1,0:T(8,128)}, u32[]{:S(2)}) copy-start(f32[128,128]{1,0:T(8,128)} %constant.19.clone.cos_ref) | copy-start | bytes 196612
  47.4 17.5 %copy-start.4 = (bf16[512,512]{1,0:T(8,128)(2,1)S(1)}, bf16[512,512]{1,0:T(8,128)(2,1)}, u32[]{:S(2)}) copy-start(bf16[512,512]{1,0:T(8,128)(2,1)} %query_ref.1) | copy-start | bytes 1572868
  60.8 4.2 %copy-start.1 = (bf16[512,512]{1,0:T(8,128)(2,1)S(1)}, bf16[512,512]{1,0:T(8,128)(2,1)}, u32[]{:S(2)}) copy-start(bf16[512,512]{1,0:T(8,128)(2,1)} %key_ref.3) | copy-start | bytes 1572868
  60.8 4.2 %copy-start.3 = (bf16[512,512]{1,0:T(8,128)(2,1)S(1)}, bf16[512,512]{1,0:T(8,128)(2,1)}, u32[]{:S(2)}) copy-start(bf16[512,512]{1,0:T(8,128)(2,1)} %value_ref.3) | copy-start | bytes 1572868
  60.8 23.2 %copy-start.12 = (f32[3,3,512]{2,1,0:T(4,128)S(1)}, f32[3,3,512]{2,1,0:T(4,128)}, u32[]{:S(2)}) copy-start(f32[3,3,512]{2,1,0:T(4,128)} %taps_ref.3) | copy-start | bytes 55300
  60.8 23.2 %copy-start.15 = (f32[512]{0:T(512)S(1)}, f32[512]{0:T(512)}, u32[]{:S(2)}) copy-start(f32[512]{0:T(512)} %param.18) | copy-start | bytes 6148
  60.8 23.2 %all-to-all-start.1 = ((bf16[32,80,128]{2,1,0:T(8,128)(2,1)}), bf16[32,80,128]{2,1,0:T(8,128)(2,1)S(1)}, u32[]{:S(2)}, u32[]{:S(2)}) async-start(bf16[32,80,128]{2,1,0:T(8,128)(2,1)} %middle.1), calls=%async_computation.1 | async-start | bytes 1310720 | tf_op jit(solution)/shard_map/all_to_all | solution.py:248
  65.0 4.3 %collective-permute-start = (bf16[3,2,512]{2,1,0:T(2,128)(2,1)S(1)}, bf16[3,2,512]{2,1,0:T(2,128)(2,1)S(1)}, u32[]{:S(2)}, u32[]{:S(2)}) collective-permute-start(bf16[3,2,512]{2,1,0:T(2,128)(2,1)S(1)} %pad_maximum_fusion), channel_id=1, source_target_pairs={{0,1},{1,2},{2,3},{3,4},{4,5},{5,6},{6,7},{7,8},{8,9},{9,10},{10,1... | collective-permute-start | bytes 18440 | tf_op jit(solution)/shard_map/ppermute | solution.py:226

commit v2 on v1

--- a/solution.py
+++ b/solution.py
@@ -17,12 +17,14 @@
 LENGTH = SIDE * SIDE
 PACK = 16
 BLOCKS = 32
+NEAR = 4
 TOKENS = 512
 CHANS = 512
 QUARTERS = TOKENS // SIDE
+BATCH = 8
+UNROLL = 2
 GROUP = 128
 SENDS = GROUP // PACK
-IN_TILES = 2 * QUARTERS + 1
 OUT_TILES = QUARTERS + 1
 
 SPAN = 252.0
@@ -93,7 +95,19 @@
     )
 
 
-def front_kernel(key_ref, value_ref, filter_ref, taps_ref, out_ref, pad_ref, edge_ref):
+def put(out_ref, tile, block):
+    out_ref[:, tile * PACK : (tile + 1) * PACK, :] = block.T.astype(BF16).reshape(SENDS, PACK, SIDE)
+
+
+def turn_kernel(*refs):
+    *blocks, out_ref = refs
+    for i, ref in enumerate(blocks):
+        for q in range(QUARTERS):
+            block = ref[q * SIDE : (q + 1) * SIDE, :].astype(F32).T.astype(BF16)
+            out_ref[:, i, :, q * PACK : (q + 1) * PACK, :] = block.reshape(NEAR, 2, PACK, SIDE)
+
+
+def product_kernel(key_ref, value_ref, taps_ref, out_ref, pad_ref, edge_ref):
     zero = jnp.zeros((2, GROUP), F32)
     key = key_ref[...].astype(F32)
     value = value_ref[...].astype(F32)
@@ -118,23 +132,52 @@
             edge_ref[row : row + 1, :] = hi.astype(F32)
             edge_ref[row + 1 : row + 2, :] = lo.astype(F32)
 
-    def put(tile, block):
-        out_ref[:, tile * PACK : (tile + 1) * PACK, :] = block.T.astype(BF16).reshape(SENDS, PACK, SIDE)
-
     for q in range(QUARTERS):
-        rows = slice(q * SIDE, (q + 1) * SIDE)
-        put(q, code[rows])
-        put(QUARTERS + q, filter_ref[rows, :].astype(F32))
-    put(2 * QUARTERS, edge_ref[...])
-
-
-def middle_kernel(in_ref, first_ref, first_exact_ref, fwd_ref, inv_ref, last_ref, cos_ref, sin_ref, out_ref, prod_ref, filt_ref, conv_ref):
+        put(out_ref, q, code[q * SIDE : (q + 1) * SIDE])
+    put(out_ref, QUARTERS, edge_ref[...])
+
+
+def rotated(block, cos, sin):
+    lhs = []
+    for i in range(block.shape[1] // SIDE):
+        re, im = block[:SIDE, i * SIDE : (i + 1) * SIDE], block[SIDE:, i * SIDE : (i + 1) * SIDE]
+        hi, lo = split(jnp.concatenate([re * cos + im * sin, im * cos - re * sin], 1))
+        lhs.append(jnp.concatenate([hi, lo, hi], 1))
+    return jnp.concatenate(lhs, 0)
+
+
+def channels(rows, batch):
+    return jnp.concatenate([rows[pl.ds(BATCH * batch + i, SIDE, stride=PACK), :] for i in range(BATCH)], 1)
+
+
+def spectrum_kernel(place_ref, b0_ref, b1_ref, b2_ref, b3_ref, other_ref, first_ref, fwd_ref, cos_ref, sin_ref, out_ref, filt_ref):
+    me = place_ref[0]
+    z, y, core = me // 8, (me // 2) % 4, me % 2
+    for dy, ref in enumerate((b0_ref, b1_ref, b2_ref, b3_ref)):
+        for dz in range(NEAR):
+            chip = ((z + NEAR - dz) % NEAR) * 8 + ((y + NEAR - dy) % NEAR) * 2
+            for q in range(QUARTERS):
+                rows = slice(q * PACK, (q + 1) * PACK)
+                filt_ref[chip + core, q] = ref[dz, core, rows, :].astype(F32)
+                filt_ref[chip + 1 - core, q] = other_ref[dy, dz, rows, :].astype(F32)
+    filt_rows = filt_ref.reshape(BLOCKS * QUARTERS * PACK, SIDE)
+
+    def one_batch(batch, carry):
+        taps = channels(filt_rows, batch).astype(BF16)
+        filt = jnp.dot(first_ref[...], jnp.concatenate([taps, taps], 0), preferred_element_type=F32)
+        lhs = rotated(filt, cos_ref[...], sin_ref[...])
+        out_ref[pl.ds(batch * BATCH * SIDE, BATCH * SIDE), :] = jnp.dot(lhs, fwd_ref[...], preferred_element_type=F32)
+        return carry
+
+    lax.fori_loop(0, PACK // BATCH, one_batch, 0, unroll=UNROLL)
+
+
+def middle_kernel(in_ref, spectra_ref, first_ref, fwd_ref, inv_ref, last_ref, cos_ref, sin_ref, out_ref, prod_ref, conv_ref):
     rows = BLOCKS * QUARTERS * PACK
-    edge = in_ref[:, 2 * QUARTERS * PACK :, :].astype(F32)
+    edge = in_ref[:, QUARTERS * PACK :, :].astype(F32)
     scale = edge[:, :, 0:1]
     for q in range(QUARTERS):
         prod_ref[:, q] = decode(in_ref[:, q * PACK : (q + 1) * PACK, :].astype(F32), scale)
-        filt_ref[:, q] = in_ref[:, (QUARTERS + q) * PACK : (QUARTERS + q + 1) * PACK, :].astype(F32)
 
     def part(place, i):
         lane = 8 + place * 8 + 2 * i
@@ -149,48 +192,28 @@
     prod_ref[:, 0] = jnp.where(lane == 0, first, jnp.where(lane == 1, second, prod_ref[:, 0]))
 
     prod_rows = prod_ref.reshape(rows, SIDE)
-    filt_rows = filt_ref.reshape(rows, SIDE)
     conv_rows = conv_ref.reshape(rows, SIDE)
 
-    def halves(x):
-        return x[:SIDE], x[SIDE:]
-
-    def one_pair(pair, carry):
-        chans = [2 * pair, 2 * pair + 1]
+    def one_batch(batch, carry):
         cos, sin = cos_ref[...], sin_ref[...]
-
-        def channels(ref):
-            return jnp.concatenate([ref[pl.ds(c, SIDE, stride=PACK), :] for c in chans], 1)
-
-        hi, lo = split(channels(prod_rows))
+        hi, lo = split(channels(prod_rows, batch))
         data = jnp.dot(first_ref[...], jnp.concatenate([hi, lo, hi], 0), preferred_element_type=F32)
-        taps = channels(filt_rows).astype(BF16)
-        filt = jnp.dot(first_exact_ref[...], jnp.concatenate([taps, taps], 0), preferred_element_type=F32)
-
-        lhs = []
-        for block in (data, filt):
-            for i in range(2):
-                re, im = halves(block[:, i * SIDE : (i + 1) * SIDE])
-                both = jnp.concatenate([re * cos + im * sin, im * cos - re * sin], 1)
-                hi, lo = split(both)
-                lhs.append(jnp.concatenate([hi, lo, hi], 1))
-        spectra = jnp.dot(jnp.concatenate(lhs, 0), fwd_ref[...], preferred_element_type=F32)
-        x, h = spectra[: 2 * SIDE], spectra[2 * SIDE :]
+        x = jnp.dot(rotated(data, cos, sin), fwd_ref[...], preferred_element_type=F32)
+        h = spectra_ref[pl.ds(batch * BATCH * SIDE, BATCH * SIDE), :]
         x_re, x_im, h_re, h_im = x[:, :SIDE], x[:, SIDE:], h[:, :SIDE], h[:, SIDE:]
-        z = jnp.concatenate([x_re * h_re - x_im * h_im, x_re * h_im + x_im * h_re], 1)
-        hi, lo = split(z)
+        hi, lo = split(jnp.concatenate([x_re * h_re - x_im * h_im, x_re * h_im + x_im * h_re], 1))
         back = jnp.dot(jnp.concatenate([hi, lo, hi], 1), inv_ref[...], preferred_element_type=F32)
         cols = []
-        for i in range(2):
+        for i in range(BATCH):
             re, im = back[i * SIDE : (i + 1) * SIDE, :SIDE], back[i * SIDE : (i + 1) * SIDE, SIDE:]
             cols.append(jnp.concatenate([re * cos - im * sin, im * cos + re * sin], 0))
         hi, lo = split(jnp.concatenate(cols, 1))
         y = jnp.dot(last_ref[...], jnp.concatenate([hi, lo, hi], 0), preferred_element_type=F32)
-        for i, c in enumerate(chans):
-            conv_rows[pl.ds(c, SIDE, stride=PACK), :] = y[:, i * SIDE : (i + 1) * SIDE]
+        for i in range(BATCH):
+            conv_rows[pl.ds(BATCH * batch + i, SIDE, stride=PACK), :] = y[:, i * SIDE : (i + 1) * SIDE]
         return carry
 
-    lax.fori_loop(0, PACK // 2, one_pair, 0)
+    lax.fori_loop(0, PACK // BATCH, one_batch, 0, unroll=UNROLL)
 
     conv = [conv_ref[:, q] for q in range(QUARTERS)]
     largest = functools.reduce(jnp.maximum, [jnp.abs(c) for c in conv])
@@ -219,32 +242,73 @@
     steps = CHANS // GROUP
     rows_spec = pl.BlockSpec((TOKENS, GROUP), lambda i: (0, i))
     taps_spec = pl.BlockSpec((3, 3, GROUP), lambda i: (0, 0, i))
-    params = pltpu.CompilerParams(vmem_limit_bytes=48 * 1024 * 1024)
+    params = pltpu.CompilerParams(vmem_limit_bytes=60 * 1024 * 1024)
+    small = pltpu.CompilerParams(vmem_limit_bytes=32 * 1024 * 1024)
 
     last_rows = jnp.stack([query_input[-2:], key_input[-2:], value_input[-2:]])
     pairs = [(i, i + 1) for i in range(BLOCKS - 1)]
     halo = lax.ppermute(last_rows, "seq", pairs)
 
-    sent = pl.pallas_call(
-        front_kernel,
+    def swap(x):
+        return lax.all_to_all(x, "seq", split_axis=0, concat_axis=0, tiled=True)
+
+    first, first_exact, fwd, inv, last, cos, sin = [jnp.asarray(c) for c in consts]
+    me = lax.axis_index("seq")
+    z, y, core = me // 8, (me // 2) % 4, me % 2
+    every = range(BLOCKS)
+    along_z = [[(i, (i + 8 * d) % 32) for i in every] for d in range(NEAR)]
+    along_y = [[(i, i // 8 * 8 + (i + 2 * d) % 8) for i in every] for d in range(NEAR)]
+
+    def filter_for(d):
+        part = lax.dynamic_slice_in_dim(filter_taps, (z + d) % NEAR * GROUP, GROUP, 1)
+        return lax.ppermute(part, "seq", along_z[d]) if d else part
+
+    turned = pl.pallas_call(
+        turn_kernel,
+        out_shape=jax.ShapeDtypeStruct((NEAR, NEAR, 2, QUARTERS * PACK, SIDE), BF16),
+        compiler_params=small,
+        cost_estimate=pl.CostEstimate(flops=10**8, bytes_accessed=2**20, transcendentals=0),
+        name="turn",
+    )(*[filter_for(d) for d in range(NEAR)])
+
+    def turned_for(d):
+        part = lax.dynamic_index_in_dim(turned, (y + d) % NEAR, 0, keepdims=False)
+        return lax.ppermute(part, "seq", along_y[d]) if d else part
+
+    bands = [turned_for(d) for d in range(NEAR)]
+    to_other = jnp.stack([lax.dynamic_index_in_dim(b, 1 - core, 1, keepdims=False) for b in bands])
+    from_other = lax.ppermute(to_other, "seq", [(i, i ^ 1) for i in every])
+
+    product_sent = pl.pallas_call(
+        product_kernel,
         grid=(steps,),
-        in_specs=[rows_spec, rows_spec, rows_spec, taps_spec],
-        out_specs=pl.BlockSpec((SENDS, IN_TILES * PACK, SIDE), lambda i: (i, 0, 0)),
-        out_shape=jax.ShapeDtypeStruct((BLOCKS, IN_TILES * PACK, SIDE), BF16),
+        in_specs=[rows_spec, rows_spec, taps_spec],
+        cost_estimate=pl.CostEstimate(flops=10**8, bytes_accessed=2**22, transcendentals=0),
+        out_specs=pl.BlockSpec((SENDS, OUT_TILES * PACK, SIDE), lambda i: (i, 0, 0)),
+        out_shape=jax.ShapeDtypeStruct((BLOCKS, OUT_TILES * PACK, SIDE), BF16),
         scratch_shapes=[pltpu.VMEM((TOKENS + 8, GROUP), F32), pltpu.VMEM((SIDE, GROUP), F32)],
         compiler_params=params,
-        name="front",
-    )(key_input, value_input, filter_taps, short_taps)
-    arrived = lax.all_to_all(sent, "seq", split_axis=0, concat_axis=0, tiled=True)
+        name="product",
+    )(key_input, value_input, short_taps)
+    product_arrived = swap(product_sent)
 
     work = pltpu.VMEM((BLOCKS, QUARTERS, PACK, SIDE), F32)
+    spectra = pl.pallas_call(
+        spectrum_kernel,
+        out_shape=jax.ShapeDtypeStruct((PACK * SIDE, 2 * SIDE), F32),
+        in_specs=[pl.BlockSpec(memory_space=pltpu.SMEM)] + [pl.BlockSpec(memory_space=pltpu.VMEM)] * 9,
+        scratch_shapes=[work],
+        compiler_params=small,
+        cost_estimate=pl.CostEstimate(flops=4 * 10**9, bytes_accessed=4 * 10**6, transcendentals=0),
+        name="spectrum",
+    )(me.astype(jnp.int32)[None], *bands, from_other, first_exact, fwd, cos, sin)
     conv = pl.pallas_call(
         middle_kernel,
         out_shape=jax.ShapeDtypeStruct((BLOCKS, OUT_TILES * PACK, SIDE), BF16),
-        scratch_shapes=[work, work, work],
-        compiler_params=params,
+        scratch_shapes=[work, work],
+        compiler_params=small,
         name="middle",
-    )(arrived, *[jnp.asarray(c) for c in consts])
+    )(product_arrived, spectra, first, fwd, inv, last, cos, sin)
     returned = lax.all_to_all(conv, "seq", split_axis=0, concat_axis=0, tiled=True)
 
     return pl.pallas_call(
@@ -262,7 +326,7 @@
         out_specs=rows_spec,
         out_shape=jax.ShapeDtypeStruct((TOKENS, CHANS), BF16),
         scratch_shapes=[pltpu.VMEM((TOKENS + 8, GROUP), F32)],
-        compiler_params=params,
+        compiler_params=small,
         name="end",
     )(query_input, key_input, value_input, halo, short_taps, skip_gain[None, :], returned)
 

time: 87.2 us -> 77 us (0.88)
  blocking collectives: 41 us -> 0 us
  starting transfers between devices: 7.65 us -> 27.5 us
  waiting for transfers between devices: 15.4 us -> 28.1 us
  Pallas kernels: 18.5 us -> 15.5 us
  local copies, waits for them, and re-layouts: 3.94 us -> 5.12 us
    all_to_all x1 -> x0, blocking collectives: 41 us -> none  [local(): lax.all_to_all(sent, 'seq', split_axis=0, concat_axis=0, tiled=True)]
    ppermute x0 -> x7, waiting for transfers between devices: none -> 12.8 us  [the longest x3 11.6 us: turned_for(): return lax.ppermute(part, 'seq', along_y[d]) if d else part]
    ppermute x0 -> x7, starting transfers between devices: none -> 10.9 us  [the longest x3 6.26 us: filter_for(): return lax.ppermute(part, 'seq', along_z[d]) if d else part]
    all_to_all x0 -> x1, starting transfers between devices: none -> 6.74 us  [swap(): return lax.all_to_all(x, 'seq', split_axis=0, concat_axis=0, tiled=True)]
    pallas_call x1, Pallas kernels: 13.3 us -> 6.67 us  [local(): pl.pallas_call(middle_kernel, out_shape=jax.ShapeDtypeStruct((BLOCKS, OUT...]
    pallas_call x1 -> x3, Pallas kernels: 2.36 us -> 6.04 us  [the longest x1 4.24 us: local(): pl.pallas_call(product_kernel, grid=(steps,), in_specs=[rows_spec, rows_s...]
    all_to_all x1, starting transfers between devices: 4.11 us -> 6.33 us  [local(): lax.all_to_all(conv, 'seq', split_axis=0, concat_axis=0, tiled=True)]
    dynamic_slice x0 -> x1, local copies, waits for them, and re-layouts: none -> 1.14 us  [filter_for(): lax.dynamic_slice_in_dim(filter_taps, (z + d) % NEAR * GROUP, GROUP, 1)]
  transfers between devices with their start and end apart: 2 -> 10, of which waited for: 2 -> 6; matrix products, arithmetic and copies ran while one was open for 0% -> 0% of each run, Pallas kernels for 0% -> 8%
where the time goes in v2:
time: 77 us; the launch traced here: 76.6 us
  waiting for transfers between devices  28.1 us (36%)
  starting transfers between devices  27.5 us (36%)
  Pallas kernels  15.5 us (20%)
  local copies, waits for them, and re-layouts  5.12 us (7%)
    all_to_all x1, waiting for transfers between devices, local(): lax.all_to_all(conv, 'seq', split_axis=0, concat_axis=0, tiled=True)  14.6 us
    ppermute x3, waiting for transfers between devices, turned_for(): return lax.ppermute(part, 'seq', along_y[d]) if d else part  11.6 us
    all_to_all x1, starting transfers between devices, swap(): return lax.all_to_all(x, 'seq', split_axis=0, concat_axis=0, tiled=True)  6.74 us
    pallas_call x1, Pallas kernels, local(): pl.pallas_call(middle_kernel, out_shape=jax.ShapeDtypeStruct((BLOCKS, OUT...  6.67 us
    all_to_all x1, starting transfers between devices, local(): lax.all_to_all(conv, 'seq', split_axis=0, concat_axis=0, tiled=True)  6.33 us
    ppermute x3, starting transfers between devices, filter_for(): return lax.ppermute(part, 'seq', along_z[d]) if d else part  6.26 us
    pallas_call x1, Pallas kernels, local(): pl.pallas_call(product_kernel, grid=(steps,), in_specs=[rows_spec, rows_s...  4.24 us
    unnamed x30, local copies, waits for them, and re-layouts  3.89 us
  transfers between devices with their start and end apart: 10, of which 6 were waited for; matrix products, arithmetic and copies ran while one was open for 0% of the time, Pallas kernels for 8%

profile of v2, /device:TPU:1, one launch (start us, length us, event | category | flops | bytes accessed | tf_op | source)
XLA Modules:
  0.0 76.6 jit_solution(18264989010433155923)
XLA Ops:
  0.0 1.1 %constant_dynamic-slice_fusion = (bf16[512,128]{1,0:T(8,128)(2,1)S(1)}, bf16[512,128]{1,0:T(8,128)(2,1)S(1)}, bf16[512,128]{1,0:T(8,128)(2,1)S(1)}, bf16[512,128]{1,0:T(8,128)(2,1)S(1)}) fusion(bf16[512,512]{1,0:T(8,128)(2,1)} %param.16, s32[]{:T(128)S(6)} %select_n.94, s32[]{:T(128)S(6)} %select_n.90, s32[]{:T(128)S(6)} %select_n.88, s32[]{:T(128)S(6)} %select_n.92), kind=kLoop, calls=%fused_computation.10 | loop fusion | bytes 1048592 | tf_op jit(solution)/shard_map/dynamic_slice | solution.py:263
  1.1 2.5 %collective-permute-start.1 = (bf16[512,128]{1,0:T(8,128)(2,1)S(1)}, bf16[512,128]{1,0:T(8,128)(2,1)S(1)}, u32[]{:S(2)}, u32[]{:S(2)}) collective-permute-start(bf16[512,128]{1,0:T(8,128)(2,1)S(1)} %get-tuple-element.10), channel_id=1, source_target_pairs={{0,8},{1,9},{2,10},{3,11},{4,12},{5,13},{6,14},{7,15},{8,16},{9,17... | collective-permute-start | bytes 393224 | tf_op jit(solution)/shard_map/ppermute | solution.py:264
  3.7 3.0 %collective-permute-start.2 = (bf16[512,128]{1,0:T(8,128)(2,1)S(1)}, bf16[512,128]{1,0:T(8,128)(2,1)S(1)}, u32[]{:S(2)}, u32[]{:S(2)}) collective-permute-start(bf16[512,128]{1,0:T(8,128)(2,1)S(1)} %get-tuple-element.12), channel_id=1, source_target_pairs={{0,16},{1,17},{2,18},{3,19},{4,20},{5,21},{6,22},{7,23},{8,24},{9,... | collective-permute-start | bytes 393224 | tf_op jit(solution)/shard_map/ppermute | solution.py:264
  6.7 0.7 collective-permute-start.3
  7.4 4.2 %product.1 = bf16[32,80,128]{2,1,0:T(8,128)(2,1)} custom-call(bf16[512,512]{1,0:T(8,128)(2,1)} %key_ref.3, bf16[512,512]{1,0:T(8,128)(2,1)} %value_ref.3, f32[3,3,512]{2,1,0:T(4,128)} %taps_ref.3), custom_call_target="tpu_custom_call" | custom-call | flops 100000000 | bytes 4194304 | tf_op jit(solution)/shard_map/product/pallas_call | solution.py:282
  11.7 0.0 copy-start.5
  11.7 0.0 copy-start.10
  11.7 0.0 copy-start.11
  11.7 0.0 copy-start.14
  11.7 6.7 %all-to-all-start = ((bf16[32,80,128]{2,1,0:T(8,128)(2,1)}), bf16[32,80,128]{2,1,0:T(8,128)(2,1)S(1)}, u32[]{:S(2)}, u32[]{:S(2)}) async-start(bf16[32,80,128]{2,1,0:T(8,128)(2,1)} %product.1), calls=%async_computation | async-start | bytes 1310720 | tf_op jit(solution)/shard_map/all_to_all | solution.py:253
  18.5 0.0 collective-permute-done.1.refs_1_
  18.5 0.0 collective-permute-done.2.refs_2_
  18.5 0.0 collective-permute-done.3.refs_3_
  18.6 0.2 turn.1
  18.8 0.1 dynamic-slice_bitcast_fusion
  18.8 2.7 %collective-permute-start.6 = (bf16[4,2,64,128]{3,2,1,0:T(8,128)(2,1)S(1)}, bf16[4,2,64,128]{3,2,1,0:T(8,128)(2,1)S(1)}, u32[]{:S(2)}, u32[]{:S(2)}) collective-permute-start(bf16[4,2,64,128]{3,2,1,0:T(8,128)(2,1)S(1)} %get-tuple-element.5), channel_id=1, source_target_pairs={{0,6},{1,7},{2,0},{3,1},{4,2},{5,3},{6,4},{7,5},{8,14},{9,15},{10,... | collective-permute-start | bytes 393224 | tf_op jit(solution)/shard_map/ppermute | solution.py:276
  21.5 0.6 collective-permute-start.5
  22.1 0.6 collective-permute-start.4
  22.7 5.9 %collective-permute-done.6.b3_ref = bf16[4,2,64,128]{3,2,1,0:T(8,128)(2,1)S(1)} collective-permute-done((bf16[4,2,64,128]{3,2,1,0:T(8,128)(2,1)S(1)}, bf16[4,2,64,128]{3,2,1,0:T(8,128)(2,1)S(1)}, u32[]{:S(2)}, u32[]{:S(2)}) %collective-permute-start.6) | collective-permute-done | bytes 131104 | tf_op jit(solution)/shard_map/ppermute | solution.py:276
  28.6 1.5 %collective-permute-done.5.b2_ref = bf16[4,2,64,128]{3,2,1,0:T(8,128)(2,1)S(1)} collective-permute-done((bf16[4,2,64,128]{3,2,1,0:T(8,128)(2,1)S(1)}, bf16[4,2,64,128]{3,2,1,0:T(8,128)(2,1)S(1)}, u32[]{:S(2)}, u32[]{:S(2)}) %collective-permute-start.5) | collective-permute-done | bytes 131104 | tf_op jit(solution)/shard_map/ppermute | solution.py:276
  30.1 4.2 %collective-permute-done.4.b1_ref = bf16[4,2,64,128]{3,2,1,0:T(8,128)(2,1)S(1)} collective-permute-done((bf16[4,2,64,128]{3,2,1,0:T(8,128)(2,1)S(1)}, bf16[4,2,64,128]{3,2,1,0:T(8,128)(2,1)S(1)}, u32[]{:S(2)}, u32[]{:S(2)}) %collective-permute-start.4) | collective-permute-done | bytes 131104 | tf_op jit(solution)/shard_map/ppermute | solution.py:276
  34.3 0.8 %collective-permute-start.7 = (bf16[4,4,64,128]{3,2,1,0:T(8,128)(2,1)S(1)}, bf16[4,4,64,128]{3,2,1,0:T(8,128)(2,1)S(1)}, u32[]{:S(2)}, u32[]{:S(2)}) collective-permute-start(bf16[4,4,64,128]{3,2,1,0:T(8,128)(2,1)S(1)} %pad_maximum_fusion), channel_id=1, source_target_pairs={{0,1},{1,0},{2,3},{3,2},{4,5},{5,4},{6,7},{7,6},{8,9},{9,8},{10,11... | collective-permute-start | bytes 786440 | tf_op jit(solution)/shard_map/ppermute | solution.py:280
  35.1 1.2 %collective-permute-done.7.other_ref = bf16[4,4,64,128]{3,2,1,0:T(8,128)(2,1)S(1)} collective-permute-done((bf16[4,4,64,128]{3,2,1,0:T(8,128)(2,1)S(1)}, bf16[4,4,64,128]{3,2,1,0:T(8,128)(2,1)S(1)}, u32[]{:S(2)}, u32[]{:S(2)}) %collective-permute-start.7) | collective-permute-done | bytes 262176 | tf_op jit(solution)/shard_map/ppermute | solution.py:280
  36.3 0.0 copy-done.5
  36.3 0.0 copy-done.10
  36.3 0.0 copy-done.11
  36.3 0.0 copy-done.14
  36.3 0.0 copy-start.6
  36.3 0.0 copy-start.7
  36.3 0.0 copy-start.8
  36.3 1.6 %spectrum.1.spectra_ref = f32[2048,256]{1,0:T(8,128)S(1)} custom-call(s32[1]{0:T(128)} %bitcast.4.place_ref, bf16[4,2,64,128]{3,2,1,0:T(8,128)(2,1)S(1)} %get-tuple-element.8.b0_ref, bf16[4,2,64,128]{3,2,1,0:T(8,128)(2,1)S(1)} %collective-permute-done.4.b1_ref, bf16[4,2,64,128]{3,2,1,0:T(8,128)(2,1)S(1)} %collective-permute-done.5.b2_ref, ...), custom_call_target="tpu_custom_call" | custom-call | flops 4000000000 | bytes 4000000 | tf_op jit(solution)/shard_map/spectrum/pallas_call | solution.py:296
  37.9 0.0 copy-start.2
  37.9 1.3 %copy-done.2 = f32[2048,256]{1,0:T(8,128)} copy-done((f32[2048,256]{1,0:T(8,128)}, f32[2048,256]{1,0:T(8,128)S(1)}, u32[]{:S(2)}) %copy-start.2) | copy-done | bytes 2097176
  39.3 0.0 copy-start
  39.3 0.0 copy-start.1
  39.3 0.0 all-to-all-done.in_ref
  39.3 0.0 copy-done.6
  39.3 0.0 copy-done.7
  39.3 0.0 copy-done.8
  39.3 0.0 copy-start.3
  39.3 1.7 %copy-done.3 = f32[2048,256]{1,0:T(8,128)S(1)} copy-done((f32[2048,256]{1,0:T(8,128)S(1)}, f32[2048,256]{1,0:T(8,128)}, u32[]{:S(2)}) %copy-start.3) | copy-done | bytes 2097176
  41.0 0.0 copy-start.12
  41.0 0.8 %copy-done.12 = f32[128,128]{1,0:T(8,128)S(1)} copy-done((f32[128,128]{1,0:T(8,128)S(1)}, f32[128,128]{1,0:T(8,128)}, u32[]{:S(2)}) %copy-start.12) | copy-done | bytes 65560
  41.8 0.0 copy-start.4
  41.8 0.0 copy-start.9
  41.8 0.0 copy-start.13
  41.8 6.7 %middle.1 = bf16[32,80,128]{2,1,0:T(8,128)(2,1)} custom-call(bf16[32,80,128]{2,1,0:T(8,128)(2,1)S(1)} %all-to-all-done.in_ref, f32[2048,256]{1,0:T(8,128)S(1)} %copy-done.3, bf16[256,384]{1,0:T(8,128)(2,1)S(1)} %copy-done.7, bf16[768,256]{1,0:T(8,128)(2,1)S(1)} %copy-done.5, bf16[768,256]{1,0:T(8,128)(2,1)S(1)} %copy-done.6, bf16[128,768]{1,0:T(8,128)(2,1)S(1)} %copy-done.8, ...), custom_call_target="tpu_custom_call" | custom-call | tf_op jit(solution)/shard_map/middle/pallas_call | solution.py:305
  48.5 6.3 %all-to-all-start.1 = ((bf16[32,80,128]{2,1,0:T(8,128)(2,1)}), bf16[32,80,128]{2,1,0:T(8,128)(2,1)S(1)}, u32[]{:S(2)}, u32[]{:S(2)}) async-start(bf16[32,80,128]{2,1,0:T(8,128)(2,1)} %middle.1), calls=%async_computation.1 | async-start | bytes 1310720 | tf_op jit(solution)/shard_map/all_to_all | solution.py:312
  54.8 0.0 copy-done.4
  54.9 0.0 copy-done
  54.9 0.0 copy-done.1
  54.9 3.5 %collective-permute-start = (bf16[3,2,512]{2,1,0:T(2,128)(2,1)S(1)}, bf16[3,2,512]{2,1,0:T(2,128)(2,1)S(1)}, u32[]{:S(2)}, u32[]{:S(2)}) collective-permute-start(bf16[3,2,512]{2,1,0:T(2,128)(2,1)S(1)} %pad_maximum_fusion.1), channel_id=1, source_target_pairs={{0,1},{1,2},{2,3},{3,4},{4,5},{5,6},{6,7},{7,8},{8,9},{9,10},{10,1... | collective-permute-start | bytes 18440 | tf_op jit(solution)/shard_map/ppermute | solution.py:250
  58.5 0.8 collective-permute-done.halo_ref
  59.2 14.6 %all-to-all-done.1.conv_ref = bf16[32,80,128]{2,1,0:T(8,128)(2,1)S(1)} async-done(((bf16[32,80,128]{2,1,0:T(8,128)(2,1)}), bf16[32,80,128]{2,1,0:T(8,128)(2,1)S(1)}, u32[]{:S(2)}, u32[]{:S(2)}) %all-to-all-start.1) | async-done | bytes 655392 | tf_op jit(solution)/shard_map/all_to_all | solution.py:312
  73.8 0.0 copy-done.9
  73.8 0.0 copy-done.13
  73.8 2.8 %end.1 = bf16[512,512]{1,0:T(8,128)(2,1)} custom-call(bf16[512,512]{1,0:T(8,128)(2,1)S(1)} %copy-done.4, bf16[512,512]{1,0:T(8,128)(2,1)S(1)} %copy-done, bf16[512,512]{1,0:T(8,128)(2,1)S(1)} %copy-done.1, bf16[3,2,512]{2,1,0:T(2,128)(2,1)S(1)} %collective-permute-done.halo_ref, f32[3,3,512]{2,1,0:T(4,128)S(1)} %copy-done.9, f32[1,512]{1,0:T(1,128)S(1)} %bitcast.24, ...), custom_call_target="tpu_custom_call" | custom-call | tf_op jit(solution)/shard_map/end/pallas_call | solution.py:314
  (8 shorter events, 0.1 us)
Async XLA Ops:
  1.1 17.4 %collective-permute-start.1 = (bf16[512,128]{1,0:T(8,128)(2,1)S(1)}, bf16[512,128]{1,0:T(8,128)(2,1)S(1)}, u32[]{:S(2)}, u32[]{:S(2)}) collective-permute-start(bf16[512,128]{1,0:T(8,128)(2,1)S(1)} %get-tuple-element.10), channel_id=1, source_target_pairs={{0,8},{1,9},{2,10},{3,11},{4,12},{5,13},{6,14},{7,15},{8,16},{9,17... | collective-permute-start | bytes 393224 | tf_op jit(solution)/shard_map/ppermute | solution.py:264
  3.7 14.8 %collective-permute-start.2 = (bf16[512,128]{1,0:T(8,128)(2,1)S(1)}, bf16[512,128]{1,0:T(8,128)(2,1)S(1)}, u32[]{:S(2)}, u32[]{:S(2)}) collective-permute-start(bf16[512,128]{1,0:T(8,128)(2,1)S(1)} %get-tuple-element.12), channel_id=1, source_target_pairs={{0,16},{1,17},{2,18},{3,19},{4,20},{5,21},{6,22},{7,23},{8,24},{9,... | collective-permute-start | bytes 393224 | tf_op jit(solution)/shard_map/ppermute | solution.py:264
  6.7 11.9 %collective-permute-start.3 = (bf16[512,128]{1,0:T(8,128)(2,1)S(1)}, bf16[512,128]{1,0:T(8,128)(2,1)S(1)}, u32[]{:S(2)}, u32[]{:S(2)}) collective-permute-start(bf16[512,128]{1,0:T(8,128)(2,1)S(1)} %get-tuple-element.9), channel_id=1, source_target_pairs={{0,24},{1,25},{2,26},{3,27},{4,28},{5,29},{6,30},{7,31},{8,0},{9,1... | collective-permute-start | bytes 393224 | tf_op jit(solution)/shard_map/ppermute | solution.py:264
  11.7 24.6 %copy-start.5 = (bf16[768,256]{1,0:T(8,128)(2,1)S(1)}, bf16[768,256]{1,0:T(8,128)(2,1)}, u32[]{:S(2)}) copy-start(bf16[768,256]{1,0:T(8,128)(2,1)} %constant.148.clone.fwd_ref) | copy-start | bytes 1179652
  11.7 24.6 %copy-start.10 = (f32[128,128]{1,0:T(8,128)S(1)}, f32[128,128]{1,0:T(8,128)}, u32[]{:S(2)}) copy-start(f32[128,128]{1,0:T(8,128)} %constant.151.clone.cos_ref) | copy-start | bytes 196612
  11.7 24.6 %copy-start.11 = (f32[128,128]{1,0:T(8,128)S(1)}, f32[128,128]{1,0:T(8,128)}, u32[]{:S(2)}) copy-start(f32[128,128]{1,0:T(8,128)} %constant.152.clone.sin_ref) | copy-start | bytes 196612
  11.7 24.6 %copy-start.14 = (bf16[256,256]{1,0:T(8,128)(2,1)S(1)}, bf16[256,256]{1,0:T(8,128)(2,1)}, u32[]{:S(2)}) copy-start(bf16[256,256]{1,0:T(8,128)(2,1)} %constant.147.clone.first_ref) | copy-start | bytes 393220
  11.7 27.6 %all-to-all-start = ((bf16[32,80,128]{2,1,0:T(8,128)(2,1)}), bf16[32,80,128]{2,1,0:T(8,128)(2,1)S(1)}, u32[]{:S(2)}, u32[]{:S(2)}) async-start(bf16[32,80,128]{2,1,0:T(8,128)(2,1)} %product.1), calls=%async_computation | async-start | bytes 1310720 | tf_op jit(solution)/shard_map/all_to_all | solution.py:253
  18.8 9.7 %collective-permute-start.6 = (bf16[4,2,64,128]{3,2,1,0:T(8,128)(2,1)S(1)}, bf16[4,2,64,128]{3,2,1,0:T(8,128)(2,1)S(1)}, u32[]{:S(2)}, u32[]{:S(2)}) collective-permute-start(bf16[4,2,64,128]{3,2,1,0:T(8,128)(2,1)S(1)} %get-tuple-element.5), channel_id=1, source_target_pairs={{0,6},{1,7},{2,0},{3,1},{4,2},{5,3},{6,4},{7,5},{8,14},{9,15},{10,... | collective-permute-start | bytes 393224 | tf_op jit(solution)/shard_map/ppermute | solution.py:276
  21.5 8.6 %collective-permute-start.5 = (bf16[4,2,64,128]{3,2,1,0:T(8,128)(2,1)S(1)}, bf16[4,2,64,128]{3,2,1,0:T(8,128)(2,1)S(1)}, u32[]{:S(2)}, u32[]{:S(2)}) collective-permute-start(bf16[4,2,64,128]{3,2,1,0:T(8,128)(2,1)S(1)} %get-tuple-element.6), channel_id=1, source_target_pairs={{0,4},{1,5},{2,6},{3,7},{4,0},{5,1},{6,2},{7,3},{8,12},{9,13},{10,... | collective-permute-start | bytes 393224 | tf_op jit(solution)/shard_map/ppermute | solution.py:276
  22.1 12.2 %collective-permute-start.4 = (bf16[4,2,64,128]{3,2,1,0:T(8,128)(2,1)S(1)}, bf16[4,2,64,128]{3,2,1,0:T(8,128)(2,1)S(1)}, u32[]{:S(2)}, u32[]{:S(2)}) collective-permute-start(bf16[4,2,64,128]{3,2,1,0:T(8,128)(2,1)S(1)} %get-tuple-element.7), channel_id=1, source_target_pairs={{0,2},{1,3},{2,4},{3,5},{4,6},{5,7},{6,0},{7,1},{8,10},{9,11},{10,... | collective-permute-start | bytes 393224 | tf_op jit(solution)/shard_map/ppermute | solution.py:276
  34.3 2.0 %collective-permute-start.7 = (bf16[4,4,64,128]{3,2,1,0:T(8,128)(2,1)S(1)}, bf16[4,4,64,128]{3,2,1,0:T(8,128)(2,1)S(1)}, u32[]{:S(2)}, u32[]{:S(2)}) collective-permute-start(bf16[4,4,64,128]{3,2,1,0:T(8,128)(2,1)S(1)} %pad_maximum_fusion), channel_id=1, source_target_pairs={{0,1},{1,0},{2,3},{3,2},{4,5},{5,4},{6,7},{7,6},{8,9},{9,8},{10,11... | collective-permute-start | bytes 786440 | tf_op jit(solution)/shard_map/ppermute | solution.py:280
  36.3 3.0 %copy-start.6 = (bf16[768,256]{1,0:T(8,128)(2,1)S(1)}, bf16[768,256]{1,0:T(8,128)(2,1)}, u32[]{:S(2)}) copy-start(bf16[768,256]{1,0:T(8,128)(2,1)} %constant.149.clone.inv_ref) | copy-start | bytes 1179652
  36.3 3.0 %copy-start.7 = (bf16[256,384]{1,0:T(8,128)(2,1)S(1)}, bf16[256,384]{1,0:T(8,128)(2,1)}, u32[]{:S(2)}) copy-start(bf16[256,384]{1,0:T(8,128)(2,1)} %constant.146.clone.first_ref) | copy-start | bytes 589828
  36.3 3.0 %copy-start.8 = (bf16[128,768]{1,0:T(8,128)(2,1)S(1)}, bf16[128,768]{1,0:T(8,128)(2,1)}, u32[]{:S(2)}) copy-start(bf16[128,768]{1,0:T(8,128)(2,1)} %constant.150.clone.last_ref) | copy-start | bytes 589828
  37.9 1.3 %copy-start.2 = (f32[2048,256]{1,0:T(8,128)}, f32[2048,256]{1,0:T(8,128)S(1)}, u32[]{:S(2)}) copy-start(f32[2048,256]{1,0:T(8,128)S(1)} %spectrum.1.spectra_ref) | copy-start | bytes 6291460
  39.3 15.6 %copy-start = (bf16[512,512]{1,0:T(8,128)(2,1)S(1)}, bf16[512,512]{1,0:T(8,128)(2,1)}, u32[]{:S(2)}) copy-start(bf16[512,512]{1,0:T(8,128)(2,1)} %key_ref.3) | copy-start | bytes 1572868
  39.3 15.6 %copy-start.1 = (bf16[512,512]{1,0:T(8,128)(2,1)S(1)}, bf16[512,512]{1,0:T(8,128)(2,1)}, u32[]{:S(2)}) copy-start(bf16[512,512]{1,0:T(8,128)(2,1)} %value_ref.3) | copy-start | bytes 1572868
  39.3 1.7 %copy-start.3 = (f32[2048,256]{1,0:T(8,128)S(1)}, f32[2048,256]{1,0:T(8,128)}, u32[]{:S(2)}) copy-start(f32[2048,256]{1,0:T(8,128)} %copy-done.2) | copy-start | bytes 6291460
  41.0 0.8 %copy-start.12 = (f32[128,128]{1,0:T(8,128)S(1)}, f32[128,128]{1,0:T(8,128)}, u32[]{:S(2)}) copy-start(f32[128,128]{1,0:T(8,128)} %constant.152.clone.sin_ref) | copy-start | bytes 196612
  41.8 13.0 %copy-start.4 = (bf16[512,512]{1,0:T(8,128)(2,1)S(1)}, bf16[512,512]{1,0:T(8,128)(2,1)}, u32[]{:S(2)}) copy-start(bf16[512,512]{1,0:T(8,128)(2,1)} %query_ref.1) | copy-start | bytes 1572868
  41.8 32.0 %copy-start.9 = (f32[3,3,512]{2,1,0:T(4,128)S(1)}, f32[3,3,512]{2,1,0:T(4,128)}, u32[]{:S(2)}) copy-start(f32[3,3,512]{2,1,0:T(4,128)} %taps_ref.3) | copy-start | bytes 55300
  41.8 32.0 %copy-start.13 = (f32[512]{0:T(512)S(1)}, f32[512]{0:T(512)}, u32[]{:S(2)}) copy-start(f32[512]{0:T(512)} %param.18) | copy-start | bytes 6148
  48.5 25.3 %all-to-all-start.1 = ((bf16[32,80,128]{2,1,0:T(8,128)(2,1)}), bf16[32,80,128]{2,1,0:T(8,128)(2,1)S(1)}, u32[]{:S(2)}, u32[]{:S(2)}) async-start(bf16[32,80,128]{2,1,0:T(8,128)(2,1)} %middle.1), calls=%async_computation.1 | async-start | bytes 1310720 | tf_op jit(solution)/shard_map/all_to_all | solution.py:312
  54.9 4.3 %collective-permute-start = (bf16[3,2,512]{2,1,0:T(2,128)(2,1)S(1)}, bf16[3,2,512]{2,1,0:T(2,128)(2,1)S(1)}, u32[]{:S(2)}, u32[]{:S(2)}) collective-permute-start(bf16[3,2,512]{2,1,0:T(2,128)(2,1)S(1)} %pad_maximum_fusion.1), channel_id=1, source_target_pairs={{0,1},{1,2},{2,3},{3,4},{4,5},{5,6},{6,7},{7,8},{8,9},{9,10},{10,1... | collective-permute-start | bytes 18440 | tf_op jit(solution)/shard_map/ppermute | solution.py:250

commit v3 on v2

v3 whole, which is shorter than its diff:
```python
import functools
import math

import jax
import jax.numpy as jnp
import ml_dtypes
import numpy as np
from jax import lax
from jax.experimental import pallas as pl
from jax.experimental.pallas import tpu as pltpu
from jax.sharding import PartitionSpec as P

F32 = jnp.float32
BF16 = jnp.bfloat16

SIDE = 128
LENGTH = SIDE * SIDE
PACK = 16
BLOCKS = 32
NEAR = 4
TOKENS = 512
CHANS = 512
QUARTERS = TOKENS // SIDE
BATCH = 8
UNROLL = 2
STEP_A, STEP_B, STEP_C, STEP_D = 8, 8, 4, 8
GROUP = 128
OUT_TILES = QUARTERS + 1

SPAN = 252.0
DROP = 125.5
TINY = 1e-35


def split_const(table):
    hi = table.astype(ml_dtypes.bfloat16)
    lo = (table - hi.astype(np.float64)).astype(ml_dtypes.bfloat16)
    return hi, lo


def tables():
    n = np.arange(SIDE, dtype=np.float64)
    ang = 2.0 * np.pi / SIDE * np.outer(n - 0.25, n)
    first = np.concatenate([np.cos(ang), -np.sin(ang)], 0)
    tw = 2.0 * np.pi / LENGTH * np.outer(n - 0.25, n)
    mid = 2.0 * np.pi / SIDE * (np.outer(n, n) % SIDE)
    cos, sin = np.cos(mid), np.sin(mid)
    fwd = np.block([[cos, -sin], [sin, cos]])
    first_hi, first_lo = split_const(first)
    fwd_hi, fwd_lo = split_const(fwd)
    matrices = np.concatenate([np.concatenate([first_hi, first_lo], 1), fwd_hi, fwd_lo], 0)
    return matrices, np.stack([np.cos(tw), np.sin(tw)]).astype(np.float32)


def split(x):
    hi = x.astype(BF16)
    lo = (x - hi.astype(F32)).astype(BF16)
    return hi, lo


def scale_up(largest):
    return jnp.maximum(largest * 1.004, TINY).astype(BF16).astype(F32)


def encode(x, inverse_scale):
    u = jnp.abs(x) * inverse_scale
    y = jnp.exp2(u * lax.rsqrt(jnp.maximum(u, TINY)) * SPAN - DROP)
    return jnp.where(x < 0.0, -y, y)


def decode(y, scale):
    g = (jnp.log2(jnp.abs(y)) + DROP) * (1.0 / SPAN)
    x = g * g * scale
    return jnp.where(y < 0.0, -x, x)


def turn_kernel(*refs):
    *blocks, out_ref = refs
    for i, ref in enumerate(blocks):
        for q in range(QUARTERS):
            block = ref[q * SIDE : (q + 1) * SIDE, :].astype(F32).T.astype(BF16)
            out_ref[:, i, :, q * PACK : (q + 1) * PACK, :] = block.reshape(NEAR, 2, PACK, SIDE)


def product_kernel(key_ref, value_ref, taps_ref, out_hbm, key_pad, value_pad, work_ref, edge_ref, out_ref, out_sems):
    key_pad[0:8, :] = jnp.zeros((8, CHANS), F32)
    value_pad[0:8, :] = jnp.zeros((8, CHANS), F32)

    def mix(pad, place, start):
        return (
            taps_ref[place, 0:1] * pad[pl.ds(8 + start, SIDE), :]
            + taps_ref[place, 1:2] * pad[pl.ds(7 + start, SIDE), :]
            + taps_ref[place, 2:3] * pad[pl.ds(6 + start, SIDE), :]
        )

    largest = jnp.zeros((1, CHANS), F32)
    for q in range(QUARTERS):
        rows = pl.ds(q * SIDE, SIDE)
        key_pad[pl.ds(8 + q * SIDE, SIDE), :] = key_ref[rows, :].astype(F32)
        value_pad[pl.ds(8 + q * SIDE, SIDE), :] = value_ref[rows, :].astype(F32)
        product = mix(key_pad, 1, q * SIDE) * mix(value_pad, 2, q * SIDE)
        work_ref[rows, :] = product
        largest = jnp.maximum(largest, jnp.max(jnp.abs(product), axis=0, keepdims=True))
    scale = scale_up(largest)
    inverse = 1.0 / scale

    out_copies = []

    def put(tile, block):
        rows = pl.ds(tile * PACK, PACK)
        out_ref[:, rows, :] = block.T.astype(BF16).reshape(BLOCKS, PACK, SIDE)
        copy = pltpu.make_async_copy(out_ref.at[:, rows], out_hbm.at[:, rows], out_sems.at[tile])
        copy.start()
        out_copies.append(copy)

    for q in range(QUARTERS):
        put(q, encode(work_ref[pl.ds(q * SIDE, SIDE), :], inverse))

    edge_ref[...] = jnp.zeros_like(edge_ref)
    edge_ref[0:1, :] = scale
    for place, pad in enumerate((key_pad, value_pad)):
        taps = taps_ref[place + 1]
        first, second = pad[8:9, :], pad[9:10, :]
        before, last = pad[TOKENS + 6 : TOKENS + 7, :], pad[TOKENS + 7 : TOKENS + 8, :]
        parts = (
            taps[0:1] * first,
            taps[0:1] * second + taps[1:2] * first,
            taps[1:2] * last + taps[2:3] * before,
            taps[2:3] * last,
        )
        for i, part in enumerate(parts):
            hi, lo = split(part)
            row = 8 + place * 8 + 2 * i
            edge_ref[row : row + 1, :] = hi.astype(F32)
            edge_ref[row + 1 : row + 2, :] = lo.astype(F32)
    put(QUARTERS, edge_ref[...])
    for copy in out_copies:
        copy.wait()


def rotated(block, cos, sin):
    lhs = []
    for i in range(block.shape[1] // SIDE):
        re, im = block[:SIDE, i * SIDE : (i + 1) * SIDE], block[SIDE:, i * SIDE : (i + 1) * SIDE]
        hi, lo = split(jnp.concatenate([re * cos + im * sin, im * cos - re * sin], 1))
        lhs.append(jnp.concatenate([hi, lo, hi], 1))
    return jnp.concatenate(lhs, 0)


def channels(rows, batch):
    return jnp.concatenate([rows[pl.ds(BATCH * batch + i, SIDE, stride=PACK), :] for i in range(BATCH)], 1)


def gather_filter(place_ref, band_refs, other_ref, filt_ref):
    me = place_ref[0]
    z, y, core = me // 8, (me // 2) % 4, me % 2
    for dy, ref in enumerate(band_refs):
        for dz in range(NEAR):
            chip = ((z + NEAR - dz) % NEAR) * 8 + ((y + NEAR - dy) % NEAR) * 2
            for q in range(QUARTERS):
                rows = slice(q * PACK, (q + 1) * PACK)
                filt_ref[chip + core, q] = ref[dz, core, rows, :].astype(F32)
                filt_ref[chip + 1 - core, q] = other_ref[dy, dz, rows, :].astype(F32)


def middle_kernel(
    place_ref, in_ref, b0_ref, b1_ref, b2_ref, b3_ref, other_ref,
    mats_ref, twiddle_ref,
    out_ref, prod_ref, filt_ref, conv_ref,
):
    gather_filter(place_ref, (b0_ref, b1_ref, b2_ref, b3_ref), other_ref, filt_ref)
    rows = BLOCKS * QUARTERS * PACK
    edge = in_ref[:, QUARTERS * PACK :, :].astype(F32)
    scale = edge[:, :, 0:1]
    for q in range(QUARTERS):
        prod_ref[:, q] = decode(in_ref[:, q * PACK : (q + 1) * PACK, :].astype(F32), scale)

    def part(place, i):
        lane = 8 + place * 8 + 2 * i
        return edge[:, :, lane : lane + 1] + edge[:, :, lane + 1 : lane + 2]

    def behind(x):
        return jnp.concatenate([jnp.zeros_like(x[:1]), x[:-1]], 0)

    first = (part(0, 0) + behind(part(0, 2))) * (part(1, 0) + behind(part(1, 2)))
    second = (part(0, 1) + behind(part(0, 3))) * (part(1, 1) + behind(part(1, 3)))
    lane = lax.broadcasted_iota(jnp.int32, (BLOCKS, PACK, SIDE), 2)
    prod_ref[:, 0] = jnp.where(lane == 0, first, jnp.where(lane == 1, second, prod_ref[:, 0]))

    prod_rows = prod_ref.reshape(rows, SIDE)
    filt_rows = filt_ref.reshape(rows, SIDE)
    conv_rows = conv_ref.reshape(rows, SIDE)

    def turned(x):
        return x.astype(F32).T

    two = 2 * SIDE
    first_exact = mats_ref[:two, :]
    first_hi, first_lo = first_exact[:, :SIDE], first_exact[:, SIDE:]
    fwd_hi, fwd_lo = mats_ref[two : 2 * two, :], mats_ref[2 * two :, :]
    inv_hi, inv_lo = turned(fwd_hi).astype(BF16), turned(fwd_lo).astype(BF16)
    last_hi, last_lo = [(turned(x) * (1.0 / LENGTH)).astype(BF16) for x in (first_hi, first_lo)]
    first = jnp.concatenate(
        [jnp.concatenate([first_hi, first_hi], 1), jnp.concatenate([first_lo, jnp.zeros_like(first_lo)], 1)], 0
    )
    fwd = jnp.concatenate([fwd_hi, fwd_hi, fwd_lo], 0)
    inv = jnp.concatenate([inv_hi, inv_hi, inv_lo], 0)
    last = jnp.concatenate([last_hi, last_lo], 0)

    def dot(left, right):
        return jnp.dot(left, right, preferred_element_type=F32)

    def by_rows(left, right, step):
        return jnp.concatenate([dot(left[i : i + step * SIDE], right) for i in range(0, BATCH * SIDE, step * SIDE)], 0)

    def by_columns(left, right, step):
        return jnp.concatenate([dot(left, right[:, i : i + step * SIDE]) for i in range(0, BATCH * SIDE, step * SIDE)], 1)

    def one_batch(batch, carry):
        cos, sin = twiddle_ref[0], twiddle_ref[1]
        hi, lo = split(channels(prod_rows, batch))
        data = by_columns(first, jnp.concatenate([hi, lo], 0), STEP_A)
        data = data[:two] + data[two:]
        taps = channels(filt_rows, batch).astype(BF16)
        filt = by_columns(first_exact, jnp.concatenate([taps, taps], 0), STEP_A)
        x = by_rows(rotated(data, cos, sin), fwd, STEP_B)
        h = by_rows(rotated(filt, cos, sin), fwd, STEP_B)
        x_re, x_im, h_re, h_im = x[:, :SIDE], x[:, SIDE:], h[:, :SIDE], h[:, SIDE:]
        hi, lo = split(jnp.concatenate([x_re * h_re - x_im * h_im, x_re * h_im + x_im * h_re], 1))
        back = by_rows(jnp.concatenate([hi, lo, hi], 1), inv, STEP_C)
        cols = []
        for i in range(BATCH):
            re, im = back[i * SIDE : (i + 1) * SIDE, :SIDE], back[i * SIDE : (i + 1) * SIDE, SIDE:]
            cols.append(jnp.concatenate([re * cos - im * sin, im * cos + re * sin], 0))
        hi, lo = split(jnp.concatenate(cols, 1))
        y = by_columns(last, hi, STEP_D)
        y = y[:SIDE] + y[SIDE:] + by_columns(last_hi, lo, STEP_D)
        for i in range(BATCH):
            conv_rows[pl.ds(BATCH * batch + i, SIDE, stride=PACK), :] = y[:, i * SIDE : (i + 1) * SIDE]
        return carry

    lax.fori_loop(0, PACK // BATCH, one_batch, 0, unroll=UNROLL)

    conv = [conv_ref[:, q] for q in range(QUARTERS)]
    largest = functools.reduce(jnp.maximum, [jnp.abs(c) for c in conv])
    scale = scale_up(jnp.max(largest, axis=2, keepdims=True))
    inverse = 1.0 / scale
    for q in range(QUARTERS):
        out_ref[:, q * PACK : (q + 1) * PACK, :] = encode(conv[q], inverse).astype(BF16)
    out_ref[:, QUARTERS * PACK :, :] = jnp.broadcast_to(scale, (BLOCKS, PACK, SIDE)).astype(BF16)


def end_kernel(query_ref, key_ref, value_ref, halo_ref, taps_ref, gain_ref, conv_ref, out_hbm, query_pad, key_pad, value_pad, out_ref, sems):
    pads = (query_pad, key_pad, value_pad)
    for place, pad in enumerate(pads):
        pad[6:8, :] = halo_ref[place].astype(F32)

    def mix(place, ref, start):
        pad, taps = pads[place], taps_ref[place]
        pad[pl.ds(8 + start, SIDE), :] = ref[pl.ds(start, SIDE), :].astype(F32)
        return (
            taps[0:1] * pad[pl.ds(8 + start, SIDE), :]
            + taps[1:2] * pad[pl.ds(7 + start, SIDE), :]
            + taps[2:3] * pad[pl.ds(6 + start, SIDE), :]
        )

    scale = conv_ref[:, QUARTERS * PACK :, 0:1].astype(F32)
    copies = []
    for q in range(QUARTERS):
        start = q * SIDE
        rows = pl.ds(start, SIDE)
        conv = decode(conv_ref[:, q * PACK : (q + 1) * PACK, :].astype(F32), scale)
        direct = gain_ref[...] * (mix(1, key_ref, start) * mix(2, value_ref, start))
        out_ref[rows, :] = (mix(0, query_ref, start) * (conv.reshape(CHANS, SIDE).T + direct)).astype(BF16)
        copy = pltpu.make_async_copy(out_ref.at[rows], out_hbm.at[rows], sems.at[q])
        copy.start()
        copies.append(copy)
    for copy in copies:
        copy.wait()


def local(consts, query_input, key_input, value_input, filter_taps, short_taps, skip_gain):
    small = pltpu.CompilerParams(vmem_limit_bytes=32 * 1024 * 1024)

    last_rows = jnp.stack([query_input[-2:], key_input[-2:], value_input[-2:]])
    pairs = [(i, i + 1) for i in range(BLOCKS - 1)]
    halo = lax.ppermute(last_rows, "seq", pairs)

    def swap(x):
        return lax.all_to_all(x, "seq", split_axis=0, concat_axis=0, tiled=True)

    me = lax.axis_index("seq")
    z, y, core = me // 8, (me // 2) % 4, me % 2
    every = range(BLOCKS)
    along_z = [[(i, (i + 8 * d) % 32) for i in every] for d in range(NEAR)]
    along_y = [[(i, i // 8 * 8 + (i + 2 * d) % 8) for i in every] for d in range(NEAR)]

    def filter_for(d):
        part = lax.dynamic_slice_in_dim(filter_taps, (z + d) % NEAR * GROUP, GROUP, 1)
        return lax.ppermute(part, "seq", along_z[d]) if d else part

    turned = pl.pallas_call(
        turn_kernel,
        out_shape=jax.ShapeDtypeStruct((NEAR, NEAR, 2, QUARTERS * PACK, SIDE), BF16),
        compiler_params=small,
        cost_estimate=pl.CostEstimate(flops=2 * 10**10, bytes_accessed=2**20, transcendentals=0),
        name="turn",
    )(*[filter_for(d) for d in range(NEAR)])

    def turned_for(d):
        part = lax.dynamic_index_in_dim(turned, (y + d) % NEAR, 0, keepdims=False)
        return lax.ppermute(part, "seq", along_y[d]) if d else part

    bands = [turned_for(d) for d in range(NEAR)]
    to_other = jnp.stack([lax.dynamic_index_in_dim(b, 1 - core, 1, keepdims=False) for b in bands])
    from_other = lax.ppermute(to_other, "seq", [(i, i ^ 1) for i in every])

    hbm = pl.BlockSpec(memory_space=pl.ANY)
    vmem = pl.BlockSpec(memory_space=pltpu.VMEM)
    product_sent = pl.pallas_call(
        product_kernel,
        in_specs=[vmem, vmem, vmem],
        out_specs=hbm,
        out_shape=jax.ShapeDtypeStruct((BLOCKS, OUT_TILES * PACK, SIDE), BF16),
        scratch_shapes=[
            pltpu.VMEM((TOKENS + 8, CHANS), F32),
            pltpu.VMEM((TOKENS + 8, CHANS), F32),
            pltpu.VMEM((TOKENS, CHANS), F32),
            pltpu.VMEM((SIDE, CHANS), F32),
            pltpu.VMEM((BLOCKS, OUT_TILES * PACK, SIDE), BF16),
            pltpu.SemaphoreType.DMA((OUT_TILES,)),
        ],
        compiler_params=small,
        cost_estimate=pl.CostEstimate(flops=2 * 10**10, bytes_accessed=2**22, transcendentals=0),
        name="product",
    )(key_input, value_input, short_taps)
    product_arrived = swap(product_sent)

    work = pltpu.VMEM((BLOCKS, QUARTERS, PACK, SIDE), F32)
    conv = pl.pallas_call(
        middle_kernel,
        out_shape=jax.ShapeDtypeStruct((BLOCKS, OUT_TILES * PACK, SIDE), BF16),
        in_specs=[pl.BlockSpec(memory_space=pltpu.SMEM)] + [pl.BlockSpec(memory_space=pltpu.VMEM)] * 8,
        scratch_shapes=[work, work, work],
        compiler_params=small,
        cost_estimate=pl.CostEstimate(flops=8 * 10**9, bytes_accessed=2 * 10**6, transcendentals=0),
        name="middle",
    )(me.astype(jnp.int32)[None], product_arrived, *bands, from_other, *[jnp.asarray(c) for c in consts])
    returned = lax.all_to_all(conv, "seq", split_axis=0, concat_axis=0, tiled=True)

    pad = pltpu.VMEM((TOKENS + 8, CHANS), F32)
    return pl.pallas_call(
        end_kernel,
        in_specs=[vmem] * 7,
        out_specs=hbm,
        out_shape=jax.ShapeDtypeStruct((TOKENS, CHANS), BF16),
        scratch_shapes=[pad, pad, pad, pltpu.VMEM((TOKENS, CHANS), BF16), pltpu.SemaphoreType.DMA((QUARTERS,))],
        compiler_params=small,
        name="end",
    )(query_input, key_input, value_input, halo, short_taps, skip_gain[None, :], returned)


def solution(mesh):
    placed = (
        P("seq", "chan"),
        P("seq", "chan"),
        P("seq", "chan"),
        P("seq", "chan"),
        P(None, None, "chan"),
        P("chan"),
    )
    return jax.shard_map(
        functools.partial(local, tables()),
        mesh=mesh,
        in_specs=placed,
        out_specs=P("seq", "chan"),
        check_vma=False,
    )
```

time: 77 us -> 69.8 us (0.906)
  local copies, waits for them, and re-layouts: 5.12 us -> 1.36 us
  Pallas kernels: 15.5 us -> 12 us
    pallas_call x3 -> x2, Pallas kernels: 8.63 us -> 4.76 us  [the longest x1 2.45 us: local(): pl.pallas_call(end_kernel, in_specs=[vmem] * 7, out_specs=hbm, out_shape=...]
    unnamed x30 -> x14, local copies, waits for them, and re-layouts: 3.89 us -> 0.03 us
    all_to_all x1, starting transfers between devices: 6.33 us -> 5.4 us  [local(): lax.all_to_all(conv, 'seq', split_axis=0, concat_axis=0, tiled=True)]
    all_to_all x1, waiting for transfers between devices: 0.01 us -> 0.87 us  [swap(): return lax.all_to_all(x, 'seq', split_axis=0, concat_axis=0, tiled=True)]
  transfers between devices with their start and end apart: 10 -> 10, of which waited for: 6 -> 6; matrix products, arithmetic and copies ran while one was open for 0% -> 0% of each run, Pallas kernels for 8% -> 4%
where the time goes in v3:
time: 69.8 us; the launch traced here: 69.4 us
  waiting for transfers between devices  28.4 us (41%)
  starting transfers between devices  27.2 us (39%)
  Pallas kernels  12 us (17%)
  local copies, waits for them, and re-layouts  1.36 us (2%)
    all_to_all x1, waiting for transfers between devices, local(): lax.all_to_all(conv, 'seq', split_axis=0, concat_axis=0, tiled=True)  14.6 us
    ppermute x3, waiting for transfers between devices, turned_for(): return lax.ppermute(part, 'seq', along_y[d]) if d else part  11 us
    pallas_call x1, Pallas kernels, local(): pl.pallas_call(middle_kernel, out_shape=jax.ShapeDtypeStruct((BLOCKS, OUT...  7.06 us
    all_to_all x1, starting transfers between devices, swap(): return lax.all_to_all(x, 'seq', split_axis=0, concat_axis=0, tiled=True)  6.6 us
    ppermute x3, starting transfers between devices, filter_for(): return lax.ppermute(part, 'seq', along_z[d]) if d else part  6.26 us
    all_to_all x1, starting transfers between devices, local(): lax.all_to_all(conv, 'seq', split_axis=0, concat_axis=0, tiled=True)  5.4 us
    ppermute x3, starting transfers between devices, turned_for(): return lax.ppermute(part, 'seq', along_y[d]) if d else part  4.43 us
    ppermute x1, starting transfers between devices, local(): halo = lax.ppermute(last_rows, 'seq', pairs)  3.54 us
  transfers between devices with their start and end apart: 10, of which 6 were waited for; matrix products, arithmetic and copies ran while one was open for 0% of the time, Pallas kernels for 4%

profile of v3, /device:TPU:1, one launch (start us, length us, event | category | flops | bytes accessed | tf_op | source)
XLA Modules:
  0.0 69.4 jit_solution(9382472049258055836)
XLA Ops:
  0.0 0.0 copy-start.3
  0.0 0.0 copy-start.1
  0.0 0.0 copy-start.2
  0.0 1.2 %constant_dynamic-slice_fusion = (bf16[512,128]{1,0:T(8,128)(2,1)S(1)}, bf16[512,128]{1,0:T(8,128)(2,1)S(1)}, bf16[512,128]{1,0:T(8,128)(2,1)S(1)}, bf16[512,128]{1,0:T(8,128)(2,1)S(1)}) fusion(bf16[512,512]{1,0:T(8,128)(2,1)} %param.11, s32[]{:T(128)S(6)} %select_n.94, s32[]{:T(128)S(6)} %select_n.90, s32[]{:T(128)S(6)} %select_n.88, s32[]{:T(128)S(6)} %select_n.92), kind=kLoop, calls=%fused_computation.10 | loop fusion | bytes 1048592 | tf_op jit(solution)/shard_map/dynamic_slice | solution.py:299
  1.3 2.5 %collective-permute-start.1 = (bf16[512,128]{1,0:T(8,128)(2,1)S(1)}, bf16[512,128]{1,0:T(8,128)(2,1)S(1)}, u32[]{:S(2)}, u32[]{:S(2)}) collective-permute-start(bf16[512,128]{1,0:T(8,128)(2,1)S(1)} %get-tuple-element.10), channel_id=1, source_target_pairs={{0,8},{1,9},{2,10},{3,11},{4,12},{5,13},{6,14},{7,15},{8,16},{9,17... | collective-permute-start | bytes 393224 | tf_op jit(solution)/shard_map/ppermute | solution.py:300
  3.8 3.0 %collective-permute-start.2 = (bf16[512,128]{1,0:T(8,128)(2,1)S(1)}, bf16[512,128]{1,0:T(8,128)(2,1)S(1)}, u32[]{:S(2)}, u32[]{:S(2)}) collective-permute-start(bf16[512,128]{1,0:T(8,128)(2,1)S(1)} %get-tuple-element.12), channel_id=1, source_target_pairs={{0,16},{1,17},{2,18},{3,19},{4,20},{5,21},{6,22},{7,23},{8,24},{9,... | collective-permute-start | bytes 393224 | tf_op jit(solution)/shard_map/ppermute | solution.py:300
  6.8 0.7 %collective-permute-start.3 = (bf16[512,128]{1,0:T(8,128)(2,1)S(1)}, bf16[512,128]{1,0:T(8,128)(2,1)S(1)}, u32[]{:S(2)}, u32[]{:S(2)}) collective-permute-start(bf16[512,128]{1,0:T(8,128)(2,1)S(1)} %get-tuple-element.9), channel_id=1, source_target_pairs={{0,24},{1,25},{2,26},{3,27},{4,28},{5,29},{6,30},{7,31},{8,0},{9,1... | collective-permute-start | bytes 393224 | tf_op jit(solution)/shard_map/ppermute | solution.py:300
  7.5 0.0 copy-done.3
  7.5 0.0 copy-done.1
  7.5 0.0 copy-done.2
  7.5 2.3 %product.1 = bf16[32,80,128]{2,1,0:T(8,128)(2,1)} custom-call(bf16[512,512]{1,0:T(8,128)(2,1)S(1)} %copy-done.1, bf16[512,512]{1,0:T(8,128)(2,1)S(1)} %copy-done.2, f32[3,3,512]{2,1,0:T(4,128)S(1)} %copy-done.3), custom_call_target="tpu_custom_call" | custom-call | flops 20000000000 | bytes 4194304 | tf_op jit(solution)/shard_map/product/pallas_call | solution.py:320
  9.8 6.6 %all-to-all-start = ((bf16[32,80,128]{2,1,0:T(8,128)(2,1)}), bf16[32,80,128]{2,1,0:T(8,128)(2,1)S(1)}, u32[]{:S(2)}, u32[]{:S(2)}) async-start(bf16[32,80,128]{2,1,0:T(8,128)(2,1)} %product.1), calls=%async_computation | async-start | bytes 1310720 | tf_op jit(solution)/shard_map/all_to_all | solution.py:290
  16.6 0.0 collective-permute-done.1.refs_1_
  16.6 0.0 collective-permute-done.2.refs_2_
  16.6 0.0 collective-permute-done.3.refs_3_
  16.6 0.2 turn.1
  16.9 2.7 %collective-permute-start.6 = (bf16[4,2,64,128]{3,2,1,0:T(8,128)(2,1)S(1)}, bf16[4,2,64,128]{3,2,1,0:T(8,128)(2,1)S(1)}, u32[]{:S(2)}, u32[]{:S(2)}) collective-permute-start(bf16[4,2,64,128]{3,2,1,0:T(8,128)(2,1)S(1)} %get-tuple-element.5), channel_id=1, source_target_pairs={{0,6},{1,7},{2,0},{3,1},{4,2},{5,3},{6,4},{7,5},{8,14},{9,15},{10,... | collective-permute-start | bytes 393224 | tf_op jit(solution)/shard_map/ppermute | solution.py:312
  19.5 0.0 collective-permute-start.4
  19.5 1.8 %collective-permute-start.5 = (bf16[4,2,64,128]{3,2,1,0:T(8,128)(2,1)S(1)}, bf16[4,2,64,128]{3,2,1,0:T(8,128)(2,1)S(1)}, u32[]{:S(2)}, u32[]{:S(2)}) collective-permute-start(bf16[4,2,64,128]{3,2,1,0:T(8,128)(2,1)S(1)} %get-tuple-element.6), channel_id=1, source_target_pairs={{0,4},{1,5},{2,6},{3,7},{4,0},{5,1},{6,2},{7,3},{8,12},{9,13},{10,... | collective-permute-start | bytes 393224 | tf_op jit(solution)/shard_map/ppermute | solution.py:312
  21.3 5.3 %collective-permute-done.6.b3_ref = bf16[4,2,64,128]{3,2,1,0:T(8,128)(2,1)S(1)} collective-permute-done((bf16[4,2,64,128]{3,2,1,0:T(8,128)(2,1)S(1)}, bf16[4,2,64,128]{3,2,1,0:T(8,128)(2,1)S(1)}, u32[]{:S(2)}, u32[]{:S(2)}) %collective-permute-start.6) | collective-permute-done | bytes 131104 | tf_op jit(solution)/shard_map/ppermute | solution.py:312
  26.6 0.0 copy-start.5
  26.6 5.7 %collective-permute-done.5.b2_ref = bf16[4,2,64,128]{3,2,1,0:T(8,128)(2,1)S(1)} collective-permute-done((bf16[4,2,64,128]{3,2,1,0:T(8,128)(2,1)S(1)}, bf16[4,2,64,128]{3,2,1,0:T(8,128)(2,1)S(1)}, u32[]{:S(2)}, u32[]{:S(2)}) %collective-permute-start.5) | collective-permute-done | bytes 131104 | tf_op jit(solution)/shard_map/ppermute | solution.py:312
  32.3 0.0 collective-permute-done.4.b1_ref
  32.3 0.0 copy-start.6
  32.4 1.0 %collective-permute-start.7 = (bf16[4,4,64,128]{3,2,1,0:T(8,128)(2,1)S(1)}, bf16[4,4,64,128]{3,2,1,0:T(8,128)(2,1)S(1)}, u32[]{:S(2)}, u32[]{:S(2)}) collective-permute-start(bf16[4,4,64,128]{3,2,1,0:T(8,128)(2,1)S(1)} %pad_maximum_fusion), channel_id=1, source_target_pairs={{0,1},{1,0},{2,3},{3,2},{4,5},{5,4},{6,7},{7,6},{8,9},{9,8},{10,11... | collective-permute-start | bytes 786440 | tf_op jit(solution)/shard_map/ppermute | solution.py:316
  33.4 1.2 %collective-permute-done.7.other_ref = bf16[4,4,64,128]{3,2,1,0:T(8,128)(2,1)S(1)} collective-permute-done((bf16[4,4,64,128]{3,2,1,0:T(8,128)(2,1)S(1)}, bf16[4,4,64,128]{3,2,1,0:T(8,128)(2,1)S(1)}, u32[]{:S(2)}, u32[]{:S(2)}) %collective-permute-start.7) | collective-permute-done | bytes 262176 | tf_op jit(solution)/shard_map/ppermute | solution.py:316
  34.5 0.9 %all-to-all-done.in_ref = bf16[32,80,128]{2,1,0:T(8,128)(2,1)S(1)} async-done(((bf16[32,80,128]{2,1,0:T(8,128)(2,1)}), bf16[32,80,128]{2,1,0:T(8,128)(2,1)S(1)}, u32[]{:S(2)}, u32[]{:S(2)}) %all-to-all-start) | async-done | bytes 655392 | tf_op jit(solution)/shard_map/all_to_all | solution.py:290
  35.4 0.0 copy-done.5
  35.4 0.0 copy-done.6
  35.4 7.1 %middle.1 = bf16[32,80,128]{2,1,0:T(8,128)(2,1)} custom-call(s32[1]{0:T(128)} %bitcast.4.place_ref, bf16[32,80,128]{2,1,0:T(8,128)(2,1)S(1)} %all-to-all-done.in_ref, bf16[4,2,64,128]{3,2,1,0:T(8,128)(2,1)S(1)} %get-tuple-element.8.b0_ref, bf16[4,2,64,128]{3,2,1,0:T(8,128)(2,1)S(1)} %collective-permute-done.4.b1_ref, ...), custom_call_target="tpu_custom_call" | custom-call | flops 8000000000 | bytes 2000000 | tf_op jit(solution)/shard_map/middle/pallas_call | solution.py:340
  42.5 0.0 copy-start
  42.5 5.4 %all-to-all-start.1 = ((bf16[32,80,128]{2,1,0:T(8,128)(2,1)}), bf16[32,80,128]{2,1,0:T(8,128)(2,1)S(1)}, u32[]{:S(2)}, u32[]{:S(2)}) async-start(bf16[32,80,128]{2,1,0:T(8,128)(2,1)} %middle.1), calls=%async_computation.1 | async-start | bytes 1310720 | tf_op jit(solution)/shard_map/all_to_all | solution.py:349
  47.9 0.0 copy-done
  47.9 0.0 copy-start.4
  47.9 3.5 %collective-permute-start = (bf16[3,2,512]{2,1,0:T(2,128)(2,1)S(1)}, bf16[3,2,512]{2,1,0:T(2,128)(2,1)S(1)}, u32[]{:S(2)}, u32[]{:S(2)}) collective-permute-start(bf16[3,2,512]{2,1,0:T(2,128)(2,1)S(1)} %pad_maximum_fusion.1), channel_id=1, source_target_pairs={{0,1},{1,2},{2,3},{3,4},{4,5},{5,6},{6,7},{7,8},{8,9},{9,10},{10,1... | collective-permute-start | bytes 18440 | tf_op jit(solution)/shard_map/ppermute | solution.py:287
  51.5 0.8 %collective-permute-done.halo_ref = bf16[3,2,512]{2,1,0:T(2,128)(2,1)S(1)} collective-permute-done((bf16[3,2,512]{2,1,0:T(2,128)(2,1)S(1)}, bf16[3,2,512]{2,1,0:T(2,128)(2,1)S(1)}, u32[]{:S(2)}, u32[]{:S(2)}) %collective-permute-start) | collective-permute-done | bytes 6176 | tf_op jit(solution)/shard_map/ppermute | solution.py:287
  52.2 14.6 %all-to-all-done.1.conv_ref = bf16[32,80,128]{2,1,0:T(8,128)(2,1)S(1)} async-done(((bf16[32,80,128]{2,1,0:T(8,128)(2,1)}), bf16[32,80,128]{2,1,0:T(8,128)(2,1)S(1)}, u32[]{:S(2)}, u32[]{:S(2)}) %all-to-all-start.1) | async-done | bytes 655392 | tf_op jit(solution)/shard_map/all_to_all | solution.py:349
  66.8 0.0 copy-done.4
  66.8 2.5 %end.1 = bf16[512,512]{1,0:T(8,128)(2,1)} custom-call(bf16[512,512]{1,0:T(8,128)(2,1)S(1)} %copy-done, bf16[512,512]{1,0:T(8,128)(2,1)S(1)} %copy-done.1, bf16[512,512]{1,0:T(8,128)(2,1)S(1)} %copy-done.2, bf16[3,2,512]{2,1,0:T(2,128)(2,1)S(1)} %collective-permute-done.halo_ref, f32[3,3,512]{2,1,0:T(4,128)S(1)} %copy-done.3, f32[1,512]{1,0:T(1,128)S(1)} %bitcast.24, ...), custom_call_target="tpu_custom_call" | custom-call | tf_op jit(solution)/shard_map/end/pallas_call | solution.py:352
  (9 shorter events, 0.1 us)
Async XLA Ops:
  0.0 7.5 %copy-start.3 = (f32[3,3,512]{2,1,0:T(4,128)S(1)}, f32[3,3,512]{2,1,0:T(4,128)}, u32[]{:S(2)}) copy-start(f32[3,3,512]{2,1,0:T(4,128)} %taps_ref.3) | copy-start | bytes 55300
  0.0 7.5 %copy-start.1 = (bf16[512,512]{1,0:T(8,128)(2,1)S(1)}, bf16[512,512]{1,0:T(8,128)(2,1)}, u32[]{:S(2)}) copy-start(bf16[512,512]{1,0:T(8,128)(2,1)} %key_ref.3) | copy-start | bytes 1572868
  0.0 7.5 %copy-start.2 = (bf16[512,512]{1,0:T(8,128)(2,1)S(1)}, bf16[512,512]{1,0:T(8,128)(2,1)}, u32[]{:S(2)}) copy-start(bf16[512,512]{1,0:T(8,128)(2,1)} %value_ref.3) | copy-start | bytes 1572868
  1.3 15.3 %collective-permute-start.1 = (bf16[512,128]{1,0:T(8,128)(2,1)S(1)}, bf16[512,128]{1,0:T(8,128)(2,1)S(1)}, u32[]{:S(2)}, u32[]{:S(2)}) collective-permute-start(bf16[512,128]{1,0:T(8,128)(2,1)S(1)} %get-tuple-element.10), channel_id=1, source_target_pairs={{0,8},{1,9},{2,10},{3,11},{4,12},{5,13},{6,14},{7,15},{8,16},{9,17... | collective-permute-start | bytes 393224 | tf_op jit(solution)/shard_map/ppermute | solution.py:300
  3.8 12.8 %collective-permute-start.2 = (bf16[512,128]{1,0:T(8,128)(2,1)S(1)}, bf16[512,128]{1,0:T(8,128)(2,1)S(1)}, u32[]{:S(2)}, u32[]{:S(2)}) collective-permute-start(bf16[512,128]{1,0:T(8,128)(2,1)S(1)} %get-tuple-element.12), channel_id=1, source_target_pairs={{0,16},{1,17},{2,18},{3,19},{4,20},{5,21},{6,22},{7,23},{8,24},{9,... | collective-permute-start | bytes 393224 | tf_op jit(solution)/shard_map/ppermute | solution.py:300
  6.8 9.8 %collective-permute-start.3 = (bf16[512,128]{1,0:T(8,128)(2,1)S(1)}, bf16[512,128]{1,0:T(8,128)(2,1)S(1)}, u32[]{:S(2)}, u32[]{:S(2)}) collective-permute-start(bf16[512,128]{1,0:T(8,128)(2,1)S(1)} %get-tuple-element.9), channel_id=1, source_target_pairs={{0,24},{1,25},{2,26},{3,27},{4,28},{5,29},{6,30},{7,31},{8,0},{9,1... | collective-permute-start | bytes 393224 | tf_op jit(solution)/shard_map/ppermute | solution.py:300
  9.8 25.6 %all-to-all-start = ((bf16[32,80,128]{2,1,0:T(8,128)(2,1)}), bf16[32,80,128]{2,1,0:T(8,128)(2,1)S(1)}, u32[]{:S(2)}, u32[]{:S(2)}) async-start(bf16[32,80,128]{2,1,0:T(8,128)(2,1)} %product.1), calls=%async_computation | async-start | bytes 1310720 | tf_op jit(solution)/shard_map/all_to_all | solution.py:290
  16.9 9.8 %collective-permute-start.6 = (bf16[4,2,64,128]{3,2,1,0:T(8,128)(2,1)S(1)}, bf16[4,2,64,128]{3,2,1,0:T(8,128)(2,1)S(1)}, u32[]{:S(2)}, u32[]{:S(2)}) collective-permute-start(bf16[4,2,64,128]{3,2,1,0:T(8,128)(2,1)S(1)} %get-tuple-element.5), channel_id=1, source_target_pairs={{0,6},{1,7},{2,0},{3,1},{4,2},{5,3},{6,4},{7,5},{8,14},{9,15},{10,... | collective-permute-start | bytes 393224 | tf_op jit(solution)/shard_map/ppermute | solution.py:312
  19.5 12.8 %collective-permute-start.4 = (bf16[4,2,64,128]{3,2,1,0:T(8,128)(2,1)S(1)}, bf16[4,2,64,128]{3,2,1,0:T(8,128)(2,1)S(1)}, u32[]{:S(2)}, u32[]{:S(2)}) collective-permute-start(bf16[4,2,64,128]{3,2,1,0:T(8,128)(2,1)S(1)} %get-tuple-element.7), channel_id=1, source_target_pairs={{0,2},{1,3},{2,4},{3,5},{4,6},{5,7},{6,0},{7,1},{8,10},{9,11},{10,... | collective-permute-start | bytes 393224 | tf_op jit(solution)/shard_map/ppermute | solution.py:312
  19.5 12.8 %collective-permute-start.5 = (bf16[4,2,64,128]{3,2,1,0:T(8,128)(2,1)S(1)}, bf16[4,2,64,128]{3,2,1,0:T(8,128)(2,1)S(1)}, u32[]{:S(2)}, u32[]{:S(2)}) collective-permute-start(bf16[4,2,64,128]{3,2,1,0:T(8,128)(2,1)S(1)} %get-tuple-element.6), channel_id=1, source_target_pairs={{0,4},{1,5},{2,6},{3,7},{4,0},{5,1},{6,2},{7,3},{8,12},{9,13},{10,... | collective-permute-start | bytes 393224 | tf_op jit(solution)/shard_map/ppermute | solution.py:312
  26.6 8.8 %copy-start.5 = (bf16[768,256]{1,0:T(8,128)(2,1)S(1)}, bf16[768,256]{1,0:T(8,128)(2,1)}, u32[]{:S(2)}) copy-start(bf16[768,256]{1,0:T(8,128)(2,1)} %constant.136.clone.mats_ref) | copy-start | bytes 1179652
  32.3 3.1 %copy-start.6 = (f32[2,128,128]{2,1,0:T(8,128)S(1)}, f32[2,128,128]{2,1,0:T(8,128)}, u32[]{:S(2)}) copy-start(f32[2,128,128]{2,1,0:T(8,128)} %constant.137.clone.twiddle_ref) | copy-start | bytes 393220
  32.4 2.1 %collective-permute-start.7 = (bf16[4,4,64,128]{3,2,1,0:T(8,128)(2,1)S(1)}, bf16[4,4,64,128]{3,2,1,0:T(8,128)(2,1)S(1)}, u32[]{:S(2)}, u32[]{:S(2)}) collective-permute-start(bf16[4,4,64,128]{3,2,1,0:T(8,128)(2,1)S(1)} %pad_maximum_fusion), channel_id=1, source_target_pairs={{0,1},{1,0},{2,3},{3,2},{4,5},{5,4},{6,7},{7,6},{8,9},{9,8},{10,11... | collective-permute-start | bytes 786440 | tf_op jit(solution)/shard_map/ppermute | solution.py:316
  42.5 5.4 %copy-start = (bf16[512,512]{1,0:T(8,128)(2,1)S(1)}, bf16[512,512]{1,0:T(8,128)(2,1)}, u32[]{:S(2)}) copy-start(bf16[512,512]{1,0:T(8,128)(2,1)} %query_ref.1) | copy-start | bytes 1572868
  42.5 24.4 %all-to-all-start.1 = ((bf16[32,80,128]{2,1,0:T(8,128)(2,1)}), bf16[32,80,128]{2,1,0:T(8,128)(2,1)S(1)}, u32[]{:S(2)}, u32[]{:S(2)}) async-start(bf16[32,80,128]{2,1,0:T(8,128)(2,1)} %middle.1), calls=%async_computation.1 | async-start | bytes 1310720 | tf_op jit(solution)/shard_map/all_to_all | solution.py:349
  47.9 18.9 %copy-start.4 = (f32[512]{0:T(512)S(1)}, f32[512]{0:T(512)}, u32[]{:S(2)}) copy-start(f32[512]{0:T(512)} %param.13) | copy-start | bytes 6148
  47.9 4.3 %collective-permute-start = (bf16[3,2,512]{2,1,0:T(2,128)(2,1)S(1)}, bf16[3,2,512]{2,1,0:T(2,128)(2,1)S(1)}, u32[]{:S(2)}, u32[]{:S(2)}) collective-permute-start(bf16[3,2,512]{2,1,0:T(2,128)(2,1)S(1)} %pad_maximum_fusion.1), channel_id=1, source_target_pairs={{0,1},{1,2},{2,3},{3,4},{4,5},{5,6},{6,7},{7,8},{8,9},{9,10},{10,1... | collective-permute-start | bytes 18440 | tf_op jit(solution)/shard_map/ppermute | solution.py:287

commit v4 on v3

--- a/solution.py
+++ b/solution.py
@@ -22,9 +22,9 @@
 CHANS = 512
 QUARTERS = TOKENS // SIDE
 BATCH = 8
-UNROLL = 2
 STEP_A, STEP_B, STEP_C, STEP_D = 8, 8, 4, 8
 GROUP = 128
+HALF_ROWS = QUARTERS * PACK // 2
 OUT_TILES = QUARTERS + 1
 
 SPAN = 252.0
@@ -82,7 +82,7 @@
             out_ref[:, i, :, q * PACK : (q + 1) * PACK, :] = block.reshape(NEAR, 2, PACK, SIDE)
 
 
-def product_kernel(key_ref, value_ref, taps_ref, out_hbm, key_pad, value_pad, work_ref, edge_ref, out_ref, out_sems):
+def product_kernel(key_ref, value_ref, taps_ref, out_ref, key_pad, value_pad, work_ref, edge_ref):
     key_pad[0:8, :] = jnp.zeros((8, CHANS), F32)
     value_pad[0:8, :] = jnp.zeros((8, CHANS), F32)
 
@@ -104,14 +104,9 @@
     scale = scale_up(largest)
     inverse = 1.0 / scale
 
-    out_copies = []
-
     def put(tile, block):
         rows = pl.ds(tile * PACK, PACK)
         out_ref[:, rows, :] = block.T.astype(BF16).reshape(BLOCKS, PACK, SIDE)
-        copy = pltpu.make_async_copy(out_ref.at[:, rows], out_hbm.at[:, rows], out_sems.at[tile])
-        copy.start()
-        out_copies.append(copy)
 
     for q in range(QUARTERS):
         put(q, encode(work_ref[pl.ds(q * SIDE, SIDE), :], inverse))
@@ -134,8 +129,12 @@
             edge_ref[row : row + 1, :] = hi.astype(F32)
             edge_ref[row + 1 : row + 2, :] = lo.astype(F32)
     put(QUARTERS, edge_ref[...])
-    for copy in out_copies:
-        copy.wait()
+
+
+def pick_kernel(*refs):
+    *blocks, out_ref = refs
+    for i, ref in enumerate(blocks):
+        out_ref[:, i] = ref[...].reshape(NEAR, 2, HALF_ROWS, SIDE)
 
 
 def rotated(block, cos, sin):
@@ -166,26 +165,33 @@
 def middle_kernel(
     place_ref, in_ref, b0_ref, b1_ref, b2_ref, b3_ref, other_ref,
     mats_ref, twiddle_ref,
-    out_ref, prod_ref, filt_ref, conv_ref,
+    out_ref, hops_ref, prod_ref, filt_ref, conv_ref,
 ):
     gather_filter(place_ref, (b0_ref, b1_ref, b2_ref, b3_ref), other_ref, filt_ref)
     rows = BLOCKS * QUARTERS * PACK
     edge = in_ref[:, QUARTERS * PACK :, :].astype(F32)
-    scale = edge[:, :, 0:1]
-    for q in range(QUARTERS):
-        prod_ref[:, q] = decode(in_ref[:, q * PACK : (q + 1) * PACK, :].astype(F32), scale)
-
-    def part(place, i):
-        lane = 8 + place * 8 + 2 * i
-        return edge[:, :, lane : lane + 1] + edge[:, :, lane + 1 : lane + 2]
 
     def behind(x):
         return jnp.concatenate([jnp.zeros_like(x[:1]), x[:-1]], 0)
 
-    first = (part(0, 0) + behind(part(0, 2))) * (part(1, 0) + behind(part(1, 2)))
-    second = (part(0, 1) + behind(part(0, 3))) * (part(1, 1) + behind(part(1, 3)))
-    lane = lax.broadcasted_iota(jnp.int32, (BLOCKS, PACK, SIDE), 2)
-    prod_ref[:, 0] = jnp.where(lane == 0, first, jnp.where(lane == 1, second, prod_ref[:, 0]))
+    lane = lax.broadcasted_iota(jnp.int32, (BLOCKS, BATCH, SIDE), 2)
+
+    def decode_batch(batch):
+        some = slice(batch * BATCH, (batch + 1) * BATCH)
+        side = edge[:, some]
+        scale = side[:, :, 0:1]
+
+        def part(place, i):
+            at = 8 + place * 8 + 2 * i
+            return side[:, :, at : at + 1] + side[:, :, at + 1 : at + 2]
+
+        first = (part(0, 0) + behind(part(0, 2))) * (part(1, 0) + behind(part(1, 2)))
+        second = (part(0, 1) + behind(part(0, 3))) * (part(1, 1) + behind(part(1, 3)))
+        for q in range(QUARTERS):
+            x = decode(in_ref[:, q * PACK : (q + 1) * PACK, :].astype(F32)[:, some], scale)
+            if q == 0:
+                x = jnp.where(lane == 0, first, jnp.where(lane == 1, second, x))
+            prod_ref[:, q, some] = x
 
     prod_rows = prod_ref.reshape(rows, SIDE)
     filt_rows = filt_ref.reshape(rows, SIDE)
@@ -216,15 +222,19 @@
     def by_columns(left, right, step):
         return jnp.concatenate([dot(left, right[:, i : i + step * SIDE]) for i in range(0, BATCH * SIDE, step * SIDE)], 1)
 
-    def one_batch(batch, carry):
-        cos, sin = twiddle_ref[0], twiddle_ref[1]
+    cos, sin = twiddle_ref[0], twiddle_ref[1]
+
+    def filter_spectra(batch):
+        taps = channels(filt_rows, batch).astype(BF16)
+        filt = by_columns(first_exact, jnp.concatenate([taps, taps], 0), STEP_A)
+        return by_rows(rotated(filt, cos, sin), fwd, STEP_B)
+
+    def data_spectra(batch):
         hi, lo = split(channels(prod_rows, batch))
         data = by_columns(first, jnp.concatenate([hi, lo], 0), STEP_A)
-        data = data[:two] + data[two:]
-        taps = channels(filt_rows, batch).astype(BF16)
-        filt = by_columns(first_exact, jnp.concatenate([taps, taps], 0), STEP_A)
-        x = by_rows(rotated(data, cos, sin), fwd, STEP_B)
-        h = by_rows(rotated(filt, cos, sin), fwd, STEP_B)
+        return by_rows(rotated(data[:two] + data[two:], cos, sin), fwd, STEP_B)
+
+    def back(batch, x, h):
         x_re, x_im, h_re, h_im = x[:, :SIDE], x[:, SIDE:], h[:, :SIDE], h[:, SIDE:]
         hi, lo = split(jnp.concatenate([x_re * h_re - x_im * h_im, x_re * h_im + x_im * h_re], 1))
         back = by_rows(jnp.concatenate([hi, lo, hi], 1), inv, STEP_C)
@@ -237,44 +247,92 @@
         y = y[:SIDE] + y[SIDE:] + by_columns(last_hi, lo, STEP_D)
         for i in range(BATCH):
             conv_rows[pl.ds(BATCH * batch + i, SIDE, stride=PACK), :] = y[:, i * SIDE : (i + 1) * SIDE]
-        return carry
-
-    lax.fori_loop(0, PACK // BATCH, one_batch, 0, unroll=UNROLL)
-
-    conv = [conv_ref[:, q] for q in range(QUARTERS)]
-    largest = functools.reduce(jnp.maximum, [jnp.abs(c) for c in conv])
-    scale = scale_up(jnp.max(largest, axis=2, keepdims=True))
-    inverse = 1.0 / scale
-    for q in range(QUARTERS):
-        out_ref[:, q * PACK : (q + 1) * PACK, :] = encode(conv[q], inverse).astype(BF16)
-    out_ref[:, QUARTERS * PACK :, :] = jnp.broadcast_to(scale, (BLOCKS, PACK, SIDE)).astype(BF16)
-
-
-def end_kernel(query_ref, key_ref, value_ref, halo_ref, taps_ref, gain_ref, conv_ref, out_hbm, query_pad, key_pad, value_pad, out_ref, sems):
+
+    scales = []
+
+    def encode_batch(batch):
+        some = slice(batch * BATCH, (batch + 1) * BATCH)
+        conv = [conv_ref[:, q, some] for q in range(QUARTERS)]
+        largest = functools.reduce(jnp.maximum, [jnp.abs(c) for c in conv])
+        scale = scale_up(jnp.max(largest, axis=2, keepdims=True))
+        inverse = 1.0 / scale
+        for q in range(QUARTERS):
+            conv_ref[:, q, some] = encode(conv[q], inverse)
+        scales.append(scale)
+
+    h0 = filter_spectra(0)
+    h1 = filter_spectra(1)
+    decode_batch(0)
+    x0 = data_spectra(0)
+    decode_batch(1)
+    x1 = data_spectra(1)
+    back(0, x0, h0)
+    back(1, x1, h1)
+    encode_batch(0)
+    encode_batch(1)
+    for batch, ref in enumerate((out_ref, hops_ref)):
+        some = slice(batch * BATCH, (batch + 1) * BATCH)
+        for p in range(QUARTERS // 2):
+            both = jnp.concatenate([conv_ref[:, 2 * p, some], conv_ref[:, 2 * p + 1, some]], 1)
+            ref[:, p * PACK : (p + 1) * PACK, :] = both.astype(BF16)
+    scale = jnp.concatenate(scales, 1)
+    out_ref[:, HALF_ROWS:, :] = jnp.broadcast_to(scale, (BLOCKS, PACK, SIDE)).astype(BF16)
+
+
+def gate_kernel(query_hbm, key_hbm, value_hbm, halo_ref, taps_ref, gain_ref, picked_hbm, mix_ref, direct_ref, rows_ref, query_pad, key_pad, value_pad, sems):
     pads = (query_pad, key_pad, value_pad)
+    copies = []
+    for place, hbm in enumerate((query_hbm, key_hbm, value_hbm)):
+        copy = pltpu.make_async_copy(hbm, rows_ref.at[place], sems.at[place])
+        copy.start()
+        copies.append(copy)
     for place, pad in enumerate(pads):
         pad[6:8, :] = halo_ref[place].astype(F32)
-
-    def mix(place, ref, start):
+        copies[place].wait()
+
+    def mix(place, start):
         pad, taps = pads[place], taps_ref[place]
-        pad[pl.ds(8 + start, SIDE), :] = ref[pl.ds(start, SIDE), :].astype(F32)
+        pad[pl.ds(8 + start, SIDE), :] = rows_ref[place, pl.ds(start, SIDE), :].astype(F32)
         return (
             taps[0:1] * pad[pl.ds(8 + start, SIDE), :]
             + taps[1:2] * pad[pl.ds(7 + start, SIDE), :]
             + taps[2:3] * pad[pl.ds(6 + start, SIDE), :]
         )
 
-    scale = conv_ref[:, QUARTERS * PACK :, 0:1].astype(F32)
-    copies = []
     for q in range(QUARTERS):
         start = q * SIDE
-        rows = pl.ds(start, SIDE)
-        conv = decode(conv_ref[:, q * PACK : (q + 1) * PACK, :].astype(F32), scale)
-        direct = gain_ref[...] * (mix(1, key_ref, start) * mix(2, value_ref, start))
-        out_ref[rows, :] = (mix(0, query_ref, start) * (conv.reshape(CHANS, SIDE).T + direct)).astype(BF16)
-        copy = pltpu.make_async_copy(out_ref.at[rows], out_hbm.at[rows], sems.at[q])
-        copy.start()
-        copies.append(copy)
+        query = mix(0, start)
+        mix_ref[pl.ds(start, SIDE), :] = query
+        direct_ref[pl.ds(start, SIDE), :] = query * (gain_ref[...] * (mix(1, start) * mix(2, start)))
+
+
+def other_kernel(place_ref, b0_ref, b1_ref, b2_ref, b3_ref, ready_hbm, out_ref):
+    core = place_ref[0] % 2
+    for dy, ref in enumerate((b0_ref, b1_ref, b2_ref, b3_ref)):
+        out_ref[dy] = ref[:, 1 - core]
+
+
+def end_kernel(place_ref, mix_ref, direct_ref, conv_ref, b0_ref, b1_ref, b2_ref, b3_ref, other_ref, out_hbm, hops_ref, out_ref, sems):
+    me = place_ref[0]
+    z, y, core = me // 8, (me // 2) % 4, me % 2
+    for dy, ref in enumerate((b0_ref, b1_ref, b2_ref, b3_ref)):
+        for dz in range(NEAR):
+            chip = ((z + NEAR - dz) % NEAR) * 8 + ((y + NEAR - dy) % NEAR) * 2
+            hops_ref[chip + core] = ref[dz, core]
+            hops_ref[chip + 1 - core] = other_ref[dy, dz]
+    scale = conv_ref[:, HALF_ROWS:, 0:1].astype(F32)
+    copies = []
+    for p in range(QUARTERS // 2):
+        tile = slice(p * PACK, (p + 1) * PACK)
+        near, far = conv_ref[:, tile, :].astype(F32), hops_ref[:, tile, :].astype(F32)
+        for i in range(2):
+            some = slice(i * BATCH, (i + 1) * BATCH)
+            conv = decode(jnp.concatenate([near[:, some], far[:, some]], 1), scale).reshape(CHANS, SIDE).T
+            rows = pl.ds((2 * p + i) * SIDE, SIDE)
+            out_ref[rows, :] = (mix_ref[rows, :] * conv + direct_ref[rows, :]).astype(BF16)
+            copy = pltpu.make_async_copy(out_ref.at[rows], out_hbm.at[rows], sems.at[2 * p + i])
+            copy.start()
+            copies.append(copy)
     for copy in copies:
         copy.wait()
 
@@ -312,23 +370,33 @@
         return lax.ppermute(part, "seq", along_y[d]) if d else part
 
     bands = [turned_for(d) for d in range(NEAR)]
-    to_other = jnp.stack([lax.dynamic_index_in_dim(b, 1 - core, 1, keepdims=False) for b in bands])
-    from_other = lax.ppermute(to_other, "seq", [(i, i ^ 1) for i in every])
-
     hbm = pl.BlockSpec(memory_space=pl.ANY)
     vmem = pl.BlockSpec(memory_space=pltpu.VMEM)
+    smem = pl.BlockSpec(memory_space=pltpu.SMEM)
+    place = me.astype(jnp.int32)[None]
+
+    def for_other(blocks, ready):
+        return pl.pallas_call(
+            other_kernel,
+            in_specs=[smem] + [vmem] * 4 + [hbm],
+            out_shape=jax.ShapeDtypeStruct((NEAR, NEAR, *blocks[0].shape[2:]), BF16),
+            compiler_params=small,
+            name="other",
+        )(place, *blocks, ready)
+
+    to_other = for_other(bands, halo)
+    from_other = lax.ppermute(to_other, "seq", [(i, i ^ 1) for i in every])
+
     product_sent = pl.pallas_call(
         product_kernel,
         in_specs=[vmem, vmem, vmem],
-        out_specs=hbm,
+        out_specs=vmem,
         out_shape=jax.ShapeDtypeStruct((BLOCKS, OUT_TILES * PACK, SIDE), BF16),
         scratch_shapes=[
             pltpu.VMEM((TOKENS + 8, CHANS), F32),
             pltpu.VMEM((TOKENS + 8, CHANS), F32),
             pltpu.VMEM((TOKENS, CHANS), F32),
             pltpu.VMEM((SIDE, CHANS), F32),
-            pltpu.VMEM((BLOCKS, OUT_TILES * PACK, SIDE), BF16),
-            pltpu.SemaphoreType.DMA((OUT_TILES,)),
         ],
         compiler_params=small,
         cost_estimate=pl.CostEstimate(flops=2 * 10**10, bytes_accessed=2**22, transcendentals=0),
@@ -337,27 +405,62 @@
     product_arrived = swap(product_sent)
 
     work = pltpu.VMEM((BLOCKS, QUARTERS, PACK, SIDE), F32)
-    conv = pl.pallas_call(
+    conv, hops = pl.pallas_call(
         middle_kernel,
-        out_shape=jax.ShapeDtypeStruct((BLOCKS, OUT_TILES * PACK, SIDE), BF16),
-        in_specs=[pl.BlockSpec(memory_space=pltpu.SMEM)] + [pl.BlockSpec(memory_space=pltpu.VMEM)] * 8,
+        in_specs=[smem] + [vmem] * 8,
+        out_shape=[
+            jax.ShapeDtypeStruct((BLOCKS, HALF_ROWS + PACK, SIDE), BF16),
+            jax.ShapeDtypeStruct((BLOCKS, HALF_ROWS, SIDE), BF16),
+        ],
         scratch_shapes=[work, work, work],
         compiler_params=small,
         cost_estimate=pl.CostEstimate(flops=8 * 10**9, bytes_accessed=2 * 10**6, transcendentals=0),
         name="middle",
-    )(me.astype(jnp.int32)[None], product_arrived, *bands, from_other, *[jnp.asarray(c) for c in consts])
-    returned = lax.all_to_all(conv, "seq", split_axis=0, concat_axis=0, tiled=True)
-
+    )(place, product_arrived, *bands, from_other, *[jnp.asarray(c) for c in consts])
+
+    def conv_for(d):
+        part = lax.dynamic_slice_in_dim(hops, (z + d) % NEAR * 8, 8, 0)
+        return lax.ppermute(part, "seq", along_z[d]) if d else part
+
+    picked = pl.pallas_call(
+        pick_kernel,
+        out_shape=jax.ShapeDtypeStruct((NEAR, NEAR, 2, HALF_ROWS, SIDE), BF16),
+        compiler_params=small,
+        cost_estimate=pl.CostEstimate(flops=2 * 10**10, bytes_accessed=2**20, transcendentals=0),
+        name="pick",
+    )(*[conv_for(d) for d in range(NEAR)])
+
+    def picked_for(d):
+        part = lax.dynamic_index_in_dim(picked, (y + d) % NEAR, 0, keepdims=False)
+        return lax.ppermute(part, "seq", along_y[d]) if d else part
+
+    returned = swap(conv)
+    conv_bands = [picked_for(d) for d in range(NEAR)]
     pad = pltpu.VMEM((TOKENS + 8, CHANS), F32)
+    query_mix, direct = pl.pallas_call(
+        gate_kernel,
+        in_specs=[hbm] * 3 + [vmem] * 3 + [hbm],
+        out_shape=[jax.ShapeDtypeStruct((TOKENS, CHANS), F32)] * 2,
+        scratch_shapes=[pltpu.VMEM((3, TOKENS, CHANS), BF16), pad, pad, pad, pltpu.SemaphoreType.DMA((3,))],
+        compiler_params=small,
+        cost_estimate=pl.CostEstimate(flops=10**9, bytes_accessed=4 * 10**6, transcendentals=0),
+        name="gate",
+    )(query_input, key_input, value_input, halo, short_taps, skip_gain[None, :], picked)
+    conv_to_other = for_other(conv_bands, direct)
+    conv_from_other = lax.ppermute(conv_to_other, "seq", [(i, i ^ 1) for i in every])
     return pl.pallas_call(
         end_kernel,
-        in_specs=[vmem] * 7,
+        in_specs=[smem] + [vmem] * 8,
         out_specs=hbm,
         out_shape=jax.ShapeDtypeStruct((TOKENS, CHANS), BF16),
-        scratch_shapes=[pad, pad, pad, pltpu.VMEM((TOKENS, CHANS), BF16), pltpu.SemaphoreType.DMA((QUARTERS,))],
+        scratch_shapes=[
+            pltpu.VMEM((BLOCKS, HALF_ROWS, SIDE), BF16),
+            pltpu.VMEM((TOKENS, CHANS), BF16),
+            pltpu.SemaphoreType.DMA((QUARTERS,)),
+        ],
         compiler_params=small,
         name="end",
-    )(query_input, key_input, value_input, halo, short_taps, skip_gain[None, :], returned)
+    )(place, query_mix, direct, returned, *conv_bands, conv_from_other)
 
 
 def solution(mesh):

time: 69.8 us -> 68.5 us (0.981)
  waiting for transfers between devices: 28.4 us -> 17 us
  starting transfers between devices: 27.2 us -> 37.3 us
    all_to_all x1 -> x0, waiting for transfers between devices: 14.6 us -> none  [local(): lax.all_to_all(conv, 'seq', split_axis=0, concat_axis=0, tiled=True)]
    ppermute x0 -> x7, starting transfers between devices: none -> 8.6 us  [the longest x3 4.6 us: conv_for(): return lax.ppermute(part, 'seq', along_z[d]) if d else part]
    all_to_all x1 -> x2, starting transfers between devices: 6.6 us -> 13.8 us  [swap(): return lax.all_to_all(x, 'seq', split_axis=0, concat_axis=0, tiled=True)]
    ppermute x3, waiting for transfers between devices: 11 us -> 3.86 us  [turned_for(): return lax.ppermute(part, 'seq', along_y[d]) if d else part]
    ppermute x0 -> x7, waiting for transfers between devices: none -> 6.92 us  [the longest x3 5.39 us: picked_for(): return lax.ppermute(part, 'seq', along_y[d]) if d else part]
    all_to_all x1 -> x0, starting transfers between devices: 5.4 us -> none  [local(): lax.all_to_all(conv, 'seq', split_axis=0, concat_axis=0, tiled=True)]
    ppermute x1, waiting for transfers between devices: 0.75 us -> 3.08 us  [local(): halo = lax.ppermute(last_rows, 'seq', pairs)]
    ppermute x1, starting transfers between devices: 3.54 us -> 4.7 us  [local(): halo = lax.ppermute(last_rows, 'seq', pairs)]
  transfers between devices with their start and end apart: 10 -> 17, of which waited for: 6 -> 9; matrix products, arithmetic and copies ran while one was open for 0% -> 0% of each run, Pallas kernels for 4% -> 7%
where the time goes in v4:
time: 68.5 us; the launch traced here: 68.2 us
  starting transfers between devices  37.3 us (54%)
  waiting for transfers between devices  17 us (25%)
  Pallas kernels  12 us (18%)
  local copies, waits for them, and re-layouts  1.39 us (2%)
    all_to_all x2, starting transfers between devices, swap(): return lax.all_to_all(x, 'seq', split_axis=0, concat_axis=0, tiled=True)  13.8 us
    pallas_call x1, Pallas kernels, local(): pl.pallas_call(middle_kernel, in_specs=[smem] + [vmem] * 8, out_shape=[ja...  6.22 us
    ppermute x3, starting transfers between devices, filter_for(): return lax.ppermute(part, 'seq', along_z[d]) if d else part  5.62 us
    ppermute x3, waiting for transfers between devices, picked_for(): return lax.ppermute(part, 'seq', along_y[d]) if d else part  5.39 us
    ppermute x1, starting transfers between devices, local(): halo = lax.ppermute(last_rows, 'seq', pairs)  4.7 us
    ppermute x3, starting transfers between devices, conv_for(): return lax.ppermute(part, 'seq', along_z[d]) if d else part  4.6 us
    ppermute x3, waiting for transfers between devices, turned_for(): return lax.ppermute(part, 'seq', along_y[d]) if d else part  3.86 us
    ppermute x3, starting transfers between devices, turned_for(): return lax.ppermute(part, 'seq', along_y[d]) if d else part  3.83 us
  transfers between devices with their start and end apart: 17, of which 9 were waited for; matrix products, arithmetic and copies ran while one was open for 0% of the time, Pallas kernels for 7%

profile of v4, /device:TPU:1, one launch (start us, length us, event | category | flops | bytes accessed | tf_op | source)
XLA Modules:
  0.0 68.2 jit_solution(1104805652754668749)
XLA Ops:
  0.0 0.0 copy-start.5
  0.0 0.0 copy-start.1
  0.0 0.0 copy-start.3
  0.0 1.2 %constant_dynamic-slice_fusion.4 = (bf16[512,128]{1,0:T(8,128)(2,1)S(1)}, bf16[512,128]{1,0:T(8,128)(2,1)S(1)}, bf16[512,128]{1,0:T(8,128)(2,1)S(1)}, bf16[512,128]{1,0:T(8,128)(2,1)S(1)}) fusion(bf16[512,512]{1,0:T(8,128)(2,1)} %param.11, s32[]{:T(128)S(6)} %select_n.112, s32[]{:T(128)S(6)} %select_n.108, s32[]{:T(128)S(6)} %select_n.106, s32[]{:T(128)S(6)} %select_n.110), kind=kLoop, calls=%fused_computation.13 | loop fusion | bytes 1048592 | tf_op jit(solution)/shard_map/dynamic_slice | solution.py:357
  1.3 5.3 %collective-permute-start.3 = (bf16[512,128]{1,0:T(8,128)(2,1)S(1)}, bf16[512,128]{1,0:T(8,128)(2,1)S(1)}, u32[]{:S(2)}, u32[]{:S(2)}) collective-permute-start(bf16[512,128]{1,0:T(8,128)(2,1)S(1)} %get-tuple-element.17), channel_id=1, source_target_pairs={{0,24},{1,25},{2,26},{3,27},{4,28},{5,29},{6,30},{7,31},{8,0},{9,1... | collective-permute-start | bytes 393224 | tf_op jit(solution)/shard_map/ppermute | solution.py:358
  6.5 0.0 collective-permute-start.1
  6.5 0.4 collective-permute-start.2
  6.9 0.0 copy-done.5
  6.9 0.0 copy-done.1
  6.9 0.0 copy-done.3
  6.9 2.4 %product.1 = bf16[32,80,128]{2,1,0:T(8,128)(2,1)} custom-call(bf16[512,512]{1,0:T(8,128)(2,1)S(1)} %copy-done.1, bf16[512,512]{1,0:T(8,128)(2,1)S(1)} %copy-done.3, f32[3,3,512]{2,1,0:T(4,128)S(1)} %copy-done.5), custom_call_target="tpu_custom_call" | custom-call | flops 20000000000 | bytes 4194304 | tf_op jit(solution)/shard_map/product/pallas_call | solution.py:390
  9.3 9.0 %all-to-all-start = ((bf16[32,80,128]{2,1,0:T(8,128)(2,1)}), bf16[32,80,128]{2,1,0:T(8,128)(2,1)S(1)}, u32[]{:S(2)}, u32[]{:S(2)}) async-start(bf16[32,80,128]{2,1,0:T(8,128)(2,1)} %product.1), calls=%async_computation | async-start | bytes 1310720 | tf_op jit(solution)/shard_map/all_to_all | solution.py:348
  18.5 0.0 collective-permute-done.3.refs_3_
  18.5 0.0 collective-permute-done.1.refs_1_
  18.5 0.0 collective-permute-done.2.refs_2_
  18.5 0.2 turn.1
  18.7 0.0 copy-start
  18.7 0.1 dynamic-slice_bitcast_fusion
  18.8 2.7 %collective-permute-start.6 = (bf16[4,2,64,128]{3,2,1,0:T(8,128)(2,1)S(1)}, bf16[4,2,64,128]{3,2,1,0:T(8,128)(2,1)S(1)}, u32[]{:S(2)}, u32[]{:S(2)}) collective-permute-start(bf16[4,2,64,128]{3,2,1,0:T(8,128)(2,1)S(1)} %get-tuple-element.13), channel_id=1, source_target_pairs={{0,6},{1,7},{2,0},{3,1},{4,2},{5,3},{6,4},{7,5},{8,14},{9,15},{10,... | collective-permute-start | bytes 393224 | tf_op jit(solution)/shard_map/ppermute | solution.py:370
  21.5 0.6 collective-permute-start.5
  22.0 0.6 collective-permute-start.4
  22.6 0.0 copy-done
  22.6 4.7 %collective-permute-start = (bf16[3,2,512]{2,1,0:T(2,128)(2,1)S(1)}, bf16[3,2,512]{2,1,0:T(2,128)(2,1)S(1)}, u32[]{:S(2)}, u32[]{:S(2)}) collective-permute-start(bf16[3,2,512]{2,1,0:T(2,128)(2,1)S(1)} %pad_maximum_fusion), channel_id=1, source_target_pairs={{0,1},{1,2},{2,3},{3,4},{4,5},{5,6},{6,7},{7,8},{8,9},{9,10},{10,1... | collective-permute-start | bytes 18440 | tf_op jit(solution)/shard_map/ppermute | solution.py:345
  27.4 3.1 %collective-permute-done.ready_hbm.halo_ref = bf16[3,2,512]{2,1,0:T(2,128)(2,1)S(1)} collective-permute-done((bf16[3,2,512]{2,1,0:T(2,128)(2,1)S(1)}, bf16[3,2,512]{2,1,0:T(2,128)(2,1)S(1)}, u32[]{:S(2)}, u32[]{:S(2)}) %collective-permute-start) | collective-permute-done | bytes 6176 | tf_op jit(solution)/shard_map/ppermute | solution.py:345
  30.4 0.0 collective-permute-done.6.b3_ref
  30.4 0.0 collective-permute-done.5.b2_ref
  30.4 3.9 %collective-permute-done.4.b1_ref = bf16[4,2,64,128]{3,2,1,0:T(8,128)(2,1)S(1)} collective-permute-done((bf16[4,2,64,128]{3,2,1,0:T(8,128)(2,1)S(1)}, bf16[4,2,64,128]{3,2,1,0:T(8,128)(2,1)S(1)}, u32[]{:S(2)}, u32[]{:S(2)}) %collective-permute-start.4) | collective-permute-done | bytes 131104 | tf_op jit(solution)/shard_map/ppermute | solution.py:370
  34.3 0.0 copy-start.7
  34.3 0.0 copy-start.8
  34.3 0.8 %collective-permute-start.7 = (bf16[4,4,64,128]{3,2,1,0:T(8,128)(2,1)S(1)}, bf16[4,4,64,128]{3,2,1,0:T(8,128)(2,1)S(1)}, u32[]{:S(2)}, u32[]{:S(2)}) collective-permute-start(bf16[4,4,64,128]{3,2,1,0:T(8,128)(2,1)S(1)} %other.2), channel_id=1, source_target_pairs={{0,1},{1,0},{2,3},{3,2},{4,5},{5,4},{6,7},{7,6},{8,9},{9,8},{10,11... | collective-permute-start | bytes 786440 | tf_op jit(solution)/shard_map/ppermute | solution.py:388
  35.1 1.2 %collective-permute-done.7.other_ref = bf16[4,4,64,128]{3,2,1,0:T(8,128)(2,1)S(1)} collective-permute-done((bf16[4,4,64,128]{3,2,1,0:T(8,128)(2,1)S(1)}, bf16[4,4,64,128]{3,2,1,0:T(8,128)(2,1)S(1)}, u32[]{:S(2)}, u32[]{:S(2)}) %collective-permute-start.7) | collective-permute-done | bytes 262176 | tf_op jit(solution)/shard_map/ppermute | solution.py:388
  36.3 1.0 %all-to-all-done.in_ref = bf16[32,80,128]{2,1,0:T(8,128)(2,1)S(1)} async-done(((bf16[32,80,128]{2,1,0:T(8,128)(2,1)}), bf16[32,80,128]{2,1,0:T(8,128)(2,1)S(1)}, u32[]{:S(2)}, u32[]{:S(2)}) %all-to-all-start) | async-done | bytes 655392 | tf_op jit(solution)/shard_map/all_to_all | solution.py:348
  37.3 0.0 copy-done.7
  37.3 0.0 copy-done.8
  37.3 6.2 %middle.1 = (bf16[32,48,128]{2,1,0:T(8,128)(2,1)}, bf16[32,32,128]{2,1,0:T(8,128)(2,1)S(1)}) custom-call(s32[1]{0:T(128)} %bitcast.place_ref, bf16[32,80,128]{2,1,0:T(8,128)(2,1)S(1)} %all-to-all-done.in_ref, bf16[4,2,64,128]{3,2,1,0:T(8,128)(2,1)S(1)} %get-tuple-element.16.b0_ref, bf16[4,2,64,128]{3,2,1,0:T(8,128)(2,1)S(1)} %collective-permute-done.4.b1_ref, ...), custom_call_target="tpu_custom_call" | custom-call | flops 8000000000 | bytes 2000000 | tf_op jit(solution)/shard_map/middle/pallas_call | solution.py:408
  43.5 2.7 %collective-permute-start.10 = (bf16[8,32,128]{2,1,0:T(8,128)(2,1)S(1)}, bf16[8,32,128]{2,1,0:T(8,128)(2,1)S(1)}, u32[]{:S(2)}, u32[]{:S(2)}) collective-permute-start(bf16[8,32,128]{2,1,0:T(8,128)(2,1)S(1)} %get-tuple-element.25), channel_id=1, source_target_pairs={{0,24},{1,25},{2,26},{3,27},{4,28},{5,29},{6,30},{7,31},{8,0},{9,1... | collective-permute-start | bytes 196616 | tf_op jit(solution)/shard_map/ppermute | solution.py:423
  46.3 0.5 collective-permute-start.9
  46.8 1.4 %collective-permute-start.8 = (bf16[8,32,128]{2,1,0:T(8,128)(2,1)S(1)}, bf16[8,32,128]{2,1,0:T(8,128)(2,1)S(1)}, u32[]{:S(2)}, u32[]{:S(2)}) collective-permute-start(bf16[8,32,128]{2,1,0:T(8,128)(2,1)S(1)} %get-tuple-element.27), channel_id=1, source_target_pairs={{0,8},{1,9},{2,10},{3,11},{4,12},{5,13},{6,14},{7,15},{8,16},{9,17... | collective-permute-start | bytes 196616 | tf_op jit(solution)/shard_map/ppermute | solution.py:423
  48.1 4.8 %all-to-all-start.1 = ((bf16[32,48,128]{2,1,0:T(8,128)(2,1)}), bf16[32,48,128]{2,1,0:T(8,128)(2,1)S(1)}, u32[]{:S(2)}, u32[]{:S(2)}) async-start(bf16[32,48,128]{2,1,0:T(8,128)(2,1)} %get-tuple-element.12), calls=%async_computation.1 | async-start | bytes 786432 | tf_op jit(solution)/shard_map/all_to_all | solution.py:348
  52.9 0.0 collective-permute-done.10.refs_3_
  52.9 0.5 collective-permute-done.9.refs_2_
  53.4 0.0 collective-permute-done.8.refs_1_
  53.5 0.0 copy-start.4
  53.5 0.0 copy-start.2
  53.5 2.2 %collective-permute-start.13 = (bf16[4,2,32,128]{3,2,1,0:T(8,128)(2,1)S(1)}, bf16[4,2,32,128]{3,2,1,0:T(8,128)(2,1)S(1)}, u32[]{:S(2)}, u32[]{:S(2)}) collective-permute-start(bf16[4,2,32,128]{3,2,1,0:T(8,128)(2,1)S(1)} %get-tuple-element.21), channel_id=1, source_target_pairs={{0,6},{1,7},{2,0},{3,1},{4,2},{5,3},{6,4},{7,5},{8,14},{9,15},{10,... | collective-permute-start | bytes 196616 | tf_op jit(solution)/shard_map/ppermute | solution.py:435
  55.7 0.0 copy-start.6
  55.7 0.5 collective-permute-start.12
  56.3 0.6 collective-permute-start.11
  56.9 0.0 copy-done.4
  56.9 0.0 copy-done.2
  56.9 0.0 copy-done.6
  56.9 1.9 %gate.1 = (f32[512,512]{1,0:T(8,128)S(1)}, f32[512,512]{1,0:T(8,128)S(1)}) custom-call(bf16[512,512]{1,0:T(8,128)(2,1)S(1)} %copy-done, bf16[512,512]{1,0:T(8,128)(2,1)S(1)} %copy-done.2, bf16[512,512]{1,0:T(8,128)(2,1)S(1)} %copy-done.4, bf16[3,2,512]{2,1,0:T(2,128)(2,1)S(1)} %collective-permute-done.ready_hbm.halo_ref, f32[3,3,512]{2,1,0:T(4,128)S(1)} %copy-done.5, ...), custom_call_target="tpu_custom_call" | custom-call | flops 1000000000 | bytes 4000000 | tf_op jit(solution)/shard_map/gate/pallas_call | solution.py:440
  58.8 0.0 collective-permute-done.13.b3_ref
  58.8 3.2 %collective-permute-done.12.b2_ref = bf16[4,2,32,128]{3,2,1,0:T(8,128)(2,1)S(1)} collective-permute-done((bf16[4,2,32,128]{3,2,1,0:T(8,128)(2,1)S(1)}, bf16[4,2,32,128]{3,2,1,0:T(8,128)(2,1)S(1)}, u32[]{:S(2)}, u32[]{:S(2)}) %collective-permute-start.12) | collective-permute-done | bytes 65568 | tf_op jit(solution)/shard_map/ppermute | solution.py:435
  62.0 2.2 %collective-permute-done.11.b1_ref = bf16[4,2,32,128]{3,2,1,0:T(8,128)(2,1)S(1)} collective-permute-done((bf16[4,2,32,128]{3,2,1,0:T(8,128)(2,1)S(1)}, bf16[4,2,32,128]{3,2,1,0:T(8,128)(2,1)S(1)}, u32[]{:S(2)}, u32[]{:S(2)}) %collective-permute-start.11) | collective-permute-done | bytes 65568 | tf_op jit(solution)/shard_map/ppermute | solution.py:435
  64.2 0.7 collective-permute-start.14
  64.8 1.0 %collective-permute-done.14.other_ref = bf16[4,4,32,128]{3,2,1,0:T(8,128)(2,1)S(1)} collective-permute-done((bf16[4,4,32,128]{3,2,1,0:T(8,128)(2,1)S(1)}, bf16[4,4,32,128]{3,2,1,0:T(8,128)(2,1)S(1)}, u32[]{:S(2)}, u32[]{:S(2)}) %collective-permute-start.14) | collective-permute-done | bytes 131104 | tf_op jit(solution)/shard_map/ppermute | solution.py:450
  65.8 1.0 %all-to-all-done.1.conv_ref = bf16[32,48,128]{2,1,0:T(8,128)(2,1)S(1)} async-done(((bf16[32,48,128]{2,1,0:T(8,128)(2,1)}), bf16[32,48,128]{2,1,0:T(8,128)(2,1)S(1)}, u32[]{:S(2)}, u32[]{:S(2)}) %all-to-all-start.1) | async-done | bytes 393248 | tf_op jit(solution)/shard_map/all_to_all | solution.py:348
  66.8 1.2 %end.1 = bf16[512,512]{1,0:T(8,128)(2,1)} custom-call(s32[1]{0:T(128)} %bitcast.place_ref, f32[512,512]{1,0:T(8,128)S(1)} %get-tuple-element.10.mix_ref, f32[512,512]{1,0:T(8,128)S(1)} %get-tuple-element.11.ready_hbm.direct_ref, bf16[32,48,128]{2,1,0:T(8,128)(2,1)S(1)} %all-to-all-done.1.conv_ref, bf16[4,2,32,128]{3,2,1,0:T(8,128)(2,1)S(1)} %get-tuple-element.24.b0_ref, ...), custom_call_target="tpu_custom_call" | custom-call | tf_op jit(solution)/shard_map/end/pallas_call | solution.py:451
  (8 shorter events, 0.1 us)
Async XLA Ops:
  0.0 6.9 %copy-start.5 = (f32[3,3,512]{2,1,0:T(4,128)S(1)}, f32[3,3,512]{2,1,0:T(4,128)}, u32[]{:S(2)}) copy-start(f32[3,3,512]{2,1,0:T(4,128)} %taps_ref.3) | copy-start | bytes 55300
  0.0 6.9 %copy-start.1 = (bf16[512,512]{1,0:T(8,128)(2,1)S(1)}, bf16[512,512]{1,0:T(8,128)(2,1)}, u32[]{:S(2)}) copy-start(bf16[512,512]{1,0:T(8,128)(2,1)} %key_hbm.1) | copy-start | bytes 1572868
  0.0 6.9 %copy-start.3 = (bf16[512,512]{1,0:T(8,128)(2,1)S(1)}, bf16[512,512]{1,0:T(8,128)(2,1)}, u32[]{:S(2)}) copy-start(bf16[512,512]{1,0:T(8,128)(2,1)} %value_hbm.1) | copy-start | bytes 1572868
  1.3 17.2 %collective-permute-start.3 = (bf16[512,128]{1,0:T(8,128)(2,1)S(1)}, bf16[512,128]{1,0:T(8,128)(2,1)S(1)}, u32[]{:S(2)}, u32[]{:S(2)}) collective-permute-start(bf16[512,128]{1,0:T(8,128)(2,1)S(1)} %get-tuple-element.17), channel_id=1, source_target_pairs={{0,24},{1,25},{2,26},{3,27},{4,28},{5,29},{6,30},{7,31},{8,0},{9,1... | collective-permute-start | bytes 393224 | tf_op jit(solution)/shard_map/ppermute | solution.py:358
  6.5 12.0 %collective-permute-start.1 = (bf16[512,128]{1,0:T(8,128)(2,1)S(1)}, bf16[512,128]{1,0:T(8,128)(2,1)S(1)}, u32[]{:S(2)}, u32[]{:S(2)}) collective-permute-start(bf16[512,128]{1,0:T(8,128)(2,1)S(1)} %get-tuple-element.18), channel_id=1, source_target_pairs={{0,8},{1,9},{2,10},{3,11},{4,12},{5,13},{6,14},{7,15},{8,16},{9,17... | collective-permute-start | bytes 393224 | tf_op jit(solution)/shard_map/ppermute | solution.py:358
  6.5 12.0 %collective-permute-start.2 = (bf16[512,128]{1,0:T(8,128)(2,1)S(1)}, bf16[512,128]{1,0:T(8,128)(2,1)S(1)}, u32[]{:S(2)}, u32[]{:S(2)}) collective-permute-start(bf16[512,128]{1,0:T(8,128)(2,1)S(1)} %get-tuple-element.20), channel_id=1, source_target_pairs={{0,16},{1,17},{2,18},{3,19},{4,20},{5,21},{6,22},{7,23},{8,24},{9,... | collective-permute-start | bytes 393224 | tf_op jit(solution)/shard_map/ppermute | solution.py:358
  9.3 28.0 %all-to-all-start = ((bf16[32,80,128]{2,1,0:T(8,128)(2,1)}), bf16[32,80,128]{2,1,0:T(8,128)(2,1)S(1)}, u32[]{:S(2)}, u32[]{:S(2)}) async-start(bf16[32,80,128]{2,1,0:T(8,128)(2,1)} %product.1), calls=%async_computation | async-start | bytes 1310720 | tf_op jit(solution)/shard_map/all_to_all | solution.py:348
  18.7 3.9 %copy-start = (bf16[512,512]{1,0:T(8,128)(2,1)S(1)}, bf16[512,512]{1,0:T(8,128)(2,1)}, u32[]{:S(2)}) copy-start(bf16[512,512]{1,0:T(8,128)(2,1)} %query_hbm.1) | copy-start | bytes 1572868
  18.8 11.7 %collective-permute-start.6 = (bf16[4,2,64,128]{3,2,1,0:T(8,128)(2,1)S(1)}, bf16[4,2,64,128]{3,2,1,0:T(8,128)(2,1)S(1)}, u32[]{:S(2)}, u32[]{:S(2)}) collective-permute-start(bf16[4,2,64,128]{3,2,1,0:T(8,128)(2,1)S(1)} %get-tuple-element.13), channel_id=1, source_target_pairs={{0,6},{1,7},{2,0},{3,1},{4,2},{5,3},{6,4},{7,5},{8,14},{9,15},{10,... | collective-permute-start | bytes 393224 | tf_op jit(solution)/shard_map/ppermute | solution.py:370
  21.5 9.0 %collective-permute-start.5 = (bf16[4,2,64,128]{3,2,1,0:T(8,128)(2,1)S(1)}, bf16[4,2,64,128]{3,2,1,0:T(8,128)(2,1)S(1)}, u32[]{:S(2)}, u32[]{:S(2)}) collective-permute-start(bf16[4,2,64,128]{3,2,1,0:T(8,128)(2,1)S(1)} %get-tuple-element.14), channel_id=1, source_target_pairs={{0,4},{1,5},{2,6},{3,7},{4,0},{5,1},{6,2},{7,3},{8,12},{9,13},{10,... | collective-permute-start | bytes 393224 | tf_op jit(solution)/shard_map/ppermute | solution.py:370
  22.0 12.3 %collective-permute-start.4 = (bf16[4,2,64,128]{3,2,1,0:T(8,128)(2,1)S(1)}, bf16[4,2,64,128]{3,2,1,0:T(8,128)(2,1)S(1)}, u32[]{:S(2)}, u32[]{:S(2)}) collective-permute-start(bf16[4,2,64,128]{3,2,1,0:T(8,128)(2,1)S(1)} %get-tuple-element.15), channel_id=1, source_target_pairs={{0,2},{1,3},{2,4},{3,5},{4,6},{5,7},{6,0},{7,1},{8,10},{9,11},{10,... | collective-permute-start | bytes 393224 | tf_op jit(solution)/shard_map/ppermute | solution.py:370
  22.6 7.8 %collective-permute-start = (bf16[3,2,512]{2,1,0:T(2,128)(2,1)S(1)}, bf16[3,2,512]{2,1,0:T(2,128)(2,1)S(1)}, u32[]{:S(2)}, u32[]{:S(2)}) collective-permute-start(bf16[3,2,512]{2,1,0:T(2,128)(2,1)S(1)} %pad_maximum_fusion), channel_id=1, source_target_pairs={{0,1},{1,2},{2,3},{3,4},{4,5},{5,6},{6,7},{7,8},{8,9},{9,10},{10,1... | collective-permute-start | bytes 18440 | tf_op jit(solution)/shard_map/ppermute | solution.py:345
  34.3 3.0 %copy-start.7 = (bf16[768,256]{1,0:T(8,128)(2,1)S(1)}, bf16[768,256]{1,0:T(8,128)(2,1)}, u32[]{:S(2)}) copy-start(bf16[768,256]{1,0:T(8,128)(2,1)} %constant.123.clone.mats_ref) | copy-start | bytes 1179652
  34.3 3.0 %copy-start.8 = (f32[2,128,128]{2,1,0:T(8,128)S(1)}, f32[2,128,128]{2,1,0:T(8,128)}, u32[]{:S(2)}) copy-start(f32[2,128,128]{2,1,0:T(8,128)} %constant.124.clone.twiddle_ref) | copy-start | bytes 393220
  34.3 1.9 %collective-permute-start.7 = (bf16[4,4,64,128]{3,2,1,0:T(8,128)(2,1)S(1)}, bf16[4,4,64,128]{3,2,1,0:T(8,128)(2,1)S(1)}, u32[]{:S(2)}, u32[]{:S(2)}) collective-permute-start(bf16[4,4,64,128]{3,2,1,0:T(8,128)(2,1)S(1)} %other.2), channel_id=1, source_target_pairs={{0,1},{1,0},{2,3},{3,2},{4,5},{5,4},{6,7},{7,6},{8,9},{9,8},{10,11... | collective-permute-start | bytes 786440 | tf_op jit(solution)/shard_map/ppermute | solution.py:388
  43.5 9.4 %collective-permute-start.10 = (bf16[8,32,128]{2,1,0:T(8,128)(2,1)S(1)}, bf16[8,32,128]{2,1,0:T(8,128)(2,1)S(1)}, u32[]{:S(2)}, u32[]{:S(2)}) collective-permute-start(bf16[8,32,128]{2,1,0:T(8,128)(2,1)S(1)} %get-tuple-element.25), channel_id=1, source_target_pairs={{0,24},{1,25},{2,26},{3,27},{4,28},{5,29},{6,30},{7,31},{8,0},{9,1... | collective-permute-start | bytes 196616 | tf_op jit(solution)/shard_map/ppermute | solution.py:423
  46.3 7.2 %collective-permute-start.9 = (bf16[8,32,128]{2,1,0:T(8,128)(2,1)S(1)}, bf16[8,32,128]{2,1,0:T(8,128)(2,1)S(1)}, u32[]{:S(2)}, u32[]{:S(2)}) collective-permute-start(bf16[8,32,128]{2,1,0:T(8,128)(2,1)S(1)} %get-tuple-element.26), channel_id=1, source_target_pairs={{0,16},{1,17},{2,18},{3,19},{4,20},{5,21},{6,22},{7,23},{8,24},{9,... | collective-permute-start | bytes 196616 | tf_op jit(solution)/shard_map/ppermute | solution.py:423
  46.8 6.7 %collective-permute-start.8 = (bf16[8,32,128]{2,1,0:T(8,128)(2,1)S(1)}, bf16[8,32,128]{2,1,0:T(8,128)(2,1)S(1)}, u32[]{:S(2)}, u32[]{:S(2)}) collective-permute-start(bf16[8,32,128]{2,1,0:T(8,128)(2,1)S(1)} %get-tuple-element.27), channel_id=1, source_target_pairs={{0,8},{1,9},{2,10},{3,11},{4,12},{5,13},{6,14},{7,15},{8,16},{9,17... | collective-permute-start | bytes 196616 | tf_op jit(solution)/shard_map/ppermute | solution.py:423
  48.1 18.7 %all-to-all-start.1 = ((bf16[32,48,128]{2,1,0:T(8,128)(2,1)}), bf16[32,48,128]{2,1,0:T(8,128)(2,1)S(1)}, u32[]{:S(2)}, u32[]{:S(2)}) async-start(bf16[32,48,128]{2,1,0:T(8,128)(2,1)} %get-tuple-element.12), calls=%async_computation.1 | async-start | bytes 786432 | tf_op jit(solution)/shard_map/all_to_all | solution.py:348
  53.5 3.4 %copy-start.4 = (bf16[512,512]{1,0:T(8,128)(2,1)S(1)}, bf16[512,512]{1,0:T(8,128)(2,1)}, u32[]{:S(2)}) copy-start(bf16[512,512]{1,0:T(8,128)(2,1)} %value_hbm.1) | copy-start | bytes 1572868
  53.5 3.4 %copy-start.2 = (bf16[512,512]{1,0:T(8,128)(2,1)S(1)}, bf16[512,512]{1,0:T(8,128)(2,1)}, u32[]{:S(2)}) copy-start(bf16[512,512]{1,0:T(8,128)(2,1)} %key_hbm.1) | copy-start | bytes 1572868
  53.5 5.2 %collective-permute-start.13 = (bf16[4,2,32,128]{3,2,1,0:T(8,128)(2,1)S(1)}, bf16[4,2,32,128]{3,2,1,0:T(8,128)(2,1)S(1)}, u32[]{:S(2)}, u32[]{:S(2)}) collective-permute-start(bf16[4,2,32,128]{3,2,1,0:T(8,128)(2,1)S(1)} %get-tuple-element.21), channel_id=1, source_target_pairs={{0,6},{1,7},{2,0},{3,1},{4,2},{5,3},{6,4},{7,5},{8,14},{9,15},{10,... | collective-permute-start | bytes 196616 | tf_op jit(solution)/shard_map/ppermute | solution.py:435
  55.7 1.2 %copy-start.6 = (f32[512]{0:T(512)S(1)}, f32[512]{0:T(512)}, u32[]{:S(2)}) copy-start(f32[512]{0:T(512)} %param.13) | copy-start | bytes 6148
  55.7 6.2 %collective-permute-start.12 = (bf16[4,2,32,128]{3,2,1,0:T(8,128)(2,1)S(1)}, bf16[4,2,32,128]{3,2,1,0:T(8,128)(2,1)S(1)}, u32[]{:S(2)}, u32[]{:S(2)}) collective-permute-start(bf16[4,2,32,128]{3,2,1,0:T(8,128)(2,1)S(1)} %get-tuple-element.22), channel_id=1, source_target_pairs={{0,4},{1,5},{2,6},{3,7},{4,0},{5,1},{6,2},{7,3},{8,12},{9,13},{10,... | collective-permute-start | bytes 196616 | tf_op jit(solution)/shard_map/ppermute | solution.py:435
  56.3 7.9 %collective-permute-start.11 = (bf16[4,2,32,128]{3,2,1,0:T(8,128)(2,1)S(1)}, bf16[4,2,32,128]{3,2,1,0:T(8,128)(2,1)S(1)}, u32[]{:S(2)}, u32[]{:S(2)}) collective-permute-start(bf16[4,2,32,128]{3,2,1,0:T(8,128)(2,1)S(1)} %get-tuple-element.23), channel_id=1, source_target_pairs={{0,2},{1,3},{2,4},{3,5},{4,6},{5,7},{6,0},{7,1},{8,10},{9,11},{10,... | collective-permute-start | bytes 196616 | tf_op jit(solution)/shard_map/ppermute | solution.py:435
  64.2 1.6 %collective-permute-start.14 = (bf16[4,4,32,128]{3,2,1,0:T(8,128)(2,1)S(1)}, bf16[4,4,32,128]{3,2,1,0:T(8,128)(2,1)S(1)}, u32[]{:S(2)}, u32[]{:S(2)}) collective-permute-start(bf16[4,4,32,128]{3,2,1,0:T(8,128)(2,1)S(1)} %other.3), channel_id=1, source_target_pairs={{0,1},{1,0},{2,3},{3,2},{4,5},{5,4},{6,7},{7,6},{8,9},{9,8},{10,11... | collective-permute-start | bytes 393224 | tf_op jit(solution)/shard_map/ppermute | solution.py:450

commit v5 on v4

--- a/solution.py
+++ b/solution.py
@@ -18,6 +18,7 @@
 PACK = 16
 BLOCKS = 32
 NEAR = 4
+TURN_ORDER = (0, 2, 3, 1)
 TOKENS = 512
 CHANS = 512
 QUARTERS = TOKENS // SIDE
@@ -76,7 +77,7 @@
 
 def turn_kernel(*refs):
     *blocks, out_ref = refs
-    for i, ref in enumerate(blocks):
+    for i, ref in zip(TURN_ORDER, blocks):
         for q in range(QUARTERS):
             block = ref[q * SIDE : (q + 1) * SIDE, :].astype(F32).T.astype(BF16)
             out_ref[:, i, :, q * PACK : (q + 1) * PACK, :] = block.reshape(NEAR, 2, PACK, SIDE)
@@ -363,7 +364,7 @@
         compiler_params=small,
         cost_estimate=pl.CostEstimate(flops=2 * 10**10, bytes_accessed=2**20, transcendentals=0),
         name="turn",
-    )(*[filter_for(d) for d in range(NEAR)])
+    )(*[filter_for(d) for d in TURN_ORDER])
 
     def turned_for(d):
         part = lax.dynamic_index_in_dim(turned, (y + d) % NEAR, 0, keepdims=False)

time: 68.5 us -> 66.7 us (0.974)
  starting transfers between devices: 37.3 us -> 35.3 us
    all_to_all x2, starting transfers between devices: 13.8 us -> 11.3 us  [swap(): return lax.all_to_all(x, 'seq', split_axis=0, concat_axis=0, tiled=True)]
where the time goes in v5:
time: 66.7 us; the launch traced here: 66.4 us
  starting transfers between devices  35.3 us (53%)
  waiting for transfers between devices  17.3 us (26%)
  Pallas kernels  12 us (18%)
  local copies, waits for them, and re-layouts  1.39 us (2%)
    all_to_all x2, starting transfers between devices, swap(): return lax.all_to_all(x, 'seq', split_axis=0, concat_axis=0, tiled=True)  11.3 us
    ppermute x3, starting transfers between devices, filter_for(): return lax.ppermute(part, 'seq', along_z[d]) if d else part  6.26 us
    pallas_call x1, Pallas kernels, local(): pl.pallas_call(middle_kernel, in_specs=[smem] + [vmem] * 8, out_shape=[ja...  6.21 us
    ppermute x3, waiting for transfers between devices, picked_for(): return lax.ppermute(part, 'seq', along_y[d]) if d else part  5.39 us
    ppermute x3, starting transfers between devices, conv_for(): return lax.ppermute(part, 'seq', along_z[d]) if d else part  4.59 us
    ppermute x1, starting transfers between devices, local(): halo = lax.ppermute(last_rows, 'seq', pairs)  4.49 us
    ppermute x3, waiting for transfers between devices, turned_for(): return lax.ppermute(part, 'seq', along_y[d]) if d else part  3.86 us
    ppermute x3, starting transfers between devices, turned_for(): return lax.ppermute(part, 'seq', along_y[d]) if d else part  3.83 us
  transfers between devices with their start and end apart: 17, of which 9 were waited for; matrix products, arithmetic and copies ran while one was open for 0% of the time, Pallas kernels for 7%

profile of v5, /device:TPU:1, one launch (start us, length us, event | category | flops | bytes accessed | tf_op | source)
XLA Modules:
  0.0 66.4 jit_solution(12956419254654928026)
XLA Ops:
  0.0 0.0 copy-start.5
  0.0 0.0 copy-start.1
  0.0 0.0 copy-start.3
  0.0 1.2 %constant_dynamic-slice_fusion.4 = (bf16[512,128]{1,0:T(8,128)(2,1)S(1)}, bf16[512,128]{1,0:T(8,128)(2,1)S(1)}, bf16[512,128]{1,0:T(8,128)(2,1)S(1)}, bf16[512,128]{1,0:T(8,128)(2,1)S(1)}) fusion(bf16[512,512]{1,0:T(8,128)(2,1)} %param.11, s32[]{:T(128)S(6)} %select_n.112, s32[]{:T(128)S(6)} %select_n.108, s32[]{:T(128)S(6)} %select_n.106, s32[]{:T(128)S(6)} %select_n.110), kind=kLoop, calls=%fused_computation.13 | loop fusion | bytes 1048592 | tf_op jit(solution)/shard_map/dynamic_slice | solution.py:358
  1.3 2.5 %collective-permute-start.3 = (bf16[512,128]{1,0:T(8,128)(2,1)S(1)}, bf16[512,128]{1,0:T(8,128)(2,1)S(1)}, u32[]{:S(2)}, u32[]{:S(2)}) collective-permute-start(bf16[512,128]{1,0:T(8,128)(2,1)S(1)} %get-tuple-element.17), channel_id=1, source_target_pairs={{0,8},{1,9},{2,10},{3,11},{4,12},{5,13},{6,14},{7,15},{8,16},{9,17... | collective-permute-start | bytes 393224 | tf_op jit(solution)/shard_map/ppermute | solution.py:359
  3.8 3.0 %collective-permute-start.1 = (bf16[512,128]{1,0:T(8,128)(2,1)S(1)}, bf16[512,128]{1,0:T(8,128)(2,1)S(1)}, u32[]{:S(2)}, u32[]{:S(2)}) collective-permute-start(bf16[512,128]{1,0:T(8,128)(2,1)S(1)} %get-tuple-element.18), channel_id=1, source_target_pairs={{0,16},{1,17},{2,18},{3,19},{4,20},{5,21},{6,22},{7,23},{8,24},{9,... | collective-permute-start | bytes 393224 | tf_op jit(solution)/shard_map/ppermute | solution.py:359
  6.8 0.7 %collective-permute-start.2 = (bf16[512,128]{1,0:T(8,128)(2,1)S(1)}, bf16[512,128]{1,0:T(8,128)(2,1)S(1)}, u32[]{:S(2)}, u32[]{:S(2)}) collective-permute-start(bf16[512,128]{1,0:T(8,128)(2,1)S(1)} %get-tuple-element.20), channel_id=1, source_target_pairs={{0,24},{1,25},{2,26},{3,27},{4,28},{5,29},{6,30},{7,31},{8,0},{9,1... | collective-permute-start | bytes 393224 | tf_op jit(solution)/shard_map/ppermute | solution.py:359
  7.5 0.0 copy-done.5
  7.5 0.0 copy-done.1
  7.5 0.0 copy-done.3
  7.5 2.4 %product.1 = bf16[32,80,128]{2,1,0:T(8,128)(2,1)} custom-call(bf16[512,512]{1,0:T(8,128)(2,1)S(1)} %copy-done.1, bf16[512,512]{1,0:T(8,128)(2,1)S(1)} %copy-done.3, f32[3,3,512]{2,1,0:T(4,128)S(1)} %copy-done.5), custom_call_target="tpu_custom_call" | custom-call | flops 20000000000 | bytes 4194304 | tf_op jit(solution)/shard_map/product/pallas_call | solution.py:391
  10.0 6.6 %all-to-all-start = ((bf16[32,80,128]{2,1,0:T(8,128)(2,1)}), bf16[32,80,128]{2,1,0:T(8,128)(2,1)S(1)}, u32[]{:S(2)}, u32[]{:S(2)}) async-start(bf16[32,80,128]{2,1,0:T(8,128)(2,1)} %product.1), calls=%async_computation | async-start | bytes 1310720 | tf_op jit(solution)/shard_map/all_to_all | solution.py:349
  16.7 0.0 collective-permute-done.3.refs_3_
  16.7 0.0 collective-permute-done.1.refs_1_
  16.7 0.0 collective-permute-done.2.refs_2_
  16.7 0.2 turn.1
  16.9 0.0 copy-start
  16.9 0.1 dynamic-slice_bitcast_fusion
  17.0 2.7 %collective-permute-start.6 = (bf16[4,2,64,128]{3,2,1,0:T(8,128)(2,1)S(1)}, bf16[4,2,64,128]{3,2,1,0:T(8,128)(2,1)S(1)}, u32[]{:S(2)}, u32[]{:S(2)}) collective-permute-start(bf16[4,2,64,128]{3,2,1,0:T(8,128)(2,1)S(1)} %get-tuple-element.13), channel_id=1, source_target_pairs={{0,6},{1,7},{2,0},{3,1},{4,2},{5,3},{6,4},{7,5},{8,14},{9,15},{10,... | collective-permute-start | bytes 393224 | tf_op jit(solution)/shard_map/ppermute | solution.py:371
  19.7 0.6 collective-permute-start.5
  20.2 0.6 collective-permute-start.4
  20.8 0.0 copy-done
  20.8 4.5 %collective-permute-start = (bf16[3,2,512]{2,1,0:T(2,128)(2,1)S(1)}, bf16[3,2,512]{2,1,0:T(2,128)(2,1)S(1)}, u32[]{:S(2)}, u32[]{:S(2)}) collective-permute-start(bf16[3,2,512]{2,1,0:T(2,128)(2,1)S(1)} %pad_maximum_fusion), channel_id=1, source_target_pairs={{0,1},{1,2},{2,3},{3,4},{4,5},{5,6},{6,7},{7,8},{8,9},{9,10},{10,1... | collective-permute-start | bytes 18440 | tf_op jit(solution)/shard_map/ppermute | solution.py:346
  25.3 3.3 %collective-permute-done.ready_hbm.halo_ref = bf16[3,2,512]{2,1,0:T(2,128)(2,1)S(1)} collective-permute-done((bf16[3,2,512]{2,1,0:T(2,128)(2,1)S(1)}, bf16[3,2,512]{2,1,0:T(2,128)(2,1)S(1)}, u32[]{:S(2)}, u32[]{:S(2)}) %collective-permute-start) | collective-permute-done | bytes 6176 | tf_op jit(solution)/shard_map/ppermute | solution.py:346
  28.6 0.0 collective-permute-done.6.b3_ref
  28.6 0.0 collective-permute-done.5.b2_ref
  28.6 3.9 %collective-permute-done.4.b1_ref = bf16[4,2,64,128]{3,2,1,0:T(8,128)(2,1)S(1)} collective-permute-done((bf16[4,2,64,128]{3,2,1,0:T(8,128)(2,1)S(1)}, bf16[4,2,64,128]{3,2,1,0:T(8,128)(2,1)S(1)}, u32[]{:S(2)}, u32[]{:S(2)}) %collective-permute-start.4) | collective-permute-done | bytes 131104 | tf_op jit(solution)/shard_map/ppermute | solution.py:371
  32.5 0.0 copy-start.7
  32.5 0.0 copy-start.8
  32.5 0.8 %collective-permute-start.7 = (bf16[4,4,64,128]{3,2,1,0:T(8,128)(2,1)S(1)}, bf16[4,4,64,128]{3,2,1,0:T(8,128)(2,1)S(1)}, u32[]{:S(2)}, u32[]{:S(2)}) collective-permute-start(bf16[4,4,64,128]{3,2,1,0:T(8,128)(2,1)S(1)} %other.2), channel_id=1, source_target_pairs={{0,1},{1,0},{2,3},{3,2},{4,5},{5,4},{6,7},{7,6},{8,9},{9,8},{10,11... | collective-permute-start | bytes 786440 | tf_op jit(solution)/shard_map/ppermute | solution.py:389
  33.3 1.2 %collective-permute-done.7.other_ref = bf16[4,4,64,128]{3,2,1,0:T(8,128)(2,1)S(1)} collective-permute-done((bf16[4,4,64,128]{3,2,1,0:T(8,128)(2,1)S(1)}, bf16[4,4,64,128]{3,2,1,0:T(8,128)(2,1)S(1)}, u32[]{:S(2)}, u32[]{:S(2)}) %collective-permute-start.7) | collective-permute-done | bytes 262176 | tf_op jit(solution)/shard_map/ppermute | solution.py:389
  34.5 1.0 %all-to-all-done.in_ref = bf16[32,80,128]{2,1,0:T(8,128)(2,1)S(1)} async-done(((bf16[32,80,128]{2,1,0:T(8,128)(2,1)}), bf16[32,80,128]{2,1,0:T(8,128)(2,1)S(1)}, u32[]{:S(2)}, u32[]{:S(2)}) %all-to-all-start) | async-done | bytes 655392 | tf_op jit(solution)/shard_map/all_to_all | solution.py:349
  35.5 0.0 copy-done.7
  35.5 0.0 copy-done.8
  35.5 6.2 %middle.1 = (bf16[32,48,128]{2,1,0:T(8,128)(2,1)}, bf16[32,32,128]{2,1,0:T(8,128)(2,1)S(1)}) custom-call(s32[1]{0:T(128)} %bitcast.place_ref, bf16[32,80,128]{2,1,0:T(8,128)(2,1)S(1)} %all-to-all-done.in_ref, bf16[4,2,64,128]{3,2,1,0:T(8,128)(2,1)S(1)} %get-tuple-element.16.b0_ref, bf16[4,2,64,128]{3,2,1,0:T(8,128)(2,1)S(1)} %collective-permute-done.4.b1_ref, ...), custom_call_target="tpu_custom_call" | custom-call | flops 8000000000 | bytes 2000000 | tf_op jit(solution)/shard_map/middle/pallas_call | solution.py:409
  41.7 2.7 %collective-permute-start.10 = (bf16[8,32,128]{2,1,0:T(8,128)(2,1)S(1)}, bf16[8,32,128]{2,1,0:T(8,128)(2,1)S(1)}, u32[]{:S(2)}, u32[]{:S(2)}) collective-permute-start(bf16[8,32,128]{2,1,0:T(8,128)(2,1)S(1)} %get-tuple-element.25), channel_id=1, source_target_pairs={{0,24},{1,25},{2,26},{3,27},{4,28},{5,29},{6,30},{7,31},{8,0},{9,1... | collective-permute-start | bytes 196616 | tf_op jit(solution)/shard_map/ppermute | solution.py:424
  44.5 0.5 collective-permute-start.9
  45.0 1.4 %collective-permute-start.8 = (bf16[8,32,128]{2,1,0:T(8,128)(2,1)S(1)}, bf16[8,32,128]{2,1,0:T(8,128)(2,1)S(1)}, u32[]{:S(2)}, u32[]{:S(2)}) collective-permute-start(bf16[8,32,128]{2,1,0:T(8,128)(2,1)S(1)} %get-tuple-element.27), channel_id=1, source_target_pairs={{0,8},{1,9},{2,10},{3,11},{4,12},{5,13},{6,14},{7,15},{8,16},{9,17... | collective-permute-start | bytes 196616 | tf_op jit(solution)/shard_map/ppermute | solution.py:424
  46.3 4.8 %all-to-all-start.1 = ((bf16[32,48,128]{2,1,0:T(8,128)(2,1)}), bf16[32,48,128]{2,1,0:T(8,128)(2,1)S(1)}, u32[]{:S(2)}, u32[]{:S(2)}) async-start(bf16[32,48,128]{2,1,0:T(8,128)(2,1)} %get-tuple-element.12), calls=%async_computation.1 | async-start | bytes 786432 | tf_op jit(solution)/shard_map/all_to_all | solution.py:349
  51.1 0.0 collective-permute-done.10.refs_3_
  51.1 0.5 collective-permute-done.9.refs_2_
  51.6 0.0 collective-permute-done.8.refs_1_
  51.6 0.0 copy-start.4
  51.7 0.0 copy-start.2
  51.7 2.2 %collective-permute-start.13 = (bf16[4,2,32,128]{3,2,1,0:T(8,128)(2,1)S(1)}, bf16[4,2,32,128]{3,2,1,0:T(8,128)(2,1)S(1)}, u32[]{:S(2)}, u32[]{:S(2)}) collective-permute-start(bf16[4,2,32,128]{3,2,1,0:T(8,128)(2,1)S(1)} %get-tuple-element.21), channel_id=1, source_target_pairs={{0,6},{1,7},{2,0},{3,1},{4,2},{5,3},{6,4},{7,5},{8,14},{9,15},{10,... | collective-permute-start | bytes 196616 | tf_op jit(solution)/shard_map/ppermute | solution.py:436
  53.9 0.0 copy-start.6
  53.9 0.5 collective-permute-start.12
  54.5 0.6 collective-permute-start.11
  55.1 0.0 copy-done.4
  55.1 0.0 copy-done.2
  55.1 0.0 copy-done.6
  55.1 1.9 %gate.1 = (f32[512,512]{1,0:T(8,128)S(1)}, f32[512,512]{1,0:T(8,128)S(1)}) custom-call(bf16[512,512]{1,0:T(8,128)(2,1)S(1)} %copy-done, bf16[512,512]{1,0:T(8,128)(2,1)S(1)} %copy-done.2, bf16[512,512]{1,0:T(8,128)(2,1)S(1)} %copy-done.4, bf16[3,2,512]{2,1,0:T(2,128)(2,1)S(1)} %collective-permute-done.ready_hbm.halo_ref, f32[3,3,512]{2,1,0:T(4,128)S(1)} %copy-done.5, ...), custom_call_target="tpu_custom_call" | custom-call | flops 1000000000 | bytes 4000000 | tf_op jit(solution)/shard_map/gate/pallas_call | solution.py:441
  57.0 0.0 collective-permute-done.13.b3_ref
  57.0 3.2 %collective-permute-done.12.b2_ref = bf16[4,2,32,128]{3,2,1,0:T(8,128)(2,1)S(1)} collective-permute-done((bf16[4,2,32,128]{3,2,1,0:T(8,128)(2,1)S(1)}, bf16[4,2,32,128]{3,2,1,0:T(8,128)(2,1)S(1)}, u32[]{:S(2)}, u32[]{:S(2)}) %collective-permute-start.12) | collective-permute-done | bytes 65568 | tf_op jit(solution)/shard_map/ppermute | solution.py:436
  60.2 2.2 %collective-permute-done.11.b1_ref = bf16[4,2,32,128]{3,2,1,0:T(8,128)(2,1)S(1)} collective-permute-done((bf16[4,2,32,128]{3,2,1,0:T(8,128)(2,1)S(1)}, bf16[4,2,32,128]{3,2,1,0:T(8,128)(2,1)S(1)}, u32[]{:S(2)}, u32[]{:S(2)}) %collective-permute-start.11) | collective-permute-done | bytes 65568 | tf_op jit(solution)/shard_map/ppermute | solution.py:436
  62.4 0.7 collective-permute-start.14
  63.0 1.0 %collective-permute-done.14.other_ref = bf16[4,4,32,128]{3,2,1,0:T(8,128)(2,1)S(1)} collective-permute-done((bf16[4,4,32,128]{3,2,1,0:T(8,128)(2,1)S(1)}, bf16[4,4,32,128]{3,2,1,0:T(8,128)(2,1)S(1)}, u32[]{:S(2)}, u32[]{:S(2)}) %collective-permute-start.14) | collective-permute-done | bytes 131104 | tf_op jit(solution)/shard_map/ppermute | solution.py:451
  64.0 1.0 %all-to-all-done.1.conv_ref = bf16[32,48,128]{2,1,0:T(8,128)(2,1)S(1)} async-done(((bf16[32,48,128]{2,1,0:T(8,128)(2,1)}), bf16[32,48,128]{2,1,0:T(8,128)(2,1)S(1)}, u32[]{:S(2)}, u32[]{:S(2)}) %all-to-all-start.1) | async-done | bytes 393248 | tf_op jit(solution)/shard_map/all_to_all | solution.py:349
  65.0 1.2 %end.1 = bf16[512,512]{1,0:T(8,128)(2,1)} custom-call(s32[1]{0:T(128)} %bitcast.place_ref, f32[512,512]{1,0:T(8,128)S(1)} %get-tuple-element.10.mix_ref, f32[512,512]{1,0:T(8,128)S(1)} %get-tuple-element.11.ready_hbm.direct_ref, bf16[32,48,128]{2,1,0:T(8,128)(2,1)S(1)} %all-to-all-done.1.conv_ref, bf16[4,2,32,128]{3,2,1,0:T(8,128)(2,1)S(1)} %get-tuple-element.24.b0_ref, ...), custom_call_target="tpu_custom_call" | custom-call | tf_op jit(solution)/shard_map/end/pallas_call | solution.py:452
  (8 shorter events, 0.1 us)
Async XLA Ops:
  0.0 7.5 %copy-start.5 = (f32[3,3,512]{2,1,0:T(4,128)S(1)}, f32[3,3,512]{2,1,0:T(4,128)}, u32[]{:S(2)}) copy-start(f32[3,3,512]{2,1,0:T(4,128)} %taps_ref.3) | copy-start | bytes 55300
  0.0 7.5 %copy-start.1 = (bf16[512,512]{1,0:T(8,128)(2,1)S(1)}, bf16[512,512]{1,0:T(8,128)(2,1)}, u32[]{:S(2)}) copy-start(bf16[512,512]{1,0:T(8,128)(2,1)} %key_hbm.1) | copy-start | bytes 1572868
  0.0 7.5 %copy-start.3 = (bf16[512,512]{1,0:T(8,128)(2,1)S(1)}, bf16[512,512]{1,0:T(8,128)(2,1)}, u32[]{:S(2)}) copy-start(bf16[512,512]{1,0:T(8,128)(2,1)} %value_hbm.1) | copy-start | bytes 1572868
  1.3 15.4 %collective-permute-start.3 = (bf16[512,128]{1,0:T(8,128)(2,1)S(1)}, bf16[512,128]{1,0:T(8,128)(2,1)S(1)}, u32[]{:S(2)}, u32[]{:S(2)}) collective-permute-start(bf16[512,128]{1,0:T(8,128)(2,1)S(1)} %get-tuple-element.17), channel_id=1, source_target_pairs={{0,8},{1,9},{2,10},{3,11},{4,12},{5,13},{6,14},{7,15},{8,16},{9,17... | collective-permute-start | bytes 393224 | tf_op jit(solution)/shard_map/ppermute | solution.py:359
  3.8 12.9 %collective-permute-start.1 = (bf16[512,128]{1,0:T(8,128)(2,1)S(1)}, bf16[512,128]{1,0:T(8,128)(2,1)S(1)}, u32[]{:S(2)}, u32[]{:S(2)}) collective-permute-start(bf16[512,128]{1,0:T(8,128)(2,1)S(1)} %get-tuple-element.18), channel_id=1, source_target_pairs={{0,16},{1,17},{2,18},{3,19},{4,20},{5,21},{6,22},{7,23},{8,24},{9,... | collective-permute-start | bytes 393224 | tf_op jit(solution)/shard_map/ppermute | solution.py:359
  6.8 9.9 %collective-permute-start.2 = (bf16[512,128]{1,0:T(8,128)(2,1)S(1)}, bf16[512,128]{1,0:T(8,128)(2,1)S(1)}, u32[]{:S(2)}, u32[]{:S(2)}) collective-permute-start(bf16[512,128]{1,0:T(8,128)(2,1)S(1)} %get-tuple-element.20), channel_id=1, source_target_pairs={{0,24},{1,25},{2,26},{3,27},{4,28},{5,29},{6,30},{7,31},{8,0},{9,1... | collective-permute-start | bytes 393224 | tf_op jit(solution)/shard_map/ppermute | solution.py:359
  10.0 25.6 %all-to-all-start = ((bf16[32,80,128]{2,1,0:T(8,128)(2,1)}), bf16[32,80,128]{2,1,0:T(8,128)(2,1)S(1)}, u32[]{:S(2)}, u32[]{:S(2)}) async-start(bf16[32,80,128]{2,1,0:T(8,128)(2,1)} %product.1), calls=%async_computation | async-start | bytes 1310720 | tf_op jit(solution)/shard_map/all_to_all | solution.py:349
  16.9 3.9 %copy-start = (bf16[512,512]{1,0:T(8,128)(2,1)S(1)}, bf16[512,512]{1,0:T(8,128)(2,1)}, u32[]{:S(2)}) copy-start(bf16[512,512]{1,0:T(8,128)(2,1)} %query_hbm.1) | copy-start | bytes 1572868
  17.0 11.7 %collective-permute-start.6 = (bf16[4,2,64,128]{3,2,1,0:T(8,128)(2,1)S(1)}, bf16[4,2,64,128]{3,2,1,0:T(8,128)(2,1)S(1)}, u32[]{:S(2)}, u32[]{:S(2)}) collective-permute-start(bf16[4,2,64,128]{3,2,1,0:T(8,128)(2,1)S(1)} %get-tuple-element.13), channel_id=1, source_target_pairs={{0,6},{1,7},{2,0},{3,1},{4,2},{5,3},{6,4},{7,5},{8,14},{9,15},{10,... | collective-permute-start | bytes 393224 | tf_op jit(solution)/shard_map/ppermute | solution.py:371
  19.7 9.0 %collective-permute-start.5 = (bf16[4,2,64,128]{3,2,1,0:T(8,128)(2,1)S(1)}, bf16[4,2,64,128]{3,2,1,0:T(8,128)(2,1)S(1)}, u32[]{:S(2)}, u32[]{:S(2)}) collective-permute-start(bf16[4,2,64,128]{3,2,1,0:T(8,128)(2,1)S(1)} %get-tuple-element.14), channel_id=1, source_target_pairs={{0,4},{1,5},{2,6},{3,7},{4,0},{5,1},{6,2},{7,3},{8,12},{9,13},{10,... | collective-permute-start | bytes 393224 | tf_op jit(solution)/shard_map/ppermute | solution.py:371
  20.2 12.3 %collective-permute-start.4 = (bf16[4,2,64,128]{3,2,1,0:T(8,128)(2,1)S(1)}, bf16[4,2,64,128]{3,2,1,0:T(8,128)(2,1)S(1)}, u32[]{:S(2)}, u32[]{:S(2)}) collective-permute-start(bf16[4,2,64,128]{3,2,1,0:T(8,128)(2,1)S(1)} %get-tuple-element.15), channel_id=1, source_target_pairs={{0,2},{1,3},{2,4},{3,5},{4,6},{5,7},{6,0},{7,1},{8,10},{9,11},{10,... | collective-permute-start | bytes 393224 | tf_op jit(solution)/shard_map/ppermute | solution.py:371
  20.8 7.8 %collective-permute-start = (bf16[3,2,512]{2,1,0:T(2,128)(2,1)S(1)}, bf16[3,2,512]{2,1,0:T(2,128)(2,1)S(1)}, u32[]{:S(2)}, u32[]{:S(2)}) collective-permute-start(bf16[3,2,512]{2,1,0:T(2,128)(2,1)S(1)} %pad_maximum_fusion), channel_id=1, source_target_pairs={{0,1},{1,2},{2,3},{3,4},{4,5},{5,6},{6,7},{7,8},{8,9},{9,10},{10,1... | collective-permute-start | bytes 18440 | tf_op jit(solution)/shard_map/ppermute | solution.py:346
  32.5 3.0 %copy-start.7 = (bf16[768,256]{1,0:T(8,128)(2,1)S(1)}, bf16[768,256]{1,0:T(8,128)(2,1)}, u32[]{:S(2)}) copy-start(bf16[768,256]{1,0:T(8,128)(2,1)} %constant.123.clone.mats_ref) | copy-start | bytes 1179652
  32.5 3.0 %copy-start.8 = (f32[2,128,128]{2,1,0:T(8,128)S(1)}, f32[2,128,128]{2,1,0:T(8,128)}, u32[]{:S(2)}) copy-start(f32[2,128,128]{2,1,0:T(8,128)} %constant.124.clone.twiddle_ref) | copy-start | bytes 393220
  32.5 1.9 %collective-permute-start.7 = (bf16[4,4,64,128]{3,2,1,0:T(8,128)(2,1)S(1)}, bf16[4,4,64,128]{3,2,1,0:T(8,128)(2,1)S(1)}, u32[]{:S(2)}, u32[]{:S(2)}) collective-permute-start(bf16[4,4,64,128]{3,2,1,0:T(8,128)(2,1)S(1)} %other.2), channel_id=1, source_target_pairs={{0,1},{1,0},{2,3},{3,2},{4,5},{5,4},{6,7},{7,6},{8,9},{9,8},{10,11... | collective-permute-start | bytes 786440 | tf_op jit(solution)/shard_map/ppermute | solution.py:389
  41.7 9.4 %collective-permute-start.10 = (bf16[8,32,128]{2,1,0:T(8,128)(2,1)S(1)}, bf16[8,32,128]{2,1,0:T(8,128)(2,1)S(1)}, u32[]{:S(2)}, u32[]{:S(2)}) collective-permute-start(bf16[8,32,128]{2,1,0:T(8,128)(2,1)S(1)} %get-tuple-element.25), channel_id=1, source_target_pairs={{0,24},{1,25},{2,26},{3,27},{4,28},{5,29},{6,30},{7,31},{8,0},{9,1... | collective-permute-start | bytes 196616 | tf_op jit(solution)/shard_map/ppermute | solution.py:424
  44.5 7.2 %collective-permute-start.9 = (bf16[8,32,128]{2,1,0:T(8,128)(2,1)S(1)}, bf16[8,32,128]{2,1,0:T(8,128)(2,1)S(1)}, u32[]{:S(2)}, u32[]{:S(2)}) collective-permute-start(bf16[8,32,128]{2,1,0:T(8,128)(2,1)S(1)} %get-tuple-element.26), channel_id=1, source_target_pairs={{0,16},{1,17},{2,18},{3,19},{4,20},{5,21},{6,22},{7,23},{8,24},{9,... | collective-permute-start | bytes 196616 | tf_op jit(solution)/shard_map/ppermute | solution.py:424
  45.0 6.7 %collective-permute-start.8 = (bf16[8,32,128]{2,1,0:T(8,128)(2,1)S(1)}, bf16[8,32,128]{2,1,0:T(8,128)(2,1)S(1)}, u32[]{:S(2)}, u32[]{:S(2)}) collective-permute-start(bf16[8,32,128]{2,1,0:T(8,128)(2,1)S(1)} %get-tuple-element.27), channel_id=1, source_target_pairs={{0,8},{1,9},{2,10},{3,11},{4,12},{5,13},{6,14},{7,15},{8,16},{9,17... | collective-permute-start | bytes 196616 | tf_op jit(solution)/shard_map/ppermute | solution.py:424
  46.3 18.7 %all-to-all-start.1 = ((bf16[32,48,128]{2,1,0:T(8,128)(2,1)}), bf16[32,48,128]{2,1,0:T(8,128)(2,1)S(1)}, u32[]{:S(2)}, u32[]{:S(2)}) async-start(bf16[32,48,128]{2,1,0:T(8,128)(2,1)} %get-tuple-element.12), calls=%async_computation.1 | async-start | bytes 786432 | tf_op jit(solution)/shard_map/all_to_all | solution.py:349
  51.6 3.4 %copy-start.4 = (bf16[512,512]{1,0:T(8,128)(2,1)S(1)}, bf16[512,512]{1,0:T(8,128)(2,1)}, u32[]{:S(2)}) copy-start(bf16[512,512]{1,0:T(8,128)(2,1)} %value_hbm.1) | copy-start | bytes 1572868
  51.7 3.4 %copy-start.2 = (bf16[512,512]{1,0:T(8,128)(2,1)S(1)}, bf16[512,512]{1,0:T(8,128)(2,1)}, u32[]{:S(2)}) copy-start(bf16[512,512]{1,0:T(8,128)(2,1)} %key_hbm.1) | copy-start | bytes 1572868
  51.7 5.2 %collective-permute-start.13 = (bf16[4,2,32,128]{3,2,1,0:T(8,128)(2,1)S(1)}, bf16[4,2,32,128]{3,2,1,0:T(8,128)(2,1)S(1)}, u32[]{:S(2)}, u32[]{:S(2)}) collective-permute-start(bf16[4,2,32,128]{3,2,1,0:T(8,128)(2,1)S(1)} %get-tuple-element.21), channel_id=1, source_target_pairs={{0,6},{1,7},{2,0},{3,1},{4,2},{5,3},{6,4},{7,5},{8,14},{9,15},{10,... | collective-permute-start | bytes 196616 | tf_op jit(solution)/shard_map/ppermute | solution.py:436
  53.9 1.2 %copy-start.6 = (f32[512]{0:T(512)S(1)}, f32[512]{0:T(512)}, u32[]{:S(2)}) copy-start(f32[512]{0:T(512)} %param.13) | copy-start | bytes 6148
  53.9 6.2 %collective-permute-start.12 = (bf16[4,2,32,128]{3,2,1,0:T(8,128)(2,1)S(1)}, bf16[4,2,32,128]{3,2,1,0:T(8,128)(2,1)S(1)}, u32[]{:S(2)}, u32[]{:S(2)}) collective-permute-start(bf16[4,2,32,128]{3,2,1,0:T(8,128)(2,1)S(1)} %get-tuple-element.22), channel_id=1, source_target_pairs={{0,4},{1,5},{2,6},{3,7},{4,0},{5,1},{6,2},{7,3},{8,12},{9,13},{10,... | collective-permute-start | bytes 196616 | tf_op jit(solution)/shard_map/ppermute | solution.py:436
  54.5 7.9 %collective-permute-start.11 = (bf16[4,2,32,128]{3,2,1,0:T(8,128)(2,1)S(1)}, bf16[4,2,32,128]{3,2,1,0:T(8,128)(2,1)S(1)}, u32[]{:S(2)}, u32[]{:S(2)}) collective-permute-start(bf16[4,2,32,128]{3,2,1,0:T(8,128)(2,1)S(1)} %get-tuple-element.23), channel_id=1, source_target_pairs={{0,2},{1,3},{2,4},{3,5},{4,6},{5,7},{6,0},{7,1},{8,10},{9,11},{10,... | collective-permute-start | bytes 196616 | tf_op jit(solution)/shard_map/ppermute | solution.py:436
  62.4 1.6 %collective-permute-start.14 = (bf16[4,4,32,128]{3,2,1,0:T(8,128)(2,1)S(1)}, bf16[4,4,32,128]{3,2,1,0:T(8,128)(2,1)S(1)}, u32[]{:S(2)}, u32[]{:S(2)}) collective-permute-start(bf16[4,4,32,128]{3,2,1,0:T(8,128)(2,1)S(1)} %other.3), channel_id=1, source_target_pairs={{0,1},{1,0},{2,3},{3,2},{4,5},{5,4},{6,7},{7,6},{8,9},{9,8},{10,11... | collective-permute-start | bytes 393224 | tf_op jit(solution)/shard_map/ppermute | solution.py:451

commit v6 on v5

--- a/solution.py
+++ b/solution.py
@@ -19,6 +19,7 @@
 BLOCKS = 32
 NEAR = 4
 TURN_ORDER = (0, 2, 3, 1)
+BAND_ORDER = (0, 3, 2, 1)
 TOKENS = 512
 CHANS = 512
 QUARTERS = TOKENS // SIDE
@@ -154,7 +155,7 @@
 def gather_filter(place_ref, band_refs, other_ref, filt_ref):
     me = place_ref[0]
     z, y, core = me // 8, (me // 2) % 4, me % 2
-    for dy, ref in enumerate(band_refs):
+    for dy, ref in zip(BAND_ORDER, band_refs):
         for dz in range(NEAR):
             chip = ((z + NEAR - dz) % NEAR) * 8 + ((y + NEAR - dy) % NEAR) * 2
             for q in range(QUARTERS):
@@ -309,14 +310,14 @@
 
 def other_kernel(place_ref, b0_ref, b1_ref, b2_ref, b3_ref, ready_hbm, out_ref):
     core = place_ref[0] % 2
-    for dy, ref in enumerate((b0_ref, b1_ref, b2_ref, b3_ref)):
+    for dy, ref in zip(BAND_ORDER, (b0_ref, b1_ref, b2_ref, b3_ref)):
         out_ref[dy] = ref[:, 1 - core]
 
 
 def end_kernel(place_ref, mix_ref, direct_ref, conv_ref, b0_ref, b1_ref, b2_ref, b3_ref, other_ref, out_hbm, hops_ref, out_ref, sems):
     me = place_ref[0]
     z, y, core = me // 8, (me // 2) % 4, me % 2
-    for dy, ref in enumerate((b0_ref, b1_ref, b2_ref, b3_ref)):
+    for dy, ref in zip(BAND_ORDER, (b0_ref, b1_ref, b2_ref, b3_ref)):
         for dz in range(NEAR):
             chip = ((z + NEAR - dz) % NEAR) * 8 + ((y + NEAR - dy) % NEAR) * 2
             hops_ref[chip + core] = ref[dz, core]
@@ -370,7 +371,7 @@
         part = lax.dynamic_index_in_dim(turned, (y + d) % NEAR, 0, keepdims=False)
         return lax.ppermute(part, "seq", along_y[d]) if d else part
 
-    bands = [turned_for(d) for d in range(NEAR)]
+    bands = [turned_for(d) for d in BAND_ORDER]
     hbm = pl.BlockSpec(memory_space=pl.ANY)
     vmem = pl.BlockSpec(memory_space=pltpu.VMEM)
     smem = pl.BlockSpec(memory_space=pltpu.SMEM)
@@ -436,7 +437,7 @@
         return lax.ppermute(part, "seq", along_y[d]) if d else part
 
     returned = swap(conv)
-    conv_bands = [picked_for(d) for d in range(NEAR)]
+    conv_bands = [picked_for(d) for d in BAND_ORDER]
     pad = pltpu.VMEM((TOKENS + 8, CHANS), F32)
     query_mix, direct = pl.pallas_call(
         gate_kernel,

time: 66.7 us -> 66.7 us (level)
  waiting for transfers between devices: 17.3 us -> 15.2 us
  starting transfers between devices: 35.3 us -> 37.3 us
    ppermute x3, waiting for transfers between devices: 5.39 us -> 2.82 us  [picked_for(): return lax.ppermute(part, 'seq', along_y[d]) if d else part]
    ppermute x1, starting transfers between devices: 4.49 us -> 3.28 us  [local(): halo = lax.ppermute(last_rows, 'seq', pairs)]
    ppermute x3, starting transfers between devices: 3.83 us -> 5.04 us  [turned_for(): return lax.ppermute(part, 'seq', along_y[d]) if d else part]
    ppermute x3, starting transfers between devices: 3.34 us -> 4.54 us  [picked_for(): return lax.ppermute(part, 'seq', along_y[d]) if d else part]
    all_to_all x2, waiting for transfers between devices: 2.01 us -> 2.97 us  [swap(): return lax.all_to_all(x, 'seq', split_axis=0, concat_axis=0, tiled=True)]
where the time goes in v6:
time: 66.7 us; the launch traced here: 66.4 us
  starting transfers between devices  37.3 us (56%)
  waiting for transfers between devices  15.2 us (23%)
  Pallas kernels  12 us (18%)
  local copies, waits for them, and re-layouts  1.39 us (2%)
    all_to_all x2, starting transfers between devices, swap(): return lax.all_to_all(x, 'seq', split_axis=0, concat_axis=0, tiled=True)  11.3 us
    ppermute x3, starting transfers between devices, filter_for(): return lax.ppermute(part, 'seq', along_z[d]) if d else part  6.26 us
    pallas_call x1, Pallas kernels, local(): pl.pallas_call(middle_kernel, in_specs=[smem] + [vmem] * 8, out_shape=[ja...  6.21 us
    ppermute x3, starting transfers between devices, turned_for(): return lax.ppermute(part, 'seq', along_y[d]) if d else part  5.04 us
    ppermute x3, starting transfers between devices, conv_for(): return lax.ppermute(part, 'seq', along_z[d]) if d else part  4.59 us
    ppermute x3, starting transfers between devices, picked_for(): return lax.ppermute(part, 'seq', along_y[d]) if d else part  4.54 us
    ppermute x3, waiting for transfers between devices, turned_for(): return lax.ppermute(part, 'seq', along_y[d]) if d else part  3.47 us
    ppermute x1, starting transfers between devices, local(): halo = lax.ppermute(last_rows, 'seq', pairs)  3.28 us
  transfers between devices with their start and end apart: 17, of which 9 were waited for; matrix products, arithmetic and copies ran while one was open for 0% of the time, Pallas kernels for 7%

profile of v6, /device:TPU:1, one launch (start us, length us, event | category | flops | bytes accessed | tf_op | source)
XLA Modules:
  0.0 66.4 jit_solution(7254248058845896119)
XLA Ops:
  0.0 0.0 copy-start.5
  0.0 0.0 copy-start.1
  0.0 0.0 copy-start.3
  0.0 1.2 %constant_dynamic-slice_fusion.4 = (bf16[512,128]{1,0:T(8,128)(2,1)S(1)}, bf16[512,128]{1,0:T(8,128)(2,1)S(1)}, bf16[512,128]{1,0:T(8,128)(2,1)S(1)}, bf16[512,128]{1,0:T(8,128)(2,1)S(1)}) fusion(bf16[512,512]{1,0:T(8,128)(2,1)} %param.11, s32[]{:T(128)S(6)} %select_n.112, s32[]{:T(128)S(6)} %select_n.108, s32[]{:T(128)S(6)} %select_n.106, s32[]{:T(128)S(6)} %select_n.110), kind=kLoop, calls=%fused_computation.13 | loop fusion | bytes 1048592 | tf_op jit(solution)/shard_map/dynamic_slice | solution.py:359
  1.3 2.5 %collective-permute-start.3 = (bf16[512,128]{1,0:T(8,128)(2,1)S(1)}, bf16[512,128]{1,0:T(8,128)(2,1)S(1)}, u32[]{:S(2)}, u32[]{:S(2)}) collective-permute-start(bf16[512,128]{1,0:T(8,128)(2,1)S(1)} %get-tuple-element.17), channel_id=1, source_target_pairs={{0,8},{1,9},{2,10},{3,11},{4,12},{5,13},{6,14},{7,15},{8,16},{9,17... | collective-permute-start | bytes 393224 | tf_op jit(solution)/shard_map/ppermute | solution.py:360
  3.8 3.0 %collective-permute-start.1 = (bf16[512,128]{1,0:T(8,128)(2,1)S(1)}, bf16[512,128]{1,0:T(8,128)(2,1)S(1)}, u32[]{:S(2)}, u32[]{:S(2)}) collective-permute-start(bf16[512,128]{1,0:T(8,128)(2,1)S(1)} %get-tuple-element.18), channel_id=1, source_target_pairs={{0,16},{1,17},{2,18},{3,19},{4,20},{5,21},{6,22},{7,23},{8,24},{9,... | collective-permute-start | bytes 393224 | tf_op jit(solution)/shard_map/ppermute | solution.py:360
  6.8 0.7 %collective-permute-start.2 = (bf16[512,128]{1,0:T(8,128)(2,1)S(1)}, bf16[512,128]{1,0:T(8,128)(2,1)S(1)}, u32[]{:S(2)}, u32[]{:S(2)}) collective-permute-start(bf16[512,128]{1,0:T(8,128)(2,1)S(1)} %get-tuple-element.20), channel_id=1, source_target_pairs={{0,24},{1,25},{2,26},{3,27},{4,28},{5,29},{6,30},{7,31},{8,0},{9,1... | collective-permute-start | bytes 393224 | tf_op jit(solution)/shard_map/ppermute | solution.py:360
  7.5 0.0 copy-done.5
  7.5 0.0 copy-done.1
  7.5 0.0 copy-done.3
  7.5 2.4 %product.1 = bf16[32,80,128]{2,1,0:T(8,128)(2,1)} custom-call(bf16[512,512]{1,0:T(8,128)(2,1)S(1)} %copy-done.1, bf16[512,512]{1,0:T(8,128)(2,1)S(1)} %copy-done.3, f32[3,3,512]{2,1,0:T(4,128)S(1)} %copy-done.5), custom_call_target="tpu_custom_call" | custom-call | flops 20000000000 | bytes 4194304 | tf_op jit(solution)/shard_map/product/pallas_call | solution.py:392
  10.0 6.6 %all-to-all-start = ((bf16[32,80,128]{2,1,0:T(8,128)(2,1)}), bf16[32,80,128]{2,1,0:T(8,128)(2,1)S(1)}, u32[]{:S(2)}, u32[]{:S(2)}) async-start(bf16[32,80,128]{2,1,0:T(8,128)(2,1)} %product.1), calls=%async_computation | async-start | bytes 1310720 | tf_op jit(solution)/shard_map/all_to_all | solution.py:350
  16.7 0.0 collective-permute-done.3.refs_3_
  16.7 0.0 collective-permute-done.1.refs_1_
  16.7 0.0 collective-permute-done.2.refs_2_
  16.7 0.2 turn.1
  16.9 0.0 copy-start
  16.9 0.1 dynamic-slice_bitcast_fusion
  17.0 1.5 %collective-permute-start.6 = (bf16[4,2,64,128]{3,2,1,0:T(8,128)(2,1)S(1)}, bf16[4,2,64,128]{3,2,1,0:T(8,128)(2,1)S(1)}, u32[]{:S(2)}, u32[]{:S(2)}) collective-permute-start(bf16[4,2,64,128]{3,2,1,0:T(8,128)(2,1)S(1)} %get-tuple-element.13), channel_id=1, source_target_pairs={{0,2},{1,3},{2,4},{3,5},{4,6},{5,7},{6,0},{7,1},{8,10},{9,11},{10,... | collective-permute-start | bytes 393224 | tf_op jit(solution)/shard_map/ppermute | solution.py:372
  18.5 2.4 %collective-permute-start.5 = (bf16[4,2,64,128]{3,2,1,0:T(8,128)(2,1)S(1)}, bf16[4,2,64,128]{3,2,1,0:T(8,128)(2,1)S(1)}, u32[]{:S(2)}, u32[]{:S(2)}) collective-permute-start(bf16[4,2,64,128]{3,2,1,0:T(8,128)(2,1)S(1)} %get-tuple-element.14), channel_id=1, source_target_pairs={{0,4},{1,5},{2,6},{3,7},{4,0},{5,1},{6,2},{7,3},{8,12},{9,13},{10,... | collective-permute-start | bytes 393224 | tf_op jit(solution)/shard_map/ppermute | solution.py:372
  20.8 1.2 %collective-permute-start.4 = (bf16[4,2,64,128]{3,2,1,0:T(8,128)(2,1)S(1)}, bf16[4,2,64,128]{3,2,1,0:T(8,128)(2,1)S(1)}, u32[]{:S(2)}, u32[]{:S(2)}) collective-permute-start(bf16[4,2,64,128]{3,2,1,0:T(8,128)(2,1)S(1)} %get-tuple-element.15), channel_id=1, source_target_pairs={{0,6},{1,7},{2,0},{3,1},{4,2},{5,3},{6,4},{7,5},{8,14},{9,15},{10,... | collective-permute-start | bytes 393224 | tf_op jit(solution)/shard_map/ppermute | solution.py:372
  22.0 0.0 copy-done
  22.1 3.3 %collective-permute-start = (bf16[3,2,512]{2,1,0:T(2,128)(2,1)S(1)}, bf16[3,2,512]{2,1,0:T(2,128)(2,1)S(1)}, u32[]{:S(2)}, u32[]{:S(2)}) collective-permute-start(bf16[3,2,512]{2,1,0:T(2,128)(2,1)S(1)} %pad_maximum_fusion), channel_id=1, source_target_pairs={{0,1},{1,2},{2,3},{3,4},{4,5},{5,6},{6,7},{7,8},{8,9},{9,10},{10,1... | collective-permute-start | bytes 18440 | tf_op jit(solution)/shard_map/ppermute | solution.py:347
  25.3 3.3 %collective-permute-done.ready_hbm.halo_ref = bf16[3,2,512]{2,1,0:T(2,128)(2,1)S(1)} collective-permute-done((bf16[3,2,512]{2,1,0:T(2,128)(2,1)S(1)}, bf16[3,2,512]{2,1,0:T(2,128)(2,1)S(1)}, u32[]{:S(2)}, u32[]{:S(2)}) %collective-permute-start) | collective-permute-done | bytes 6176 | tf_op jit(solution)/shard_map/ppermute | solution.py:347
  28.6 0.0 collective-permute-done.6.b3_ref
  28.6 3.5 %collective-permute-done.5.b2_ref = bf16[4,2,64,128]{3,2,1,0:T(8,128)(2,1)S(1)} collective-permute-done((bf16[4,2,64,128]{3,2,1,0:T(8,128)(2,1)S(1)}, bf16[4,2,64,128]{3,2,1,0:T(8,128)(2,1)S(1)}, u32[]{:S(2)}, u32[]{:S(2)}) %collective-permute-start.5) | collective-permute-done | bytes 131104 | tf_op jit(solution)/shard_map/ppermute | solution.py:372
  32.1 0.0 collective-permute-done.4.b1_ref
  32.1 0.0 copy-start.7
  32.1 0.0 copy-start.8
  32.1 1.3 %collective-permute-start.7 = (bf16[4,4,64,128]{3,2,1,0:T(8,128)(2,1)S(1)}, bf16[4,4,64,128]{3,2,1,0:T(8,128)(2,1)S(1)}, u32[]{:S(2)}, u32[]{:S(2)}) collective-permute-start(bf16[4,4,64,128]{3,2,1,0:T(8,128)(2,1)S(1)} %other.2), channel_id=1, source_target_pairs={{0,1},{1,0},{2,3},{3,2},{4,5},{5,4},{6,7},{7,6},{8,9},{9,8},{10,11... | collective-permute-start | bytes 786440 | tf_op jit(solution)/shard_map/ppermute | solution.py:390
  33.4 1.2 %collective-permute-done.7.other_ref = bf16[4,4,64,128]{3,2,1,0:T(8,128)(2,1)S(1)} collective-permute-done((bf16[4,4,64,128]{3,2,1,0:T(8,128)(2,1)S(1)}, bf16[4,4,64,128]{3,2,1,0:T(8,128)(2,1)S(1)}, u32[]{:S(2)}, u32[]{:S(2)}) %collective-permute-start.7) | collective-permute-done | bytes 262176 | tf_op jit(solution)/shard_map/ppermute | solution.py:390
  34.6 0.9 %all-to-all-done.in_ref = bf16[32,80,128]{2,1,0:T(8,128)(2,1)S(1)} async-done(((bf16[32,80,128]{2,1,0:T(8,128)(2,1)}), bf16[32,80,128]{2,1,0:T(8,128)(2,1)S(1)}, u32[]{:S(2)}, u32[]{:S(2)}) %all-to-all-start) | async-done | bytes 655392 | tf_op jit(solution)/shard_map/all_to_all | solution.py:350
  35.5 0.0 copy-done.7
  35.5 0.0 copy-done.8
  35.5 6.2 %middle.1 = (bf16[32,48,128]{2,1,0:T(8,128)(2,1)}, bf16[32,32,128]{2,1,0:T(8,128)(2,1)S(1)}) custom-call(s32[1]{0:T(128)} %bitcast.place_ref, bf16[32,80,128]{2,1,0:T(8,128)(2,1)S(1)} %all-to-all-done.in_ref, bf16[4,2,64,128]{3,2,1,0:T(8,128)(2,1)S(1)} %get-tuple-element.16.b0_ref, bf16[4,2,64,128]{3,2,1,0:T(8,128)(2,1)S(1)} %collective-permute-done.4.b1_ref, ...), custom_call_target="tpu_custom_call" | custom-call | flops 8000000000 | bytes 2000000 | tf_op jit(solution)/shard_map/middle/pallas_call | solution.py:410
  41.7 2.7 %collective-permute-start.10 = (bf16[8,32,128]{2,1,0:T(8,128)(2,1)S(1)}, bf16[8,32,128]{2,1,0:T(8,128)(2,1)S(1)}, u32[]{:S(2)}, u32[]{:S(2)}) collective-permute-start(bf16[8,32,128]{2,1,0:T(8,128)(2,1)S(1)} %get-tuple-element.25), channel_id=1, source_target_pairs={{0,24},{1,25},{2,26},{3,27},{4,28},{5,29},{6,30},{7,31},{8,0},{9,1... | collective-permute-start | bytes 196616 | tf_op jit(solution)/shard_map/ppermute | solution.py:425
  44.4 0.5 collective-permute-start.9
  45.0 1.4 %collective-permute-start.8 = (bf16[8,32,128]{2,1,0:T(8,128)(2,1)S(1)}, bf16[8,32,128]{2,1,0:T(8,128)(2,1)S(1)}, u32[]{:S(2)}, u32[]{:S(2)}) collective-permute-start(bf16[8,32,128]{2,1,0:T(8,128)(2,1)S(1)} %get-tuple-element.27), channel_id=1, source_target_pairs={{0,8},{1,9},{2,10},{3,11},{4,12},{5,13},{6,14},{7,15},{8,16},{9,17... | collective-permute-start | bytes 196616 | tf_op jit(solution)/shard_map/ppermute | solution.py:425
  46.3 4.8 %all-to-all-start.1 = ((bf16[32,48,128]{2,1,0:T(8,128)(2,1)}), bf16[32,48,128]{2,1,0:T(8,128)(2,1)S(1)}, u32[]{:S(2)}, u32[]{:S(2)}) async-start(bf16[32,48,128]{2,1,0:T(8,128)(2,1)} %get-tuple-element.12), calls=%async_computation.1 | async-start | bytes 786432 | tf_op jit(solution)/shard_map/all_to_all | solution.py:350
  51.1 0.0 collective-permute-done.10.refs_3_
  51.1 0.6 collective-permute-done.9.refs_2_
  51.7 0.0 collective-permute-done.8.refs_1_
  51.7 0.0 copy-start.4
  51.7 0.0 copy-start.2
  51.7 0.9 %collective-permute-start.13 = (bf16[4,2,32,128]{3,2,1,0:T(8,128)(2,1)S(1)}, bf16[4,2,32,128]{3,2,1,0:T(8,128)(2,1)S(1)}, u32[]{:S(2)}, u32[]{:S(2)}) collective-permute-start(bf16[4,2,32,128]{3,2,1,0:T(8,128)(2,1)S(1)} %get-tuple-element.21), channel_id=1, source_target_pairs={{0,2},{1,3},{2,4},{3,5},{4,6},{5,7},{6,0},{7,1},{8,10},{9,11},{10,... | collective-permute-start | bytes 196616 | tf_op jit(solution)/shard_map/ppermute | solution.py:437
  52.7 0.0 copy-start.6
  52.7 2.4 %collective-permute-start.12 = (bf16[4,2,32,128]{3,2,1,0:T(8,128)(2,1)S(1)}, bf16[4,2,32,128]{3,2,1,0:T(8,128)(2,1)S(1)}, u32[]{:S(2)}, u32[]{:S(2)}) collective-permute-start(bf16[4,2,32,128]{3,2,1,0:T(8,128)(2,1)S(1)} %get-tuple-element.22), channel_id=1, source_target_pairs={{0,4},{1,5},{2,6},{3,7},{4,0},{5,1},{6,2},{7,3},{8,12},{9,13},{10,... | collective-permute-start | bytes 196616 | tf_op jit(solution)/shard_map/ppermute | solution.py:437
  55.1 1.2 %collective-permute-start.11 = (bf16[4,2,32,128]{3,2,1,0:T(8,128)(2,1)S(1)}, bf16[4,2,32,128]{3,2,1,0:T(8,128)(2,1)S(1)}, u32[]{:S(2)}, u32[]{:S(2)}) collective-permute-start(bf16[4,2,32,128]{3,2,1,0:T(8,128)(2,1)S(1)} %get-tuple-element.23), channel_id=1, source_target_pairs={{0,6},{1,7},{2,0},{3,1},{4,2},{5,3},{6,4},{7,5},{8,14},{9,15},{10,... | collective-permute-start | bytes 196616 | tf_op jit(solution)/shard_map/ppermute | solution.py:437
  56.3 0.0 copy-done.4
  56.3 0.0 copy-done.2
  56.3 0.0 copy-done.6
  56.3 1.9 %gate.1 = (f32[512,512]{1,0:T(8,128)S(1)}, f32[512,512]{1,0:T(8,128)S(1)}) custom-call(bf16[512,512]{1,0:T(8,128)(2,1)S(1)} %copy-done, bf16[512,512]{1,0:T(8,128)(2,1)S(1)} %copy-done.2, bf16[512,512]{1,0:T(8,128)(2,1)S(1)} %copy-done.4, bf16[3,2,512]{2,1,0:T(2,128)(2,1)S(1)} %collective-permute-done.ready_hbm.halo_ref, f32[3,3,512]{2,1,0:T(4,128)S(1)} %copy-done.5, ...), custom_call_target="tpu_custom_call" | custom-call | flops 1000000000 | bytes 4000000 | tf_op jit(solution)/shard_map/gate/pallas_call | solution.py:442
  58.2 0.1 collective-permute-done.13.b3_ref
  58.3 2.7 %collective-permute-done.12.b2_ref = bf16[4,2,32,128]{3,2,1,0:T(8,128)(2,1)S(1)} collective-permute-done((bf16[4,2,32,128]{3,2,1,0:T(8,128)(2,1)S(1)}, bf16[4,2,32,128]{3,2,1,0:T(8,128)(2,1)S(1)}, u32[]{:S(2)}, u32[]{:S(2)}) %collective-permute-start.12) | collective-permute-done | bytes 65568 | tf_op jit(solution)/shard_map/ppermute | solution.py:437
  61.0 0.0 collective-permute-done.11.b1_ref
  61.0 0.9 %collective-permute-start.14 = (bf16[4,4,32,128]{3,2,1,0:T(8,128)(2,1)S(1)}, bf16[4,4,32,128]{3,2,1,0:T(8,128)(2,1)S(1)}, u32[]{:S(2)}, u32[]{:S(2)}) collective-permute-start(bf16[4,4,32,128]{3,2,1,0:T(8,128)(2,1)S(1)} %other.3), channel_id=1, source_target_pairs={{0,1},{1,0},{2,3},{3,2},{4,5},{5,4},{6,7},{7,6},{8,9},{9,8},{10,11... | collective-permute-start | bytes 393224 | tf_op jit(solution)/shard_map/ppermute | solution.py:452
  62.0 1.0 %collective-permute-done.14.other_ref = bf16[4,4,32,128]{3,2,1,0:T(8,128)(2,1)S(1)} collective-permute-done((bf16[4,4,32,128]{3,2,1,0:T(8,128)(2,1)S(1)}, bf16[4,4,32,128]{3,2,1,0:T(8,128)(2,1)S(1)}, u32[]{:S(2)}, u32[]{:S(2)}) %collective-permute-start.14) | collective-permute-done | bytes 131104 | tf_op jit(solution)/shard_map/ppermute | solution.py:452
  63.0 2.0 %all-to-all-done.1.conv_ref = bf16[32,48,128]{2,1,0:T(8,128)(2,1)S(1)} async-done(((bf16[32,48,128]{2,1,0:T(8,128)(2,1)}), bf16[32,48,128]{2,1,0:T(8,128)(2,1)S(1)}, u32[]{:S(2)}, u32[]{:S(2)}) %all-to-all-start.1) | async-done | bytes 393248 | tf_op jit(solution)/shard_map/all_to_all | solution.py:350
  65.0 1.2 %end.1 = bf16[512,512]{1,0:T(8,128)(2,1)} custom-call(s32[1]{0:T(128)} %bitcast.place_ref, f32[512,512]{1,0:T(8,128)S(1)} %get-tuple-element.10.mix_ref, f32[512,512]{1,0:T(8,128)S(1)} %get-tuple-element.11.ready_hbm.direct_ref, bf16[32,48,128]{2,1,0:T(8,128)(2,1)S(1)} %all-to-all-done.1.conv_ref, bf16[4,2,32,128]{3,2,1,0:T(8,128)(2,1)S(1)} %get-tuple-element.24.b0_ref, ...), custom_call_target="tpu_custom_call" | custom-call | tf_op jit(solution)/shard_map/end/pallas_call | solution.py:453
  (8 shorter events, 0.1 us)
Async XLA Ops:
  0.0 7.5 %copy-start.5 = (f32[3,3,512]{2,1,0:T(4,128)S(1)}, f32[3,3,512]{2,1,0:T(4,128)}, u32[]{:S(2)}) copy-start(f32[3,3,512]{2,1,0:T(4,128)} %taps_ref.3) | copy-start | bytes 55300
  0.0 7.5 %copy-start.1 = (bf16[512,512]{1,0:T(8,128)(2,1)S(1)}, bf16[512,512]{1,0:T(8,128)(2,1)}, u32[]{:S(2)}) copy-start(bf16[512,512]{1,0:T(8,128)(2,1)} %key_hbm.1) | copy-start | bytes 1572868
  0.0 7.5 %copy-start.3 = (bf16[512,512]{1,0:T(8,128)(2,1)S(1)}, bf16[512,512]{1,0:T(8,128)(2,1)}, u32[]{:S(2)}) copy-start(bf16[512,512]{1,0:T(8,128)(2,1)} %value_hbm.1) | copy-start | bytes 1572868
  1.3 15.4 %collective-permute-start.3 = (bf16[512,128]{1,0:T(8,128)(2,1)S(1)}, bf16[512,128]{1,0:T(8,128)(2,1)S(1)}, u32[]{:S(2)}, u32[]{:S(2)}) collective-permute-start(bf16[512,128]{1,0:T(8,128)(2,1)S(1)} %get-tuple-element.17), channel_id=1, source_target_pairs={{0,8},{1,9},{2,10},{3,11},{4,12},{5,13},{6,14},{7,15},{8,16},{9,17... | collective-permute-start | bytes 393224 | tf_op jit(solution)/shard_map/ppermute | solution.py:360
  3.8 12.9 %collective-permute-start.1 = (bf16[512,128]{1,0:T(8,128)(2,1)S(1)}, bf16[512,128]{1,0:T(8,128)(2,1)S(1)}, u32[]{:S(2)}, u32[]{:S(2)}) collective-permute-start(bf16[512,128]{1,0:T(8,128)(2,1)S(1)} %get-tuple-element.18), channel_id=1, source_target_pairs={{0,16},{1,17},{2,18},{3,19},{4,20},{5,21},{6,22},{7,23},{8,24},{9,... | collective-permute-start | bytes 393224 | tf_op jit(solution)/shard_map/ppermute | solution.py:360
  6.8 9.9 %collective-permute-start.2 = (bf16[512,128]{1,0:T(8,128)(2,1)S(1)}, bf16[512,128]{1,0:T(8,128)(2,1)S(1)}, u32[]{:S(2)}, u32[]{:S(2)}) collective-permute-start(bf16[512,128]{1,0:T(8,128)(2,1)S(1)} %get-tuple-element.20), channel_id=1, source_target_pairs={{0,24},{1,25},{2,26},{3,27},{4,28},{5,29},{6,30},{7,31},{8,0},{9,1... | collective-permute-start | bytes 393224 | tf_op jit(solution)/shard_map/ppermute | solution.py:360
  10.0 25.6 %all-to-all-start = ((bf16[32,80,128]{2,1,0:T(8,128)(2,1)}), bf16[32,80,128]{2,1,0:T(8,128)(2,1)S(1)}, u32[]{:S(2)}, u32[]{:S(2)}) async-start(bf16[32,80,128]{2,1,0:T(8,128)(2,1)} %product.1), calls=%async_computation | async-start | bytes 1310720 | tf_op jit(solution)/shard_map/all_to_all | solution.py:350
  16.9 5.1 %copy-start = (bf16[512,512]{1,0:T(8,128)(2,1)S(1)}, bf16[512,512]{1,0:T(8,128)(2,1)}, u32[]{:S(2)}) copy-start(bf16[512,512]{1,0:T(8,128)(2,1)} %query_hbm.1) | copy-start | bytes 1572868
  17.0 11.6 %collective-permute-start.6 = (bf16[4,2,64,128]{3,2,1,0:T(8,128)(2,1)S(1)}, bf16[4,2,64,128]{3,2,1,0:T(8,128)(2,1)S(1)}, u32[]{:S(2)}, u32[]{:S(2)}) collective-permute-start(bf16[4,2,64,128]{3,2,1,0:T(8,128)(2,1)S(1)} %get-tuple-element.13), channel_id=1, source_target_pairs={{0,2},{1,3},{2,4},{3,5},{4,6},{5,7},{6,0},{7,1},{8,10},{9,11},{10,... | collective-permute-start | bytes 393224 | tf_op jit(solution)/shard_map/ppermute | solution.py:372
  18.5 13.6 %collective-permute-start.5 = (bf16[4,2,64,128]{3,2,1,0:T(8,128)(2,1)S(1)}, bf16[4,2,64,128]{3,2,1,0:T(8,128)(2,1)S(1)}, u32[]{:S(2)}, u32[]{:S(2)}) collective-permute-start(bf16[4,2,64,128]{3,2,1,0:T(8,128)(2,1)S(1)} %get-tuple-element.14), channel_id=1, source_target_pairs={{0,4},{1,5},{2,6},{3,7},{4,0},{5,1},{6,2},{7,3},{8,12},{9,13},{10,... | collective-permute-start | bytes 393224 | tf_op jit(solution)/shard_map/ppermute | solution.py:372
  20.8 11.2 %collective-permute-start.4 = (bf16[4,2,64,128]{3,2,1,0:T(8,128)(2,1)S(1)}, bf16[4,2,64,128]{3,2,1,0:T(8,128)(2,1)S(1)}, u32[]{:S(2)}, u32[]{:S(2)}) collective-permute-start(bf16[4,2,64,128]{3,2,1,0:T(8,128)(2,1)S(1)} %get-tuple-element.15), channel_id=1, source_target_pairs={{0,6},{1,7},{2,0},{3,1},{4,2},{5,3},{6,4},{7,5},{8,14},{9,15},{10,... | collective-permute-start | bytes 393224 | tf_op jit(solution)/shard_map/ppermute | solution.py:372
  22.1 6.5 %collective-permute-start = (bf16[3,2,512]{2,1,0:T(2,128)(2,1)S(1)}, bf16[3,2,512]{2,1,0:T(2,128)(2,1)S(1)}, u32[]{:S(2)}, u32[]{:S(2)}) collective-permute-start(bf16[3,2,512]{2,1,0:T(2,128)(2,1)S(1)} %pad_maximum_fusion), channel_id=1, source_target_pairs={{0,1},{1,2},{2,3},{3,4},{4,5},{5,6},{6,7},{7,8},{8,9},{9,10},{10,1... | collective-permute-start | bytes 18440 | tf_op jit(solution)/shard_map/ppermute | solution.py:347
  32.1 3.4 %copy-start.7 = (bf16[768,256]{1,0:T(8,128)(2,1)S(1)}, bf16[768,256]{1,0:T(8,128)(2,1)}, u32[]{:S(2)}) copy-start(bf16[768,256]{1,0:T(8,128)(2,1)} %constant.123.clone.mats_ref) | copy-start | bytes 1179652
  32.1 3.4 %copy-start.8 = (f32[2,128,128]{2,1,0:T(8,128)S(1)}, f32[2,128,128]{2,1,0:T(8,128)}, u32[]{:S(2)}) copy-start(f32[2,128,128]{2,1,0:T(8,128)} %constant.124.clone.twiddle_ref) | copy-start | bytes 393220
  32.1 2.5 %collective-permute-start.7 = (bf16[4,4,64,128]{3,2,1,0:T(8,128)(2,1)S(1)}, bf16[4,4,64,128]{3,2,1,0:T(8,128)(2,1)S(1)}, u32[]{:S(2)}, u32[]{:S(2)}) collective-permute-start(bf16[4,4,64,128]{3,2,1,0:T(8,128)(2,1)S(1)} %other.2), channel_id=1, source_target_pairs={{0,1},{1,0},{2,3},{3,2},{4,5},{5,4},{6,7},{7,6},{8,9},{9,8},{10,11... | collective-permute-start | bytes 786440 | tf_op jit(solution)/shard_map/ppermute | solution.py:390
  41.7 9.4 %collective-permute-start.10 = (bf16[8,32,128]{2,1,0:T(8,128)(2,1)S(1)}, bf16[8,32,128]{2,1,0:T(8,128)(2,1)S(1)}, u32[]{:S(2)}, u32[]{:S(2)}) collective-permute-start(bf16[8,32,128]{2,1,0:T(8,128)(2,1)S(1)} %get-tuple-element.25), channel_id=1, source_target_pairs={{0,24},{1,25},{2,26},{3,27},{4,28},{5,29},{6,30},{7,31},{8,0},{9,1... | collective-permute-start | bytes 196616 | tf_op jit(solution)/shard_map/ppermute | solution.py:425
  44.4 7.2 %collective-permute-start.9 = (bf16[8,32,128]{2,1,0:T(8,128)(2,1)S(1)}, bf16[8,32,128]{2,1,0:T(8,128)(2,1)S(1)}, u32[]{:S(2)}, u32[]{:S(2)}) collective-permute-start(bf16[8,32,128]{2,1,0:T(8,128)(2,1)S(1)} %get-tuple-element.26), channel_id=1, source_target_pairs={{0,16},{1,17},{2,18},{3,19},{4,20},{5,21},{6,22},{7,23},{8,24},{9,... | collective-permute-start | bytes 196616 | tf_op jit(solution)/shard_map/ppermute | solution.py:425
  45.0 6.7 %collective-permute-start.8 = (bf16[8,32,128]{2,1,0:T(8,128)(2,1)S(1)}, bf16[8,32,128]{2,1,0:T(8,128)(2,1)S(1)}, u32[]{:S(2)}, u32[]{:S(2)}) collective-permute-start(bf16[8,32,128]{2,1,0:T(8,128)(2,1)S(1)} %get-tuple-element.27), channel_id=1, source_target_pairs={{0,8},{1,9},{2,10},{3,11},{4,12},{5,13},{6,14},{7,15},{8,16},{9,17... | collective-permute-start | bytes 196616 | tf_op jit(solution)/shard_map/ppermute | solution.py:425
  46.3 18.7 %all-to-all-start.1 = ((bf16[32,48,128]{2,1,0:T(8,128)(2,1)}), bf16[32,48,128]{2,1,0:T(8,128)(2,1)S(1)}, u32[]{:S(2)}, u32[]{:S(2)}) async-start(bf16[32,48,128]{2,1,0:T(8,128)(2,1)} %get-tuple-element.12), calls=%async_computation.1 | async-start | bytes 786432 | tf_op jit(solution)/shard_map/all_to_all | solution.py:350
  51.7 4.6 %copy-start.4 = (bf16[512,512]{1,0:T(8,128)(2,1)S(1)}, bf16[512,512]{1,0:T(8,128)(2,1)}, u32[]{:S(2)}) copy-start(bf16[512,512]{1,0:T(8,128)(2,1)} %value_hbm.1) | copy-start | bytes 1572868
  51.7 4.6 %copy-start.2 = (bf16[512,512]{1,0:T(8,128)(2,1)S(1)}, bf16[512,512]{1,0:T(8,128)(2,1)}, u32[]{:S(2)}) copy-start(bf16[512,512]{1,0:T(8,128)(2,1)} %key_hbm.1) | copy-start | bytes 1572868
  51.7 6.6 %collective-permute-start.13 = (bf16[4,2,32,128]{3,2,1,0:T(8,128)(2,1)S(1)}, bf16[4,2,32,128]{3,2,1,0:T(8,128)(2,1)S(1)}, u32[]{:S(2)}, u32[]{:S(2)}) collective-permute-start(bf16[4,2,32,128]{3,2,1,0:T(8,128)(2,1)S(1)} %get-tuple-element.21), channel_id=1, source_target_pairs={{0,2},{1,3},{2,4},{3,5},{4,6},{5,7},{6,0},{7,1},{8,10},{9,11},{10,... | collective-permute-start | bytes 196616 | tf_op jit(solution)/shard_map/ppermute | solution.py:437
  52.7 3.6 %copy-start.6 = (f32[512]{0:T(512)S(1)}, f32[512]{0:T(512)}, u32[]{:S(2)}) copy-start(f32[512]{0:T(512)} %param.13) | copy-start | bytes 6148
  52.7 8.3 %collective-permute-start.12 = (bf16[4,2,32,128]{3,2,1,0:T(8,128)(2,1)S(1)}, bf16[4,2,32,128]{3,2,1,0:T(8,128)(2,1)S(1)}, u32[]{:S(2)}, u32[]{:S(2)}) collective-permute-start(bf16[4,2,32,128]{3,2,1,0:T(8,128)(2,1)S(1)} %get-tuple-element.22), channel_id=1, source_target_pairs={{0,4},{1,5},{2,6},{3,7},{4,0},{5,1},{6,2},{7,3},{8,12},{9,13},{10,... | collective-permute-start | bytes 196616 | tf_op jit(solution)/shard_map/ppermute | solution.py:437
  55.1 5.9 %collective-permute-start.11 = (bf16[4,2,32,128]{3,2,1,0:T(8,128)(2,1)S(1)}, bf16[4,2,32,128]{3,2,1,0:T(8,128)(2,1)S(1)}, u32[]{:S(2)}, u32[]{:S(2)}) collective-permute-start(bf16[4,2,32,128]{3,2,1,0:T(8,128)(2,1)S(1)} %get-tuple-element.23), channel_id=1, source_target_pairs={{0,6},{1,7},{2,0},{3,1},{4,2},{5,3},{6,4},{7,5},{8,14},{9,15},{10,... | collective-permute-start | bytes 196616 | tf_op jit(solution)/shard_map/ppermute | solution.py:437
  61.0 1.9 %collective-permute-start.14 = (bf16[4,4,32,128]{3,2,1,0:T(8,128)(2,1)S(1)}, bf16[4,4,32,128]{3,2,1,0:T(8,128)(2,1)S(1)}, u32[]{:S(2)}, u32[]{:S(2)}) collective-permute-start(bf16[4,4,32,128]{3,2,1,0:T(8,128)(2,1)S(1)} %other.3), channel_id=1, source_target_pairs={{0,1},{1,0},{2,3},{3,2},{4,5},{5,4},{6,7},{7,6},{8,9},{9,8},{10,11... | collective-permute-start | bytes 393224 | tf_op jit(solution)/shard_map/ppermute | solution.py:452
